TPU v7x, 256 devices: a whole 4x4x8 slice. The times are simulated.
256 devices in a mesh: tm: 4 (over y), height: 4 (over x), width: 16 (over z, core).
Axes of the slice: x: 4, y: 4, z: 8, core: 2. Of those that a mesh axis runs over, the one named last changes fastest.
Arguments:
- features: bfloat16 [16, 32, 160, 384], P('tm', 'height', 'width'), may hold values from -6 to 6
- first_gain: float32 [384], replicated, may hold values from 0.5 to 2
- first_kernel: bfloat16 [27, 384, 384], P(None, ('height', 'width')), may hold values from -0.0625 to 0.0625
- first_bias: float32 [384], replicated, may hold values from -3 to 3
- second_gain: float32 [384], replicated, may hold values from 0.5 to 2
- second_kernel: bfloat16 [27, 384, 384], P(None, ('height', 'width')), may hold values from -0.0625 to 0.0625
- second_bias: float32 [384], replicated, may hold values from -3 to 3
Outputs:
- block_out: bfloat16 [16, 32, 160, 384], P('tm', 'height', 'width')
All inputs are finite; a program needn't handle non-finite values.
Results may differ from a plain program's by a relative error of at most 0.012.
Values may be sent and summed in bfloat16 or wider, within the bound.
No kernel may reach another device: no remote copies, remote signals or barrier semaphores. Data moves between devices by JAX's collectives and lax.ppermute only.
A program may use at most 128 MiB of HBM per device.

v0:
```python
import jax
import jax.numpy as jnp
from jax import lax
from jax.sharding import PartitionSpec as P


def passed_along(x, axis, by):
    devices = lax.axis_size(axis)
    pairs = [(i, i + by) for i in range(devices) if 0 <= i + by < devices]
    return lax.ppermute(x, axis, pairs)


def extended(x, sides, width):
    for axis, dim in sides:
        devices, length = (lax.axis_size(axis), x.shape[dim])
        up = [(i, (i + 1) % devices) for i in range(devices - 1)]
        down = [(j, i) for i, j in up]
        last = lax.slice_in_dim(x, length - width, length, axis=dim)
        first = lax.slice_in_dim(x, 0, width, axis=dim)
        before = lax.ppermute(last, axis, up)
        after = lax.ppermute(first, axis, down)
        x = jnp.concatenate([before, x, after], axis=dim)
    return x


def activate(volume, gain):
    values = volume.astype(jnp.float32)
    square_mean = jnp.mean(values * values, axis=-1, keepdims=True)
    normed = values * lax.rsqrt(square_mean + 1e-06) * gain
    return jax.nn.silu(normed).astype(jnp.bfloat16)


def make_folder(widened, frames, rows, cols):

    def fold_piece(total, piece, start):
        count_in = piece.shape[1]
        for step_t in range(3):
            for step_h in range(3):
                for step_w in range(3):
                    window = widened[
                        step_t : step_t + frames, step_h : step_h + rows, step_w : step_w + cols
                    ]
                    total = total + jnp.dot(
                        window.reshape(-1, count_in),
                        piece[9 * step_t + 3 * step_h + step_w],
                        preferred_element_type=jnp.float32,
                    )
        return total

    return fold_piece


def convolve(widened, kernel, bias, frames, rows, cols):
    out_chans = kernel.shape[2]
    empty = jnp.zeros((frames * rows * cols, out_chans), jnp.float32)
    fold_piece = make_folder(widened, frames, rows, cols)
    row_kernel = lax.all_gather(kernel, "width", axis=1, tiled=True)
    total = fold_piece(
        empty, lax.all_gather(row_kernel, "height", axis=1, tiled=True), jnp.int32(0)
    )
    return total.reshape(frames, rows, cols, out_chans) + bias


def widen(active):
    earlier = passed_along(active[-2:], "tm", 1)
    tall = jnp.concatenate([earlier, active], axis=0)
    return extended(tall, (("height", 1), ("width", 2)), 1)


def on_device(
    features, first_gain, first_kernel, first_bias, second_gain, second_kernel, second_bias
):
    frames, rows, cols, chans = features.shape
    first_active = activate(features, first_gain)
    middle = convolve(widen(first_active), first_kernel, first_bias, frames, rows, cols).astype(
        jnp.bfloat16
    )
    second_active = activate(middle, second_gain)
    second_wide = widen(second_active)
    summed = convolve(
        second_wide, second_kernel, second_bias, frames, rows, cols
    ) + features.astype(jnp.float32)
    return summed.astype(jnp.bfloat16)


def solution(mesh):
    placed = (
        P("tm", "height", "width", None),
        P(),
        P(None, ("height", "width"), None),
        P(),
        P(),
        P(None, ("height", "width"), None),
        P(),
    )
    return jax.shard_map(
        on_device,
        mesh=mesh,
        in_specs=placed,
        out_specs=P("tm", "height", "width", None),
        check_vma=False,
    )
```

profile of v0, /device:TPU:1, one launch (start us, length us, event | category | flops | bytes accessed | tf_op | source)
XLA Modules:
  0.0 329.2 jit_solution(13650596367216335500)
XLA Ops:
  8.1 45.3 %all-gather.5.cloned.1.call-done = bf16[27,96,384]{2,0,1:T(8,128)(2,1)} async-done(((bf16[27,6,384]{2,0,1:T(8,128)(2,1)}), bf16[27,96,384]{2,0,1:T(8,128)(2,1)}) %all-gather.5.cloned.1.call-update) | async-done | bytes 1990672 | tf_op jit(solution)/shard_map/all_gather | solution.py:57
  53.4 3.7 %copy.15 = bf16[27,96,384]{2,1,0:T(8,128)(2,1)} copy(bf16[27,96,384]{2,0,1:T(8,128)(2,1)} %all-gather.5.cloned.1.call-done) | data formatting | bytes 3981312 | tf_op jit(solution)/shard_map/all_gather | solution.py:57
  57.1 36.5 %all-gather.9.cloned.1.call-done = bf16[27,96,384]{2,0,1:T(8,128)(2,1)} async-done(((bf16[27,6,384]{2,0,1:T(8,128)(2,1)}), bf16[27,96,384]{2,0,1:T(8,128)(2,1)}) %all-gather.9.cloned.1.call-update) | async-done | bytes 1990672 | tf_op jit(solution)/shard_map/all_gather | solution.py:57
  93.6 3.7 %copy.16 = bf16[27,96,384]{2,1,0:T(8,128)(2,1)} copy(bf16[27,96,384]{2,0,1:T(8,128)(2,1)} %all-gather.9.cloned.1.call-done) | data formatting | bytes 3981312 | tf_op jit(solution)/shard_map/all_gather | solution.py:57
  97.9 3.1 collective-permute-start
  101.8 3.2 collective-permute-done
  106.3 4.0 %collective-permute-start.1 = (bf16[6,1,10,384]{3,2,1,0:T(8,128)(2,1)S(1)}, bf16[6,1,10,384]{3,2,1,0:T(8,128)(2,1)S(1)}, u32[]{:S(2)}, u32[]{:S(2)}) collective-permute-start(bf16[6,1,10,384]{3,2,1,0:T(8,128)(2,1)S(1)} %get-tuple-element.71), channel_id=1, source_target_pairs={{0,16},{16,32},{32,48},{1,17},{17,33},{33,49},{2,18},{18,34},{34,5... | collective-permute-start | bytes 138248 | tf_op jit(solution)/shard_map/ppermute | solution.py:20
  114.2 4.9 %collective-permute-start.3 = (bf16[6,10,1,384]{3,2,1,0:T(2,128)(2,1)}, bf16[6,10,1,384]{3,2,1,0:T(2,128)(2,1)S(1)}, u32[]{:S(2)}, u32[]{:S(2)}) collective-permute-start(bf16[6,10,1,384]{3,2,1,0:T(2,128)(2,1)} %get-tuple-element.47), channel_id=1, source_target_pairs={{0,1},{1,2},{2,3},{3,4},{4,5},{5,6},{6,7},{7,8},{8,9},{9,10},{10,1... | collective-permute-start | bytes 138248 | tf_op jit(solution)/shard_map/ppermute | solution.py:20
  119.1 2.1 collective-permute-start.4
  127.2 2.3 fusion.32
  129.4 1.8 reshape.211
  131.2 1.8 reshape.197
  133.0 1.8 reshape.199
  134.8 1.8 reshape.200
  136.6 1.8 reshape.202
  138.4 1.8 reshape.203
  140.2 1.8 reshape.205
  142.0 1.8 reshape.206
  143.8 1.8 reshape.208
  145.6 1.8 reshape.209
  151.7 24.5 %all-gather.7.cloned.1.call-done = bf16[27,384,384]{2,1,0:T(8,128)(2,1)} async-done(((bf16[27,96,384]{2,1,0:T(8,128)(2,1)}), bf16[27,384,384]{2,1,0:T(8,128)(2,1)}) %all-gather.7.cloned.1.call-update) | async-done | bytes 7962640 | tf_op jit(solution)/shard_map/all_gather | solution.py:59
  176.2 1.6 fusion.23
  177.8 1.8 fusion.24
  179.5 1.4 convolution_add_fusion.49
  181.0 1.5 convolution_add_fusion.48
  182.4 1.5 convolution_add_fusion.47
  183.9 1.3 convolution_add_fusion.46
  186.4 1.3 convolution_add_fusion.42
  194.3 3.3 collective-permute-start.5
  197.6 3.5 %collective-permute-done.5 = bf16[2,8,10,384]{3,2,1,0:T(8,128)(2,1)S(1)} collective-permute-done((bf16[2,8,10,384]{3,2,1,0:T(8,128)(2,1)S(1)}, bf16[2,8,10,384]{3,2,1,0:T(8,128)(2,1)S(1)}, u32[]{:S(2)}, u32[]{:S(2)}) %collective-permute-start.5) | collective-permute-done | bytes 122912 | tf_op jit(solution)/shard_map/ppermute | solution.py:10
  202.5 4.2 %collective-permute-start.6 = (bf16[6,1,10,384]{3,2,1,0:T(8,128)(2,1)S(1)}, bf16[6,1,10,384]{3,2,1,0:T(8,128)(2,1)S(1)}, u32[]{:S(2)}, u32[]{:S(2)}) collective-permute-start(bf16[6,1,10,384]{3,2,1,0:T(8,128)(2,1)S(1)} %get-tuple-element.65), channel_id=1, source_target_pairs={{0,16},{16,32},{32,48},{1,17},{17,33},{33,49},{2,18},{18,34},{34,5... | collective-permute-start | bytes 138248 | tf_op jit(solution)/shard_map/ppermute | solution.py:20
  210.1 5.8 %collective-permute-start.8 = (bf16[6,10,1,384]{3,2,1,0:T(2,128)(2,1)}, bf16[6,10,1,384]{3,2,1,0:T(2,128)(2,1)}, u32[]{:S(2)}, u32[]{:S(2)}) collective-permute-start(bf16[6,10,1,384]{3,2,1,0:T(2,128)(2,1)} %get-tuple-element.25), channel_id=1, source_target_pairs={{0,1},{1,2},{2,3},{3,4},{4,5},{5,6},{6,7},{7,8},{8,9},{9,10},{10,1... | collective-permute-start | bytes 138248 | tf_op jit(solution)/shard_map/ppermute | solution.py:20
  215.9 1.9 collective-permute-start.9
  220.1 42.1 %all-gather.11.cloned.1.call-done = bf16[27,384,384]{2,1,0:T(8,128)(2,1)} async-done(((bf16[27,96,384]{2,1,0:T(8,128)(2,1)}), bf16[27,384,384]{2,1,0:T(8,128)(2,1)}) %all-gather.11.cloned.1.call-update) | async-done | bytes 7962640 | tf_op jit(solution)/shard_map/all_gather | solution.py:59
  262.2 1.4 fusion.22
  263.6 1.8 reshape.232
  266.2 1.8 reshape.241
  268.8 1.8 reshape.249
  270.5 1.6 maximum_maximum_fusion.1
  272.1 1.8 fusion.30
  273.9 1.8 reshape.239
  275.7 1.9 fusion.31
  277.6 1.9 reshape.225
  279.4 1.8 reshape.227
  281.2 1.8 reshape.228
  283.0 1.8 reshape.230
  284.8 1.8 reshape.231
  286.6 1.8 reshape.233
  288.4 1.8 reshape.234
  290.1 1.8 reshape.236
  291.9 1.8 reshape.237
  293.7 1.8 reshape.240
  295.5 1.8 reshape.242
  297.3 1.8 reshape.243
  300.3 1.6 fusion.21
  301.9 1.4 convolution_add_fusion.24
  303.3 1.5 convolution_add_fusion.23
  304.8 1.5 convolution_add_fusion.22
  306.2 1.5 convolution_add_fusion.21
  307.7 1.6 convolution_add_fusion.20
  309.3 1.5 convolution_add_fusion.19
  310.8 1.5 convolution_add_fusion.18
  312.2 1.5 convolution_add_fusion.17
  313.7 1.3 convolution_add_fusion.16
  (186 shorter events, 42.7 us)
Async XLA Ops:
  6.5 90.8 %copy-start.1 = (bf16[4,8,10,384]{3,1,2,0:T(8,128)(2,1)S(1)}, bf16[4,8,10,384]{3,1,2,0:T(8,128)(2,1)}, u32[]{:S(2)}) copy-start(bf16[4,8,10,384]{3,1,2,0:T(8,128)(2,1)} %param.7) | copy-start | bytes 737284
  6.5 91.0 %copy-start.35 = (f32[384]{0:T(512)S(1)}, f32[384]{0:T(512)}, u32[]{:S(2)}) copy-start(f32[384]{0:T(512)} %param.8) | copy-start | bytes 4612
  6.5 46.8 %all-gather.5.cloned.1.call-start = ((), (), s32[]{:S(2)}) async-start(), calls=%async_computation | async-start | bytes 2506752 | tf_op jit(solution)/shard_map/all_gather | solution.py:57
  7.3 86.4 %all-gather.9.cloned.1.call-start = ((), (), s32[]{:S(2)}) async-start(), calls=%async_computation.2 | async-start | bytes 2506752 | tf_op jit(solution)/shard_map/all_gather | solution.py:57
  8.0 168.2 %all-gather.7.cloned.1.call-start = ((), (), s32[]{:S(2)}) async-start(), calls=%async_computation.1 | async-start | bytes 9953280 | tf_op jit(solution)/shard_map/all_gather | solution.py:59
  57.1 205.1 %all-gather.11.cloned.1.call-start = ((), (), s32[]{:S(2)}) async-start(), calls=%async_computation.3 | async-start | bytes 9953280 | tf_op jit(solution)/shard_map/all_gather | solution.py:59
  97.9 7.1 %collective-permute-start = (bf16[2,8,10,384]{3,2,1,0:T(8,128)(2,1)S(1)}, bf16[2,8,10,384]{3,2,1,0:T(8,128)(2,1)S(1)}, u32[]{:S(2)}, u32[]{:S(2)}) collective-permute-start(bf16[2,8,10,384]{3,2,1,0:T(8,128)(2,1)S(1)} %slice.512), channel_id=1, source_target_pairs={{0,64},{64,128},{128,192},{1,65},{65,129},{129,193},{2,66},{66,130... | collective-permute-start | bytes 368648 | tf_op jit(solution)/shard_map/ppermute | solution.py:10
  105.0 7.0 %collective-permute-start.2 = (bf16[6,1,10,384]{3,2,1,0:T(8,128)(2,1)S(1)}, bf16[6,1,10,384]{3,2,1,0:T(8,128)(2,1)S(1)}, u32[]{:S(2)}, u32[]{:S(2)}) collective-permute-start(bf16[6,1,10,384]{3,2,1,0:T(8,128)(2,1)S(1)} %get-tuple-element.72), channel_id=1, source_target_pairs={{16,0},{32,16},{48,32},{17,1},{33,17},{49,33},{18,2},{34,18},{50,3... | collective-permute-start | bytes 138248 | tf_op jit(solution)/shard_map/ppermute | solution.py:21
  106.3 7.0 %collective-permute-start.1 = (bf16[6,1,10,384]{3,2,1,0:T(8,128)(2,1)S(1)}, bf16[6,1,10,384]{3,2,1,0:T(8,128)(2,1)S(1)}, u32[]{:S(2)}, u32[]{:S(2)}) collective-permute-start(bf16[6,1,10,384]{3,2,1,0:T(8,128)(2,1)S(1)} %get-tuple-element.71), channel_id=1, source_target_pairs={{0,16},{16,32},{32,48},{1,17},{17,33},{33,49},{2,18},{18,34},{34,5... | collective-permute-start | bytes 138248 | tf_op jit(solution)/shard_map/ppermute | solution.py:20
  114.2 12.3 %collective-permute-start.3 = (bf16[6,10,1,384]{3,2,1,0:T(2,128)(2,1)}, bf16[6,10,1,384]{3,2,1,0:T(2,128)(2,1)S(1)}, u32[]{:S(2)}, u32[]{:S(2)}) collective-permute-start(bf16[6,10,1,384]{3,2,1,0:T(2,128)(2,1)} %get-tuple-element.47), channel_id=1, source_target_pairs={{0,1},{1,2},{2,3},{3,4},{4,5},{5,6},{6,7},{7,8},{8,9},{9,10},{10,1... | collective-permute-start | bytes 138248 | tf_op jit(solution)/shard_map/ppermute | solution.py:20
  119.1 7.4 %collective-permute-start.4 = (bf16[6,10,1,384]{3,2,1,0:T(2,128)(2,1)}, bf16[6,10,1,384]{3,2,1,0:T(2,128)(2,1)S(1)}, u32[]{:S(2)}, u32[]{:S(2)}) collective-permute-start(bf16[6,10,1,384]{3,2,1,0:T(2,128)(2,1)} %get-tuple-element.48), channel_id=1, source_target_pairs={{1,0},{2,1},{3,2},{4,3},{5,4},{6,5},{7,6},{8,7},{9,8},{10,9},{11,1... | collective-permute-start | bytes 138248 | tf_op jit(solution)/shard_map/ppermute | solution.py:21
  148.1 35.8 %copy-start.7 = (bf16[320,384]{1,0:T(8,128)(2,1)S(1)}, bf16[320,384]{1,0:T(8,128)(2,1)}, u32[]{:S(2)}) copy-start(bf16[320,384]{1,0:T(8,128)(2,1)} %reshape.201) | copy-start | bytes 737284
  148.9 37.1 %copy-start.14 = (bf16[320,384]{1,0:T(8,128)(2,1)S(1)}, bf16[320,384]{1,0:T(8,128)(2,1)}, u32[]{:S(2)}) copy-start(bf16[320,384]{1,0:T(8,128)(2,1)} %reshape.204) | copy-start | bytes 737284
  151.4 36.3 %copy-start.26 = (bf16[320,384]{1,0:T(8,128)(2,1)S(1)}, bf16[320,384]{1,0:T(8,128)(2,1)}, u32[]{:S(2)}) copy-start(bf16[320,384]{1,0:T(8,128)(2,1)} %reshape.206) | copy-start | bytes 737284
  151.5 33.8 %copy-start.31 = (bf16[320,384]{1,0:T(8,128)(2,1)S(1)}, bf16[320,384]{1,0:T(8,128)(2,1)}, u32[]{:S(2)}) copy-start(bf16[320,384]{1,0:T(8,128)(2,1)} %reshape.202) | copy-start | bytes 737284
  151.5 34.2 %copy-start.29 = (bf16[320,384]{1,0:T(8,128)(2,1)S(1)}, bf16[320,384]{1,0:T(8,128)(2,1)}, u32[]{:S(2)}) copy-start(bf16[320,384]{1,0:T(8,128)(2,1)} %reshape.203) | copy-start | bytes 737284
  176.2 9.1 %copy-start = (bf16[27,384,384]{2,1,0:T(8,128)(2,1)S(1)}, bf16[27,384,384]{2,1,0:T(8,128)(2,1)}, u32[]{:S(2)}) copy-start(bf16[27,384,384]{2,1,0:T(8,128)(2,1)} %all-gather.7.cloned.1.call-done) | copy-start | bytes 23887876
  176.2 11.9 %copy-start.12 = (bf16[320,384]{1,0:T(8,128)(2,1)S(1)}, bf16[320,384]{1,0:T(8,128)(2,1)}, u32[]{:S(2)}) copy-start(bf16[320,384]{1,0:T(8,128)(2,1)} %reshape.207) | copy-start | bytes 737284
  177.8 10.7 %copy-start.25 = (bf16[320,384]{1,0:T(8,128)(2,1)S(1)}, bf16[320,384]{1,0:T(8,128)(2,1)}, u32[]{:S(2)}) copy-start(bf16[320,384]{1,0:T(8,128)(2,1)} %reshape.208) | copy-start | bytes 737284
  181.0 7.8 %copy-start.23 = (bf16[320,384]{1,0:T(8,128)(2,1)S(1)}, bf16[320,384]{1,0:T(8,128)(2,1)}, u32[]{:S(2)}) copy-start(bf16[320,384]{1,0:T(8,128)(2,1)} %reshape.209) | copy-start | bytes 737284
  182.4 6.7 %copy-start.33 = (bf16[320,384]{1,0:T(8,128)(2,1)S(1)}, bf16[320,384]{1,0:T(8,128)(2,1)}, u32[]{:S(2)}) copy-start(bf16[320,384]{1,0:T(8,128)(2,1)} %reshape.210) | copy-start | bytes 737284
  183.9 5.6 %copy-start.20 = (bf16[320,384]{1,0:T(8,128)(2,1)S(1)}, bf16[320,384]{1,0:T(8,128)(2,1)}, u32[]{:S(2)}) copy-start(bf16[320,384]{1,0:T(8,128)(2,1)} %reshape.212) | copy-start | bytes 737284
  185.3 4.5 %copy-start.10 = (bf16[320,384]{1,0:T(8,128)(2,1)S(1)}, bf16[320,384]{1,0:T(8,128)(2,1)}, u32[]{:S(2)}) copy-start(bf16[320,384]{1,0:T(8,128)(2,1)} %reshape.213) | copy-start | bytes 737284
  185.7 4.5 %copy-start.18 = (bf16[320,384]{1,0:T(8,128)(2,1)S(1)}, bf16[320,384]{1,0:T(8,128)(2,1)}, u32[]{:S(2)}) copy-start(bf16[320,384]{1,0:T(8,128)(2,1)} %reshape.214) | copy-start | bytes 737284
  186.0 4.5 %copy-start.17 = (bf16[320,384]{1,0:T(8,128)(2,1)S(1)}, bf16[320,384]{1,0:T(8,128)(2,1)}, u32[]{:S(2)}) copy-start(bf16[320,384]{1,0:T(8,128)(2,1)} %reshape.215) | copy-start | bytes 737284
  186.4 4.5 %copy-start.8 = (bf16[320,384]{1,0:T(8,128)(2,1)S(1)}, bf16[320,384]{1,0:T(8,128)(2,1)}, u32[]{:S(2)}) copy-start(bf16[320,384]{1,0:T(8,128)(2,1)} %reshape.216) | copy-start | bytes 737284
  187.7 3.5 %copy-start.16 = (bf16[320,384]{1,0:T(8,128)(2,1)S(1)}, bf16[320,384]{1,0:T(8,128)(2,1)}, u32[]{:S(2)}) copy-start(bf16[320,384]{1,0:T(8,128)(2,1)} %reshape.217) | copy-start | bytes 737284
  188.1 3.5 %copy-start.15 = (bf16[320,384]{1,0:T(8,128)(2,1)S(1)}, bf16[320,384]{1,0:T(8,128)(2,1)}, u32[]{:S(2)}) copy-start(bf16[320,384]{1,0:T(8,128)(2,1)} %reshape.218) | copy-start | bytes 737284
  188.4 3.5 %copy-start.4 = (bf16[320,384]{1,0:T(8,128)(2,1)S(1)}, bf16[320,384]{1,0:T(8,128)(2,1)}, u32[]{:S(2)}) copy-start(bf16[320,384]{1,0:T(8,128)(2,1)} %reshape.219) | copy-start | bytes 737284
  189.5 3.5 %copy-start.5 = (bf16[320,384]{1,0:T(8,128)(2,1)S(1)}, bf16[320,384]{1,0:T(8,128)(2,1)}, u32[]{:S(2)}) copy-start(bf16[320,384]{1,0:T(8,128)(2,1)} %reshape.222) | copy-start | bytes 737284
  189.9 3.5 %copy-start.34 = (f32[384]{0:T(512)S(1)}, f32[384]{0:T(512)}, u32[]{:S(2)}) copy-start(f32[384]{0:T(512)} %param.10) | copy-start | bytes 4612
  190.2 3.8 %copy-start.36 = (f32[384]{0:T(512)S(1)}, f32[384]{0:T(512)}, u32[]{:S(2)}) copy-start(f32[384]{0:T(512)} %param.11) | copy-start | bytes 4612
  194.3 6.8 %collective-permute-start.5 = (bf16[2,8,10,384]{3,2,1,0:T(8,128)(2,1)S(1)}, bf16[2,8,10,384]{3,2,1,0:T(8,128)(2,1)S(1)}, u32[]{:S(2)}, u32[]{:S(2)}) collective-permute-start(bf16[2,8,10,384]{3,2,1,0:T(8,128)(2,1)S(1)} %slice.566), channel_id=1, source_target_pairs={{0,64},{64,128},{128,192},{1,65},{65,129},{129,193},{2,66},{66,130... | collective-permute-start | bytes 368648 | tf_op jit(solution)/shard_map/ppermute | solution.py:10
  201.2 7.2 %collective-permute-start.7 = (bf16[6,1,10,384]{3,2,1,0:T(8,128)(2,1)S(1)}, bf16[6,1,10,384]{3,2,1,0:T(8,128)(2,1)S(1)}, u32[]{:S(2)}, u32[]{:S(2)}) collective-permute-start(bf16[6,1,10,384]{3,2,1,0:T(8,128)(2,1)S(1)} %get-tuple-element.66), channel_id=1, source_target_pairs={{16,0},{32,16},{48,32},{17,1},{33,17},{49,33},{18,2},{34,18},{50,3... | collective-permute-start | bytes 138248 | tf_op jit(solution)/shard_map/ppermute | solution.py:21
  202.5 6.8 %collective-permute-start.6 = (bf16[6,1,10,384]{3,2,1,0:T(8,128)(2,1)S(1)}, bf16[6,1,10,384]{3,2,1,0:T(8,128)(2,1)S(1)}, u32[]{:S(2)}, u32[]{:S(2)}) collective-permute-start(bf16[6,1,10,384]{3,2,1,0:T(8,128)(2,1)S(1)} %get-tuple-element.65), channel_id=1, source_target_pairs={{0,16},{16,32},{32,48},{1,17},{17,33},{33,49},{2,18},{18,34},{34,5... | collective-permute-start | bytes 138248 | tf_op jit(solution)/shard_map/ppermute | solution.py:20
  210.1 60.4 %collective-permute-start.8 = (bf16[6,10,1,384]{3,2,1,0:T(2,128)(2,1)}, bf16[6,10,1,384]{3,2,1,0:T(2,128)(2,1)}, u32[]{:S(2)}, u32[]{:S(2)}) collective-permute-start(bf16[6,10,1,384]{3,2,1,0:T(2,128)(2,1)} %get-tuple-element.25), channel_id=1, source_target_pairs={{0,1},{1,2},{2,3},{3,4},{4,5},{5,6},{6,7},{7,8},{8,9},{9,10},{10,1... | collective-permute-start | bytes 138248 | tf_op jit(solution)/shard_map/ppermute | solution.py:20
  215.9 54.6 %collective-permute-start.9 = (bf16[6,10,1,384]{3,2,1,0:T(2,128)(2,1)}, bf16[6,10,1,384]{3,2,1,0:T(2,128)(2,1)}, u32[]{:S(2)}, u32[]{:S(2)}) collective-permute-start(bf16[6,10,1,384]{3,2,1,0:T(2,128)(2,1)} %get-tuple-element.26), channel_id=1, source_target_pairs={{1,0},{2,1},{3,2},{4,3},{5,4},{6,5},{7,6},{8,7},{9,8},{10,9},{11,1... | collective-permute-start | bytes 138248 | tf_op jit(solution)/shard_map/ppermute | solution.py:21
  277.6 22.3 %copy-start.3 = (bf16[4,8,10,384]{3,2,1,0:T(8,128)(2,1)S(1)}, bf16[4,8,10,384]{3,2,1,0:T(8,128)(2,1)}, u32[]{:S(2)}) copy-start(bf16[4,8,10,384]{3,2,1,0:T(8,128)(2,1)} %get-tuple-element.15) | copy-start | bytes 737284
  277.6 22.5 %copy-start.2 = (bf16[4,8,10,384]{3,2,1,0:T(8,128)(2,1)S(1)}, bf16[4,8,10,384]{3,2,1,0:T(8,128)(2,1)}, u32[]{:S(2)}) copy-start(bf16[4,8,10,384]{3,2,1,0:T(8,128)(2,1)} %get-tuple-element.14) | copy-start | bytes 737284
  299.9 13.8 %copy-start.30 = (bf16[320,384]{1,0:T(8,128)(2,1)S(1)}, bf16[320,384]{1,0:T(8,128)(2,1)}, u32[]{:S(2)}) copy-start(bf16[320,384]{1,0:T(8,128)(2,1)} %reshape.234) | copy-start | bytes 737284
  300.1 15.0 %copy-start.13 = (bf16[320,384]{1,0:T(8,128)(2,1)S(1)}, bf16[320,384]{1,0:T(8,128)(2,1)}, u32[]{:S(2)}) copy-start(bf16[320,384]{1,0:T(8,128)(2,1)} %reshape.235) | copy-start | bytes 737284
  300.3 16.1 %slice-start = ((s8[7962624]{0:T(1024)(128)(4,1)}), s8[4194304]{0:T(1024)(128)(4,1)S(1)}, s32[]{:S(2)}) async-start(s8[7962624]{0:T(1024)(128)(4,1)} %bitcast.217), calls=%async_computation.4 | async-start | bytes 8388608
  300.3 16.1 %copy-start.28 = (bf16[320,384]{1,0:T(8,128)(2,1)S(1)}, bf16[320,384]{1,0:T(8,128)(2,1)}, u32[]{:S(2)}) copy-start(bf16[320,384]{1,0:T(8,128)(2,1)} %reshape.236) | copy-start | bytes 737284
  303.3 13.4 %copy-start.27 = (bf16[320,384]{1,0:T(8,128)(2,1)S(1)}, bf16[320,384]{1,0:T(8,128)(2,1)}, u32[]{:S(2)}) copy-start(bf16[320,384]{1,0:T(8,128)(2,1)} %reshape.237) | copy-start | bytes 737284
  304.8 12.3 %copy-start.32 = (bf16[320,384]{1,0:T(8,128)(2,1)S(1)}, bf16[320,384]{1,0:T(8,128)(2,1)}, u32[]{:S(2)}) copy-start(bf16[320,384]{1,0:T(8,128)(2,1)} %reshape.238) | copy-start | bytes 737284
  306.2 11.2 %copy-start.24 = (bf16[320,384]{1,0:T(8,128)(2,1)S(1)}, bf16[320,384]{1,0:T(8,128)(2,1)}, u32[]{:S(2)}) copy-start(bf16[320,384]{1,0:T(8,128)(2,1)} %reshape.240) | copy-start | bytes 737284
  307.7 8.7 %slice-start.1 = ((s8[7962624]{0:T(1024)(128)(4,1)}), s8[3768320]{0:T(1024)(128)(4,1)S(1)}, s32[]{:S(2)}) async-start(s8[7962624]{0:T(1024)(128)(4,1)} %bitcast.217), calls=%async_computation.5 | async-start | bytes 7536640
  307.7 10.1 %copy-start.11 = (bf16[320,384]{1,0:T(8,128)(2,1)S(1)}, bf16[320,384]{1,0:T(8,128)(2,1)}, u32[]{:S(2)}) copy-start(bf16[320,384]{1,0:T(8,128)(2,1)} %reshape.241) | copy-start | bytes 737284
  309.3 8.9 %copy-start.22 = (bf16[320,384]{1,0:T(8,128)(2,1)S(1)}, bf16[320,384]{1,0:T(8,128)(2,1)}, u32[]{:S(2)}) copy-start(bf16[320,384]{1,0:T(8,128)(2,1)} %reshape.242) | copy-start | bytes 737284
  310.8 7.7 %copy-start.21 = (bf16[320,384]{1,0:T(8,128)(2,1)S(1)}, bf16[320,384]{1,0:T(8,128)(2,1)}, u32[]{:S(2)}) copy-start(bf16[320,384]{1,0:T(8,128)(2,1)} %reshape.243) | copy-start | bytes 737284
  312.2 6.6 %copy-start.9 = (bf16[320,384]{1,0:T(8,128)(2,1)S(1)}, bf16[320,384]{1,0:T(8,128)(2,1)}, u32[]{:S(2)}) copy-start(bf16[320,384]{1,0:T(8,128)(2,1)} %reshape.244) | copy-start | bytes 737284
  313.7 5.5 %copy-start.19 = (bf16[320,384]{1,0:T(8,128)(2,1)S(1)}, bf16[320,384]{1,0:T(8,128)(2,1)}, u32[]{:S(2)}) copy-start(bf16[320,384]{1,0:T(8,128)(2,1)} %reshape.245) | copy-start | bytes 737284
  317.8 3.3 copy-start.6
  318.5 3.3 %copy-start.37 = (f32[384]{0:T(512)S(1)}, f32[384]{0:T(512)}, u32[]{:S(2)}) copy-start(f32[384]{0:T(512)} %param.13) | copy-start | bytes 4612
Sparse Core Ops, SparseCore 0:
  9.2 44.1 all-gather.4
  55.2 38.3 all-gather.8
  95.4 80.7 all-gather.6
  177.9 84.2 all-gather.10
where the time goes:
time: 331 us; the launch traced here: 329 us
  waiting for transfers between devices  159 us (48%)
  local copies, waits for them, and re-layouts  79.1 us (24%)
  matrix products  39.5 us (12%)
  starting transfers between devices  32 us (10%)
  between operations  14.3 us (4%)
  other arithmetic  5.48 us (2%)
    all_gather x2, waiting for transfers between devices, convolve(): row_kernel = lax.all_gather(kernel, 'width', axis=1, tiled=True)  81.8 us
    all_gather x2, waiting for transfers between devices, convolve(): lax.all_gather(row_kernel, 'height', axis=1, tiled=True)  66.6 us
    reshape x53, local copies, waits for them, and re-layouts, fold_piece(): window.reshape(-1, count_in)  63 us
    dot_general x54, matrix products, fold_piece(): jnp.dot(window.reshape(-1, count_in), piece[9 * step_t + 3 * step_h + ste...  39.5 us
    ppermute x4, starting transfers between devices, extended(): before = lax.ppermute(last, axis, up)  18.9 us
    slice x6, local copies, waits for them, and re-layouts, fold_piece(): widened[step_t:step_t + frames, step_h:step_h + rows, step_w:step_w + cols]  7.5 us
    all_gather x2, local copies, waits for them, and re-layouts, convolve(): row_kernel = lax.all_gather(kernel, 'width', axis=1, tiled=True)  7.38 us
    ppermute x2, waiting for transfers between devices, passed_along(): return lax.ppermute(x, axis, pairs)  6.76 us
  transfers between devices with their start and end apart: 14, of which 8 were waited for; matrix products, arithmetic and copies ran while one was open for 22% of the time, Pallas kernels for 0%

commit v1 on v0

v1 whole, which is shorter than its diff:
```python
import jax
import jax.numpy as jnp
from jax import lax
from jax.experimental import pallas as pl
from jax.experimental.pallas import tpu as pltpu
from jax.sharding import Mesh, PartitionSpec as P

AXES = ("t", "h", "z", "c")
SHIFT = ((0, 4), (1, -3), (-1, 3), (2, -2))
MAIN = tuple(t for t in range(27) if t % 3 != 1)
PAIRED = (1, 4, 7, 10, 13, 16)
ALONE = (19, 22, 25)
GROUPS = len(MAIN) + len(ALONE)
CHANS = 384
LANES = 256
WIDE = 32
BF = jnp.bfloat16
F32 = jnp.float32
VMEM = pltpu.CompilerParams(vmem_limit_bytes=56 * 2**20)
whole = pl.BlockSpec(memory_space=pltpu.VMEM)
scalars = pl.BlockSpec(memory_space=pltpu.SMEM)


def move(x, sizes, source):
    def place(at):
        index = 0
        for coordinate, size in zip(at, sizes):
            index = index * size + coordinate % size
        return index

    pairs = []
    for index in range(sizes[0] * sizes[1] * sizes[2] * sizes[3]):
        rest, c = divmod(index, sizes[3])
        rest, z = divmod(rest, sizes[2])
        t, h = divmod(rest, sizes[1])
        at = source(t, h, z, c)
        if at is not None:
            pairs.append((place(at), index))
    return lax.ppermute(x, AXES, pairs)


def fold_kernel(k_ref, out_ref):
    for g in range(GROUPS):
        if g < len(MAIN):
            low = k_ref[MAIN[g]].astype(F32)
            k = 2 * (g % 3)
            high = k_ref[PAIRED[g // 3]].astype(F32)[k : k + 2]
        else:
            low = k_ref[ALONE[g - len(MAIN)]].astype(F32)
            high = jnp.zeros((2, CHANS), F32)
        out_ref[g] = jnp.concatenate([low, high], axis=0).astype(BF)


def fold(kernel):
    return pl.pallas_call(
        fold_kernel,
        out_shape=jax.ShapeDtypeStruct((GROUPS, 8, CHANS), BF),
        in_specs=[whole],
        out_specs=whole,
        name="fold",
    )(kernel)


def spread(place_ref):
    t, h, z, c = (place_ref[0], place_ref[1], place_ref[2], place_ref[3])
    lane = lax.broadcasted_iota(jnp.int32, (1, LANES), 1)
    j = lane & 7
    p = lane >> 3
    outer, inner, far = p >> 3, (p >> 1) & 3, p & 1
    t_of = (t + jnp.where(c == 0, inner, outer)) & 3
    h_of = (h + jnp.where(c == 0, outer, inner)) & 3
    shift = jnp.where(t_of == 0, 0, jnp.where(t_of == 1, 1, jnp.where(t_of == 2, 7, 2)))
    z_of = (z + shift + 4 * far) & 7
    base = 96 * h_of + 12 * z_of + 6 * c
    chan = lax.broadcasted_iota(jnp.int32, (CHANS, LANES), 0)
    matrices = [jnp.where(chan == jnp.where(j < 6, base + j, -1), 1.0, 0.0)]
    for k in range(3):
        wanted = jnp.where(j >= 6, base + 2 * k + j - 6, -1)
        matrices.append(jnp.where(chan == wanted, 1.0, 0.0))
    return [m.astype(BF) for m in matrices]


def activated(values, gain):
    square_mean = jnp.mean(values * values, axis=-1, keepdims=True)
    normed = values * lax.rsqrt(square_mean + 1e-06) * gain
    return normed * jax.nn.sigmoid(normed)


def lay_out(active, rows, place_ref, out_ref):
    p0, p1, p2, p3 = spread(place_ref)
    count = rows * 24

    def put(slot, value, matrix):
        laid = jnp.dot(value, matrix, preferred_element_type=F32).astype(BF)
        out_ref[slot, 0, :, 0:24, :] = laid.reshape(rows, 24, LANES)

    put(0, active.astype(BF), p0)
    one = pltpu.roll(active, count - 1, 0).astype(BF)
    put(1, one, p0)
    put(3, one, p1)
    put(4, one, p2)
    put(5, one, p3)
    put(2, pltpu.roll(active, count - 2, 0).astype(BF), p0)


def first_layout_kernel(place_ref, x_ref, gain_ref, out_ref):
    values = x_ref[0].astype(F32).reshape(12 * 24, CHANS)
    lay_out(activated(values, gain_ref[...]), 12, place_ref, out_ref)


def first_layout(place, features, gain):
    return pl.pallas_call(
        first_layout_kernel,
        grid=(8,),
        out_shape=jax.ShapeDtypeStruct((6, 8, 12, WIDE, LANES), BF),
        in_specs=[
            scalars,
            pl.BlockSpec((1, 12, 24, CHANS), lambda f: (f, 0, 0, 0)),
            pl.BlockSpec((1, CHANS), lambda f: (0, 0)),
        ],
        out_specs=pl.BlockSpec((6, 1, 12, WIDE, LANES), lambda f: (0, f, 0, 0, 0)),
        compiler_params=VMEM,
        name="first_layout",
    )(place, features, gain)


def second_layout_kernel(place_ref, mine_ref, other_ref, bias_ref, gain_ref, out_ref):
    frame = pl.program_id(0) - 2 + 4 * place_ref[0]
    total = mine_ref[0] + other_ref[0].astype(F32)
    total = total.reshape(10 * 24, CHANS) + bias_ref[...]
    active = activated(total.astype(BF).astype(F32), gain_ref[...])
    index = lax.broadcasted_iota(jnp.int32, (10, 24, 1), 0)
    row = index + 8 * place_ref[1] - 1
    col = lax.broadcasted_iota(jnp.int32, (10, 24, 1), 1) + 20 * place_ref[2] - 1
    inside = (row >= 0) & (row < 32) & (col >= 0) & (col < 160) & (frame >= 0)
    keep = jnp.where(inside, 1.0, 0.0)
    active = (active.reshape(10, 24, CHANS) * keep).reshape(10 * 24, CHANS)
    lay_out(active, 10, place_ref, out_ref)


def second_layout(place, mine, other, bias, gain):
    return pl.pallas_call(
        second_layout_kernel,
        grid=(6,),
        out_shape=jax.ShapeDtypeStruct((6, 6, 10, WIDE, LANES), BF),
        in_specs=[
            scalars,
            pl.BlockSpec((1, 10, 24, CHANS), lambda f: (f, 0, 0, 0)),
            pl.BlockSpec((1, 10, 24, CHANS), lambda f: (f, 0, 0, 0)),
            pl.BlockSpec((1, CHANS), lambda f: (0, 0)),
            pl.BlockSpec((1, CHANS), lambda f: (0, 0)),
        ],
        out_specs=pl.BlockSpec((6, 1, 10, WIDE, LANES), lambda f: (0, f, 0, 0, 0)),
        compiler_params=VMEM,
        name="second_layout",
    )(place, mine, other, bias, gain)


def tap_sum(laid_ref, blocks, first, frames, rows):
    def window(slot, tap):
        dt, dh = tap // 9, tap % 9 // 3
        at = pl.ds(first + dt, frames)
        return laid_ref[slot, at, dh : dh + rows].reshape(-1, LANES)

    total = jnp.zeros((frames * rows * WIDE, CHANS), F32)
    for g in range(GROUPS):
        if g < len(MAIN):
            left = window(MAIN[g] % 3, MAIN[g]) + window(3 + g % 3, PAIRED[g // 3])
        else:
            left = window(1, ALONE[g - len(MAIN)])
        right = jnp.concatenate([b[i, g] for b in blocks for i in range(b.shape[0])], axis=0)
        total = total + jnp.dot(left, right, preferred_element_type=F32)
    return total.reshape(frames, rows, WIDE, CHANS)


def first_conv_kernel(laid_ref, b0, b1, b2, b3, b4, mine_ref, sent_ref):
    step = pl.program_id(0)
    total = tap_sum(laid_ref, (b0, b1, b2, b3, b4), 2 * step, 2, 10)[:, :, 0:24]
    mine_ref[...] = total
    sent_ref[...] = total.astype(BF)


def first_conv(laid, blocks):
    out = pl.BlockSpec((2, 10, 24, CHANS), lambda f: (f, 0, 0, 0))
    return pl.pallas_call(
        first_conv_kernel,
        grid=(3,),
        out_shape=(
            jax.ShapeDtypeStruct((6, 10, 24, CHANS), F32),
            jax.ShapeDtypeStruct((6, 10, 24, CHANS), BF),
        ),
        in_specs=[whole] * 6,
        out_specs=(out, out),
        compiler_params=VMEM,
        name="first_conv",
    )(laid, *blocks)


def second_conv_kernel(place_ref, laid_ref, b0, b1, b2, b3, b4, mine_ref, sent_ref):
    step = pl.program_id(0)
    total = tap_sum(laid_ref, (b0, b1, b2, b3, b4), 2 * step, 2, 8)
    left, right = total[:, :, 0:10], total[:, :, 10:20]
    low = place_ref[3] == 0
    mine_ref[...] = jnp.where(low, left, right)
    sent_ref[...] = jnp.where(low, right, left)


def second_conv(place, laid, blocks):
    out = pl.BlockSpec((2, 8, 10, CHANS), lambda f: (f, 0, 0, 0))
    return pl.pallas_call(
        second_conv_kernel,
        grid=(2,),
        out_shape=(
            jax.ShapeDtypeStruct((4, 8, 10, CHANS), F32),
            jax.ShapeDtypeStruct((4, 8, 10, CHANS), F32),
        ),
        in_specs=[scalars] + [whole] * 6,
        out_specs=(out, out),
        compiler_params=VMEM,
        name="second_conv",
    )(place, laid, *blocks)


def solution(mesh):
    sizes = (mesh.shape["tm"], mesh.shape["height"], mesh.shape["width"] // 2, 2)
    split = Mesh(mesh.devices.reshape(sizes), AXES)

    def sent(x, source):
        return move(x, sizes, source)

    def along(first, step):
        def source(t, h, z, c):
            return (t + step, h, z, c) if (c == 0) == first else (t, h + step, z, c)

        return source

    def z_stage(x):
        near = sent(x, lambda t, h, z, c: (t, h, z + SHIFT[t][0], c))
        far = sent(x, lambda t, h, z, c: (t, h, z + SHIFT[t][1], c))
        return jnp.concatenate([near, far], axis=1)

    def first_ring(x):
        up, down = sent(x, along(True, 1)), sent(x, along(True, -1))
        return jnp.stack([x, up, sent(x, along(True, 2)), down])

    def second_ring(x):
        up, down = sent(x, along(False, 1)), sent(x, along(False, -1))
        half = sent(up[:2], along(False, 1))
        other = sent(down[2:], along(False, -1))
        return x, up, half, other, down

    def swapped(x):
        return sent(x, lambda t, h, z, c: (t, h, z, 1 - c))

    def inner(at, d):
        return at if all(0 <= a < s for a, s in zip(at, sizes)) else None

    def widened(x, core):
        earlier = sent(x, lambda t, h, z, c: inner((t - 1, h, z, c), 0))
        x = jnp.concatenate([earlier, x], axis=0)
        above = sent(x[:, -2:], lambda t, h, z, c: inner((t, h - 1, z, c), 0))
        below = sent(x[:, :2], lambda t, h, z, c: inner((t, h + 1, z, c), 0))
        x = jnp.concatenate([above, x, below], axis=1)
        edge = jnp.where(core == 0, x[:, :, :2], x[:, :, -2:])
        beside = sent(edge, lambda t, h, z, c: inner((t, h, z + 2 * c - 1, 1 - c), 0))
        mine = jnp.where(
            core == 0,
            jnp.concatenate([beside, x], axis=2),
            jnp.concatenate([x, beside], axis=2),
        )
        other = swapped(mine)
        return jnp.where(
            core == 0,
            jnp.concatenate([mine, other], axis=2),
            jnp.concatenate([other, mine], axis=2),
        )

    def on_device(features, gain_1, kernel_1, bias_1, gain_2, kernel_2, bias_2):
        place = jnp.stack([lax.axis_index(a) for a in AXES]).astype(jnp.int32)
        core = lax.axis_index("c")
        one = first_ring(z_stage(fold(kernel_1)))
        two = first_ring(z_stage(fold(kernel_2)))
        laid = first_layout(place, widened(features, core), gain_1.reshape(1, CHANS))
        mine, passed = first_conv(laid, second_ring(one))
        laid = second_layout(
            place, mine, swapped(passed), bias_1.reshape(1, CHANS), gain_2.reshape(1, CHANS)
        )
        mine, passed = second_conv(place, laid, second_ring(two))
        total = mine + swapped(passed) + bias_2 + features.astype(F32)
        return total.astype(BF)

    volume = P("t", "h", ("z", "c"), None)
    weights = P(None, ("h", "z", "c"), None)
    return jax.shard_map(
        on_device,
        mesh=split,
        in_specs=(volume, P(), weights, P(), P(), weights, P()),
        out_specs=volume,
        check_vma=False,
    )
```

time: 331 us -> 157 us (0.47)
  waiting for transfers between devices: 159 us -> 27.3 us
  local copies, waits for them, and re-layouts: 79.1 us -> 17.7 us
  Pallas kernels: 0 us -> 48.4 us
  matrix products: 39.5 us -> 0 us
  starting transfers between devices: 32 us -> 56.6 us
  between operations: 14.3 us -> 0.25 us
    all_gather x4 -> x0, waiting for transfers between devices: 148 us -> none  [the longest x2 81.8 us: convolve(): row_kernel = lax.all_gather(kernel, 'width', axis=1, tiled=True)]
    reshape x55 -> x3, local copies, waits for them, and re-layouts: 63.1 us -> 1.7 us  [the longest x1 0.58 us: on_device(): gain_2.reshape(1, CHANS)]
    pallas_call x0 -> x6, Pallas kernels: none -> 48.4 us  [the longest x1 17.1 us: first_conv(): pl.pallas_call(first_conv_kernel, grid=(3,), out_shape=(jax.ShapeDtypeStr...]
    dot_general x54 -> x0, matrix products: 39.5 us -> none  [fold_piece(): jnp.dot(window.reshape(-1, count_in), piece[9 * step_t + 3 * step_h + ste...]
    ppermute x10 -> x25, starting transfers between devices: 31.9 us -> 56.6 us  [move(): return lax.ppermute(x, AXES, pairs)]
    ppermute x10 -> x25, waiting for transfers between devices: 8.99 us -> 27.3 us  [move(): return lax.ppermute(x, AXES, pairs)]
    all_gather x2 -> x0, local copies, waits for them, and re-layouts: 7.38 us -> none  [convolve(): row_kernel = lax.all_gather(kernel, 'width', axis=1, tiled=True)]
    unnamed x80 -> x34, local copies, waits for them, and re-layouts: 0.17 us -> 6.01 us
  transfers between devices with their start and end apart: 14 -> 25, of which waited for: 8 -> 7; matrix products, arithmetic and copies ran while one was open for 22% -> 11% of each run, Pallas kernels for 0% -> 23%
where the time goes in v1:
time: 157 us; the launch traced here: 156 us
  starting transfers between devices  56.6 us (36%)
  Pallas kernels  48.4 us (31%)
  waiting for transfers between devices  27.3 us (17%)
  local copies, waits for them, and re-layouts  17.7 us (11%)
  other arithmetic  5.99 us (4%)
    ppermute x25, starting transfers between devices, move(): return lax.ppermute(x, AXES, pairs)  56.6 us
    ppermute x25, waiting for transfers between devices, move(): return lax.ppermute(x, AXES, pairs)  27.3 us
    pallas_call x1, Pallas kernels, first_conv(): pl.pallas_call(first_conv_kernel, grid=(3,), out_shape=(jax.ShapeDtypeStr...  17.1 us
    pallas_call x1, Pallas kernels, second_conv(): pl.pallas_call(second_conv_kernel, grid=(2,), out_shape=(jax.ShapeDtypeSt...  10.8 us
    pallas_call x1, Pallas kernels, first_layout(): pl.pallas_call(first_layout_kernel, grid=(8,), out_shape=jax.ShapeDtypeSt...  9.61 us
    pallas_call x1, Pallas kernels, second_layout(): pl.pallas_call(second_layout_kernel, grid=(6,), out_shape=jax.ShapeDtypeS...  7.79 us
    unnamed x34, local copies, waits for them, and re-layouts  6.01 us
    pallas_call x2, Pallas kernels, fold(): pl.pallas_call(fold_kernel, out_shape=jax.ShapeDtypeStruct((GROUPS, 8, CH...  3.18 us
  transfers between devices with their start and end apart: 25, of which 7 were waited for; matrix products, arithmetic and copies ran while one was open for 11% of the time, Pallas kernels for 23%

profile of v1, /device:TPU:1, one launch (start us, length us, event | category | flops | bytes accessed | tf_op | source)
XLA Modules:
  0.0 156.3 jit_solution(5573797071213715946)
XLA Ops:
  0.0 1.7 %copy.19.k_ref = bf16[27,6,384]{2,1,0:T(8,128)(2,1)} copy(bf16[27,6,384]{2,0,1:T(8,128)(2,1)} %param.9) | data formatting | bytes 248832 | tf_op args[2]
  1.7 1.6 %fold.2 = bf16[21,8,384]{2,1,0:T(8,128)(2,1)} custom-call(bf16[27,6,384]{2,1,0:T(8,128)(2,1)} %copy.19.k_ref), custom_call_target="tpu_custom_call" | custom-call | tf_op jit(solution)/shard_map/fold/pallas_call | solution.py:55
  3.3 1.5 collective-permute-start.5
  4.8 1.0 copy.14
  5.8 10.0 %collective-permute-start = (bf16[4,8,10,384]{3,2,1,0:T(8,128)(2,1)S(1)}, bf16[4,8,10,384]{3,2,1,0:T(8,128)(2,1)S(1)}, u32[]{:S(2)}, u32[]{:S(2)}) collective-permute-start(bf16[4,8,10,384]{3,2,1,0:T(8,128)(2,1)S(1)} %copy.14), channel_id=1, source_target_pairs={{0,64},{1,65},{2,66},{3,67},{4,68},{5,69},{6,70},{7,71},{8,72},{9,... | collective-permute-start | bytes 737288 | tf_op jit(solution)/shard_map/ppermute | solution.py:39
  15.8 1.4 collective-permute-start.6
  17.2 0.0 collective-permute-done.5
  17.2 9.5 %collective-permute-done.6 = bf16[21,8,384]{2,1,0:T(8,128)(2,1)S(1)} collective-permute-done((bf16[21,8,384]{2,1,0:T(8,128)(2,1)}, bf16[21,8,384]{2,1,0:T(8,128)(2,1)S(1)}, u32[]{:S(2)}, u32[]{:S(2)}) %collective-permute-start.6) | collective-permute-done | bytes 129056 | tf_op jit(solution)/shard_map/ppermute | solution.py:39
  26.8 2.6 %collective-permute-start.7 = (bf16[21,16,384]{2,1,0:T(8,128)(2,1)S(1)}, bf16[21,16,384]{2,1,0:T(8,128)(2,1)S(1)}, u32[]{:S(2)}, u32[]{:S(2)}) collective-permute-start(bf16[21,16,384]{2,1,0:T(8,128)(2,1)S(1)} %constant_dynamic-update-slice_fusion.1), channel_id=1, source_target_pairs={{64,0},{17,1},{66,2},{19,3},{68,4},{21,5},{70,6},{23,7},{72,8},{25... | collective-permute-start | bytes 774152 | tf_op jit(solution)/shard_map/ppermute | solution.py:39
  29.4 0.5 collective-permute-start.8
  29.9 0.6 collective-permute-start.9
  30.5 0.0 collective-permute-done
  30.6 0.1 copy_dynamic-update-slice_fusion
  30.6 4.8 %collective-permute-done.7 = bf16[21,16,384]{2,1,0:T(8,128)(2,1)S(1)} collective-permute-done((bf16[21,16,384]{2,1,0:T(8,128)(2,1)S(1)}, bf16[21,16,384]{2,1,0:T(8,128)(2,1)S(1)}, u32[]{:S(2)}, u32[]{:S(2)}) %collective-permute-start.7) | collective-permute-done | bytes 258080 | tf_op jit(solution)/shard_map/ppermute | solution.py:39
  35.4 0.7 collective-permute-done.8
  36.2 2.7 %collective-permute-done.9 = bf16[21,16,384]{2,1,0:T(8,128)(2,1)S(1)} collective-permute-done((bf16[21,16,384]{2,1,0:T(8,128)(2,1)S(1)}, bf16[21,16,384]{2,1,0:T(8,128)(2,1)S(1)}, u32[]{:S(2)}, u32[]{:S(2)}) %collective-permute-start.9) | collective-permute-done | bytes 258080 | tf_op jit(solution)/shard_map/ppermute | solution.py:39
  38.8 0.2 pad_maximum_fusion.b0
  39.0 0.1 collective-permute-start.10
  39.1 1.3 collective-permute-start.1
  40.5 1.3 collective-permute-start.2
  41.8 1.5 collective-permute-start.12
  43.3 6.2 %collective-permute-done.2 = bf16[8,2,10,384]{3,2,1,0:T(8,128)(2,1)S(1)} collective-permute-done((bf16[8,2,10,384]{3,2,1,0:T(8,128)(2,1)S(1)}, bf16[8,2,10,384]{3,2,1,0:T(8,128)(2,1)S(1)}, u32[]{:S(2)}, u32[]{:S(2)}) %collective-permute-start.2) | collective-permute-done | bytes 122912 | tf_op jit(solution)/shard_map/ppermute | solution.py:39
  49.4 0.2 broadcast_select_fusion
  49.6 11.3 %collective-permute-start.3 = (bf16[8,12,2,384]{3,2,1,0:T(2,128)(2,1)S(1)}, bf16[8,12,2,384]{3,2,1,0:T(2,128)(2,1)}, u32[]{:S(2)}, u32[]{:S(2)}) collective-permute-start(bf16[8,12,2,384]{3,2,1,0:T(2,128)(2,1)S(1)} %broadcast_select_fusion), channel_id=1, source_target_pairs={{2,1},{1,2},{4,3},{3,4},{6,5},{5,6},{8,7},{7,8},{10,9},{9,10},{12,... | collective-permute-start | bytes 442376 | tf_op jit(solution)/shard_map/ppermute | solution.py:39
  60.9 0.7 copy.20.k_ref
  61.6 1.6 %fold.3 = bf16[21,8,384]{2,1,0:T(8,128)(2,1)} custom-call(bf16[27,6,384]{2,1,0:T(8,128)(2,1)} %copy.20.k_ref), custom_call_target="tpu_custom_call" | custom-call | tf_op jit(solution)/shard_map/fold/pallas_call | solution.py:55
  63.2 1.5 collective-permute-start.15
  64.8 2.4 %collective-permute-start.16 = (bf16[21,8,384]{2,1,0:T(8,128)(2,1)}, bf16[21,8,384]{2,1,0:T(8,128)(2,1)S(1)}, u32[]{:S(2)}, u32[]{:S(2)}) collective-permute-start(bf16[21,8,384]{2,1,0:T(8,128)(2,1)} %fold.3), channel_id=1, source_target_pairs={{8,0},{9,1},{10,2},{11,3},{12,4},{13,5},{14,6},{15,7},{0,8},{1,9},... | collective-permute-start | bytes 387080 | tf_op jit(solution)/shard_map/ppermute | solution.py:39
  67.2 0.0 collective-permute-done.3
  67.2 2.1 %maximum_select_fusion.1 = bf16[8,12,12,384]{3,2,1,0:T(8,128)(2,1)S(1)} fusion(bf16[8,2,10,384]{3,2,1,0:T(8,128)(2,1)} %copy-done.6, bf16[8,8,10,384]{3,2,1,0:T(8,128)(2,1)S(1)} %copy_dynamic-update-slice_fusion, bf16[8,2,10,384]{3,2,1,0:T(8,128)(2,1)S(1)} %collective-permute-done.1, bf16[8,12,2,384]{3,2,1,0:T(2,128)(2,1)} %collective-permute-done.3, pred[]{:T(512)S(6)} %eq.2), kind=kLoop, calls=%fused_computation.1 | loop fusion | flops 7520256 | bytes 1769473 | tf_op jit(solution)/shard_map/jit(_where)/select_n | solution.py:266
  69.3 1.5 copy.16
  70.7 2.1 %collective-permute-start.4 = (bf16[8,12,12,384]{3,0,2,1:T(8,128)(2,1)}, bf16[8,12,12,384]{3,0,2,1:T(8,128)(2,1)}, u32[]{:S(2)}, u32[]{:S(2)}) collective-permute-start(bf16[8,12,12,384]{3,0,2,1:T(8,128)(2,1)} %copy.16), channel_id=1, source_target_pairs={{1,0},{0,1},{3,2},{2,3},{5,4},{4,5},{7,6},{6,7},{9,8},{8,9},{11,10... | collective-permute-start | bytes 2654216 | tf_op jit(solution)/shard_map/ppermute | solution.py:39
  72.8 1.9 %collective-permute-done.16 = bf16[21,8,384]{2,1,0:T(8,128)(2,1)S(1)} collective-permute-done((bf16[21,8,384]{2,1,0:T(8,128)(2,1)}, bf16[21,8,384]{2,1,0:T(8,128)(2,1)S(1)}, u32[]{:S(2)}, u32[]{:S(2)}) %collective-permute-start.16) | collective-permute-done | bytes 129056 | tf_op jit(solution)/shard_map/ppermute | solution.py:39
  74.8 3.0 %collective-permute-start.18 = (bf16[21,16,384]{2,1,0:T(8,128)(2,1)S(1)}, bf16[21,16,384]{2,1,0:T(8,128)(2,1)S(1)}, u32[]{:S(2)}, u32[]{:S(2)}) collective-permute-start(bf16[21,16,384]{2,1,0:T(8,128)(2,1)S(1)} %constant_dynamic-update-slice_fusion.3), channel_id=1, source_target_pairs={{128,0},{33,1},{130,2},{35,3},{132,4},{37,5},{134,6},{39,7},{136,8... | collective-permute-start | bytes 774152 | tf_op jit(solution)/shard_map/ppermute | solution.py:39
  77.8 2.7 %collective-permute-start.17 = (bf16[21,16,384]{2,1,0:T(8,128)(2,1)S(1)}, bf16[21,16,384]{2,1,0:T(8,128)(2,1)S(1)}, u32[]{:S(2)}, u32[]{:S(2)}) collective-permute-start(bf16[21,16,384]{2,1,0:T(8,128)(2,1)S(1)} %constant_dynamic-update-slice_fusion.3), channel_id=1, source_target_pairs={{64,0},{17,1},{66,2},{19,3},{68,4},{21,5},{70,6},{23,7},{72,8},{25... | collective-permute-start | bytes 774152 | tf_op jit(solution)/shard_map/ppermute | solution.py:39
  80.5 1.9 %slice.34 = bf16[2,21,16,384]{3,2,1,0:T(8,128)(2,1)} slice(bf16[4,21,16,384]{3,2,1,0:T(8,128)(2,1)} %collective-permute-done.10.b1), slice={[0:2], [0:21], [0:16], [0:384]} | slice | bytes 1032192 | tf_op jit(solution)/shard_map/slice | solution.py:248
  82.4 3.5 %collective-permute-start.11 = (bf16[2,21,16,384]{3,2,1,0:T(8,128)(2,1)}, bf16[2,21,16,384]{3,2,1,0:T(8,128)(2,1)}, u32[]{:S(2)}, u32[]{:S(2)}) collective-permute-start(bf16[2,21,16,384]{3,2,1,0:T(8,128)(2,1)} %slice.34), channel_id=1, source_target_pairs={{16,0},{65,1},{18,2},{67,3},{20,4},{69,5},{22,6},{71,7},{24,8},{73... | collective-permute-start | bytes 1548296 | tf_op jit(solution)/shard_map/ppermute | solution.py:39
  85.9 1.9 %slice.35 = bf16[2,21,16,384]{3,2,1,0:T(8,128)(2,1)} slice(bf16[4,21,16,384]{3,2,1,0:T(8,128)(2,1)} %collective-permute-done.12.b4), slice={[2:4], [0:21], [0:16], [0:384]} | slice | bytes 1032192 | tf_op jit(solution)/shard_map/slice | solution.py:249
  87.8 0.0 collective-permute-start.13
  87.8 0.2 pad_maximum_fusion.1.b0
  88.0 2.7 %collective-permute-start.20 = (bf16[4,21,16,384]{3,2,1,0:T(8,128)(2,1)S(1)}, bf16[4,21,16,384]{3,2,1,0:T(8,128)(2,1)S(1)}, u32[]{:S(2)}, u32[]{:S(2)}) collective-permute-start(bf16[4,21,16,384]{3,2,1,0:T(8,128)(2,1)S(1)} %pad_maximum_fusion.1.b0), channel_id=1, source_target_pairs={{16,0},{65,1},{18,2},{67,3},{20,4},{69,5},{22,6},{71,7},{24,8},{73... | collective-permute-start | bytes 3096584 | tf_op jit(solution)/shard_map/ppermute | solution.py:39
  90.7 0.6 reshape.10.gain_ref
  91.3 0.6 pad_add_fusion.place_ref
  91.9 1.3 copy.17
  93.2 2.7 %maximum_select_fusion.x_ref = bf16[8,12,24,384]{3,2,1,0:T(8,128)(2,1)} fusion(bf16[8,12,12,384]{3,2,1,0:T(8,128)(2,1)S(1)} %copy.17, bf16[8,12,12,384]{3,2,1,0:T(8,128)(2,1)S(1)} %maximum_select_fusion.1, pred[]{:T(512)S(6)} %eq.2), kind=kLoop, calls=%fused_computation | loop fusion | flops 7962624 | bytes 3538945 | tf_op jit(solution)/shard_map/jit(_where)/select_n | solution.py:272
  95.9 9.6 %first_layout.1.laid_ref = bf16[6,8,12,32,256]{4,3,2,1,0:T(8,128)(2,1)} custom-call(s32[4]{0:T(128)} %pad_add_fusion.place_ref, bf16[8,12,24,384]{3,2,1,0:T(8,128)(2,1)} %maximum_select_fusion.x_ref, f32[1,384]{1,0:T(1,128)} %reshape.10.gain_ref), custom_call_target="tpu_custom_call" | custom-call | tf_op jit(solution)/shard_map/first_layout/pallas_call | solution.py:112
  105.5 17.1 %first_conv.1 = (f32[6,10,24,384]{3,2,1,0:T(8,128)}, bf16[6,10,24,384]{3,2,1,0:T(8,128)(2,1)}) custom-call(bf16[6,8,12,32,256]{4,3,2,1,0:T(8,128)(2,1)} %first_layout.1.laid_ref, bf16[4,21,16,384]{3,2,1,0:T(8,128)(2,1)} %copy-done, bf16[4,21,16,384]{3,2,1,0:T(8,128)(2,1)} %collective-permute-done.10.b1, bf16[2,21,16,384]{3,2,1,0:T(8,128)(2,1)} %collective-permute-done.11.b2, ...), custom_call_target="tpu_custom_call" | custom-call | tf_op jit(solution)/shard_map/first_conv/pallas_call | solution.py:185
  122.6 3.0 %collective-permute-start.14 = (bf16[6,10,24,384]{3,2,1,0:T(8,128)(2,1)}, bf16[6,10,24,384]{3,2,1,0:T(8,128)(2,1)S(1)}, u32[]{:S(2)}, u32[]{:S(2)}) collective-permute-start(bf16[6,10,24,384]{3,2,1,0:T(8,128)(2,1)} %get-tuple-element.10), channel_id=1, source_target_pairs={{1,0},{0,1},{3,2},{2,3},{5,4},{4,5},{7,6},{6,7},{9,8},{8,9},{11,10... | collective-permute-start | bytes 3317768 | tf_op jit(solution)/shard_map/ppermute | solution.py:39
  125.6 0.1 slice.36
  125.7 2.4 %collective-permute-start.21 = (bf16[2,21,16,384]{3,2,1,0:T(8,128)(2,1)S(1)}, bf16[2,21,16,384]{3,2,1,0:T(8,128)(2,1)S(1)}, u32[]{:S(2)}, u32[]{:S(2)}) collective-permute-start(bf16[2,21,16,384]{3,2,1,0:T(8,128)(2,1)S(1)} %slice.36), channel_id=1, source_target_pairs={{16,0},{65,1},{18,2},{67,3},{20,4},{69,5},{22,6},{71,7},{24,8},{73... | collective-permute-start | bytes 1548296 | tf_op jit(solution)/shard_map/ppermute | solution.py:39
  128.1 1.1 slice.37
  129.2 0.1 collective-permute-start.23
  129.3 0.6 reshape.11.bias_ref
  129.8 0.6 reshape.12.gain_ref
  130.4 1.0 copy-done.4
  131.4 7.8 %second_layout.1.laid_ref = bf16[6,6,10,32,256]{4,3,2,1,0:T(8,128)(2,1)} custom-call(s32[4]{0:T(128)} %pad_add_fusion.place_ref, f32[6,10,24,384]{3,2,1,0:T(8,128)} %get-tuple-element.9.mine_ref, bf16[6,10,24,384]{3,2,1,0:T(8,128)(2,1)} %copy-done.4, f32[1,384]{1,0:T(1,128)} %reshape.11.bias_ref, f32[1,384]{1,0:T(1,128)} %reshape.12.gain_ref), custom_call_target="tpu_custom_call" | custom-call | tf_op jit(solution)/shard_map/second_layout/pallas_call | solution.py:142
  139.2 0.8 copy-done.7
  140.0 0.8 copy-done.8
  140.8 10.8 %second_conv.1 = (f32[4,8,10,384]{3,2,1,0:T(8,128)}, f32[4,8,10,384]{3,2,1,0:T(8,128)}) custom-call(s32[4]{0:T(128)} %pad_add_fusion.place_ref, bf16[6,6,10,32,256]{4,3,2,1,0:T(8,128)(2,1)} %second_layout.1.laid_ref, bf16[4,21,16,384]{3,2,1,0:T(8,128)(2,1)} %copy-done.1, bf16[4,21,16,384]{3,2,1,0:T(8,128)(2,1)} %copy-done.2, ...), custom_call_target="tpu_custom_call" | custom-call | tf_op jit(solution)/shard_map/second_conv/pallas_call | solution.py:210
  151.5 1.4 copy.21
  152.9 1.0 collective-permute-start.24
  153.9 1.5 collective-permute-done.24
  155.4 0.2 fusion.2
  155.6 0.7 copy.24
  (48 shorter events, 0.2 us)
Async XLA Ops:
  0.0 30.6 %copy-start.3 = (bf16[4,8,10,384]{3,1,2,0:T(8,128)(2,1)S(1)}, bf16[4,8,10,384]{3,1,2,0:T(8,128)(2,1)}, u32[]{:S(2)}) copy-start(bf16[4,8,10,384]{3,1,2,0:T(8,128)(2,1)} %param.7) | copy-start | bytes 737284
  3.3 14.0 %collective-permute-start.5 = (bf16[21,8,384]{2,1,0:T(8,128)(2,1)}, bf16[21,8,384]{2,1,0:T(8,128)(2,1)S(1)}, u32[]{:S(2)}, u32[]{:S(2)}) collective-permute-start(bf16[21,8,384]{2,1,0:T(8,128)(2,1)} %fold.2), channel_id=1, source_target_pairs={{0,0},{1,1},{2,2},{3,3},{4,4},{5,5},{6,6},{7,7},{8,8},{9,9},{10,10... | collective-permute-start | bytes 387080 | tf_op jit(solution)/shard_map/ppermute | solution.py:39
  5.8 24.7 %collective-permute-start = (bf16[4,8,10,384]{3,2,1,0:T(8,128)(2,1)S(1)}, bf16[4,8,10,384]{3,2,1,0:T(8,128)(2,1)S(1)}, u32[]{:S(2)}, u32[]{:S(2)}) collective-permute-start(bf16[4,8,10,384]{3,2,1,0:T(8,128)(2,1)S(1)} %copy.14), channel_id=1, source_target_pairs={{0,64},{1,65},{2,66},{3,67},{4,68},{5,69},{6,70},{7,71},{8,72},{9,... | collective-permute-start | bytes 737288 | tf_op jit(solution)/shard_map/ppermute | solution.py:39
  15.8 11.0 %collective-permute-start.6 = (bf16[21,8,384]{2,1,0:T(8,128)(2,1)}, bf16[21,8,384]{2,1,0:T(8,128)(2,1)S(1)}, u32[]{:S(2)}, u32[]{:S(2)}) collective-permute-start(bf16[21,8,384]{2,1,0:T(8,128)(2,1)} %fold.2), channel_id=1, source_target_pairs={{8,0},{9,1},{10,2},{11,3},{12,4},{13,5},{14,6},{15,7},{0,8},{1,9},... | collective-permute-start | bytes 387080 | tf_op jit(solution)/shard_map/ppermute | solution.py:39
  26.8 8.6 %collective-permute-start.7 = (bf16[21,16,384]{2,1,0:T(8,128)(2,1)S(1)}, bf16[21,16,384]{2,1,0:T(8,128)(2,1)S(1)}, u32[]{:S(2)}, u32[]{:S(2)}) collective-permute-start(bf16[21,16,384]{2,1,0:T(8,128)(2,1)S(1)} %constant_dynamic-update-slice_fusion.1), channel_id=1, source_target_pairs={{64,0},{17,1},{66,2},{19,3},{68,4},{21,5},{70,6},{23,7},{72,8},{25... | collective-permute-start | bytes 774152 | tf_op jit(solution)/shard_map/ppermute | solution.py:39
  29.4 6.8 %collective-permute-start.8 = (bf16[21,16,384]{2,1,0:T(8,128)(2,1)S(1)}, bf16[21,16,384]{2,1,0:T(8,128)(2,1)S(1)}, u32[]{:S(2)}, u32[]{:S(2)}) collective-permute-start(bf16[21,16,384]{2,1,0:T(8,128)(2,1)S(1)} %constant_dynamic-update-slice_fusion.1), channel_id=1, source_target_pairs={{128,0},{33,1},{130,2},{35,3},{132,4},{37,5},{134,6},{39,7},{136,8... | collective-permute-start | bytes 774152 | tf_op jit(solution)/shard_map/ppermute | solution.py:39
  29.9 8.9 %collective-permute-start.9 = (bf16[21,16,384]{2,1,0:T(8,128)(2,1)S(1)}, bf16[21,16,384]{2,1,0:T(8,128)(2,1)S(1)}, u32[]{:S(2)}, u32[]{:S(2)}) collective-permute-start(bf16[21,16,384]{2,1,0:T(8,128)(2,1)S(1)} %constant_dynamic-update-slice_fusion.1), channel_id=1, source_target_pairs={{192,0},{49,1},{194,2},{51,3},{196,4},{53,5},{198,6},{55,7},{200,8... | collective-permute-start | bytes 774152 | tf_op jit(solution)/shard_map/ppermute | solution.py:39
  38.8 22.1 %copy-start.9 = (bf16[27,6,384]{2,0,1:T(8,128)(2,1)S(1)}, bf16[27,6,384]{2,0,1:T(8,128)(2,1)}, u32[]{:S(2)}) copy-start(bf16[27,6,384]{2,0,1:T(8,128)(2,1)} %param.12) | copy-start | bytes 373252
  39.0 30.3 %copy-start = (bf16[4,21,16,384]{3,2,1,0:T(8,128)(2,1)}, bf16[4,21,16,384]{3,2,1,0:T(8,128)(2,1)S(1)}, u32[]{:S(2)}) copy-start(bf16[4,21,16,384]{3,2,1,0:T(8,128)(2,1)S(1)} %pad_maximum_fusion.b0) | copy-start | bytes 3096580
  39.0 38.8 %collective-permute-start.10 = (bf16[4,21,16,384]{3,2,1,0:T(8,128)(2,1)S(1)}, bf16[4,21,16,384]{3,2,1,0:T(8,128)(2,1)}, u32[]{:S(2)}, u32[]{:S(2)}) collective-permute-start(bf16[4,21,16,384]{3,2,1,0:T(8,128)(2,1)S(1)} %pad_maximum_fusion.b0), channel_id=1, source_target_pairs={{16,0},{65,1},{18,2},{67,3},{20,4},{69,5},{22,6},{71,7},{24,8},{73... | collective-permute-start | bytes 3096584 | tf_op jit(solution)/shard_map/ppermute | solution.py:39
  39.1 4.1 %collective-permute-start.1 = (bf16[8,2,10,384]{3,2,1,0:T(8,128)(2,1)S(1)}, bf16[8,2,10,384]{3,2,1,0:T(8,128)(2,1)S(1)}, u32[]{:S(2)}, u32[]{:S(2)}) collective-permute-start(bf16[8,2,10,384]{3,2,1,0:T(8,128)(2,1)S(1)} %get-tuple-element.13), channel_id=1, source_target_pairs={{0,16},{1,17},{2,18},{3,19},{4,20},{5,21},{6,22},{7,23},{8,24},{9,... | collective-permute-start | bytes 368648 | tf_op jit(solution)/shard_map/ppermute | solution.py:39
  40.5 9.0 %collective-permute-start.2 = (bf16[8,2,10,384]{3,2,1,0:T(8,128)(2,1)S(1)}, bf16[8,2,10,384]{3,2,1,0:T(8,128)(2,1)S(1)}, u32[]{:S(2)}, u32[]{:S(2)}) collective-permute-start(bf16[8,2,10,384]{3,2,1,0:T(8,128)(2,1)S(1)} %get-tuple-element.14), channel_id=1, source_target_pairs={{16,0},{17,1},{18,2},{19,3},{20,4},{21,5},{22,6},{23,7},{24,8},{25... | collective-permute-start | bytes 368648 | tf_op jit(solution)/shard_map/ppermute | solution.py:39
  41.8 40.6 %collective-permute-start.12 = (bf16[4,21,16,384]{3,2,1,0:T(8,128)(2,1)S(1)}, bf16[4,21,16,384]{3,2,1,0:T(8,128)(2,1)}, u32[]{:S(2)}, u32[]{:S(2)}) collective-permute-start(bf16[4,21,16,384]{3,2,1,0:T(8,128)(2,1)S(1)} %pad_maximum_fusion.b0), channel_id=1, source_target_pairs={{48,0},{193,1},{50,2},{195,3},{52,4},{197,5},{54,6},{199,7},{56,8}... | collective-permute-start | bytes 3096584 | tf_op jit(solution)/shard_map/ppermute | solution.py:39
  49.4 17.7 %copy-start.6 = (bf16[8,2,10,384]{3,2,1,0:T(8,128)(2,1)}, bf16[8,2,10,384]{3,2,1,0:T(8,128)(2,1)S(1)}, u32[]{:S(2)}) copy-start(bf16[8,2,10,384]{3,2,1,0:T(8,128)(2,1)S(1)} %collective-permute-done.2) | copy-start | bytes 368644
  49.6 17.6 %collective-permute-start.3 = (bf16[8,12,2,384]{3,2,1,0:T(2,128)(2,1)S(1)}, bf16[8,12,2,384]{3,2,1,0:T(2,128)(2,1)}, u32[]{:S(2)}, u32[]{:S(2)}) collective-permute-start(bf16[8,12,2,384]{3,2,1,0:T(2,128)(2,1)S(1)} %broadcast_select_fusion), channel_id=1, source_target_pairs={{2,1},{1,2},{4,3},{3,4},{6,5},{5,6},{8,7},{7,8},{10,9},{9,10},{12,... | collective-permute-start | bytes 442376 | tf_op jit(solution)/shard_map/ppermute | solution.py:39
  63.2 9.6 %collective-permute-start.15 = (bf16[21,8,384]{2,1,0:T(8,128)(2,1)}, bf16[21,8,384]{2,1,0:T(8,128)(2,1)S(1)}, u32[]{:S(2)}, u32[]{:S(2)}) collective-permute-start(bf16[21,8,384]{2,1,0:T(8,128)(2,1)} %fold.3), channel_id=1, source_target_pairs={{0,0},{1,1},{2,2},{3,3},{4,4},{5,5},{6,6},{7,7},{8,8},{9,9},{10,10... | collective-permute-start | bytes 387080 | tf_op jit(solution)/shard_map/ppermute | solution.py:39
  64.8 10.0 %collective-permute-start.16 = (bf16[21,8,384]{2,1,0:T(8,128)(2,1)}, bf16[21,8,384]{2,1,0:T(8,128)(2,1)S(1)}, u32[]{:S(2)}, u32[]{:S(2)}) collective-permute-start(bf16[21,8,384]{2,1,0:T(8,128)(2,1)} %fold.3), channel_id=1, source_target_pairs={{8,0},{9,1},{10,2},{11,3},{12,4},{13,5},{14,6},{15,7},{0,8},{1,9},... | collective-permute-start | bytes 387080 | tf_op jit(solution)/shard_map/ppermute | solution.py:39
  70.7 21.2 %collective-permute-start.4 = (bf16[8,12,12,384]{3,0,2,1:T(8,128)(2,1)}, bf16[8,12,12,384]{3,0,2,1:T(8,128)(2,1)}, u32[]{:S(2)}, u32[]{:S(2)}) collective-permute-start(bf16[8,12,12,384]{3,0,2,1:T(8,128)(2,1)} %copy.16), channel_id=1, source_target_pairs={{1,0},{0,1},{3,2},{2,3},{5,4},{4,5},{7,6},{6,7},{9,8},{8,9},{11,10... | collective-permute-start | bytes 2654216 | tf_op jit(solution)/shard_map/ppermute | solution.py:39
  74.8 13.0 %collective-permute-start.18 = (bf16[21,16,384]{2,1,0:T(8,128)(2,1)S(1)}, bf16[21,16,384]{2,1,0:T(8,128)(2,1)S(1)}, u32[]{:S(2)}, u32[]{:S(2)}) collective-permute-start(bf16[21,16,384]{2,1,0:T(8,128)(2,1)S(1)} %constant_dynamic-update-slice_fusion.3), channel_id=1, source_target_pairs={{128,0},{33,1},{130,2},{35,3},{132,4},{37,5},{134,6},{39,7},{136,8... | collective-permute-start | bytes 774152 | tf_op jit(solution)/shard_map/ppermute | solution.py:39
  77.8 10.0 %collective-permute-start.19 = (bf16[21,16,384]{2,1,0:T(8,128)(2,1)S(1)}, bf16[21,16,384]{2,1,0:T(8,128)(2,1)S(1)}, u32[]{:S(2)}, u32[]{:S(2)}) collective-permute-start(bf16[21,16,384]{2,1,0:T(8,128)(2,1)S(1)} %constant_dynamic-update-slice_fusion.3), channel_id=1, source_target_pairs={{192,0},{49,1},{194,2},{51,3},{196,4},{53,5},{198,6},{55,7},{200,8... | collective-permute-start | bytes 774152 | tf_op jit(solution)/shard_map/ppermute | solution.py:39
  77.8 10.0 %collective-permute-start.17 = (bf16[21,16,384]{2,1,0:T(8,128)(2,1)S(1)}, bf16[21,16,384]{2,1,0:T(8,128)(2,1)S(1)}, u32[]{:S(2)}, u32[]{:S(2)}) collective-permute-start(bf16[21,16,384]{2,1,0:T(8,128)(2,1)S(1)} %constant_dynamic-update-slice_fusion.3), channel_id=1, source_target_pairs={{64,0},{17,1},{66,2},{19,3},{68,4},{21,5},{70,6},{23,7},{72,8},{25... | collective-permute-start | bytes 774152 | tf_op jit(solution)/shard_map/ppermute | solution.py:39
  82.4 8.4 %copy-start.11 = (f32[384]{0:T(512)S(1)}, f32[384]{0:T(512)}, u32[]{:S(2)}) copy-start(f32[384]{0:T(512)} %param.8) | copy-start | bytes 4612
  82.4 23.1 %collective-permute-start.11 = (bf16[2,21,16,384]{3,2,1,0:T(8,128)(2,1)}, bf16[2,21,16,384]{3,2,1,0:T(8,128)(2,1)}, u32[]{:S(2)}, u32[]{:S(2)}) collective-permute-start(bf16[2,21,16,384]{3,2,1,0:T(8,128)(2,1)} %slice.34), channel_id=1, source_target_pairs={{16,0},{65,1},{18,2},{67,3},{20,4},{69,5},{22,6},{71,7},{24,8},{73... | collective-permute-start | bytes 1548296 | tf_op jit(solution)/shard_map/ppermute | solution.py:39
  87.8 17.7 %collective-permute-start.13 = (bf16[2,21,16,384]{3,2,1,0:T(8,128)(2,1)}, bf16[2,21,16,384]{3,2,1,0:T(8,128)(2,1)}, u32[]{:S(2)}, u32[]{:S(2)}) collective-permute-start(bf16[2,21,16,384]{3,2,1,0:T(8,128)(2,1)} %slice.35), channel_id=1, source_target_pairs={{48,0},{193,1},{50,2},{195,3},{52,4},{197,5},{54,6},{199,7},{56,8}... | collective-permute-start | bytes 1548296 | tf_op jit(solution)/shard_map/ppermute | solution.py:39
  88.0 7.9 %copy-start.1 = (bf16[4,21,16,384]{3,2,1,0:T(8,128)(2,1)}, bf16[4,21,16,384]{3,2,1,0:T(8,128)(2,1)S(1)}, u32[]{:S(2)}) copy-start(bf16[4,21,16,384]{3,2,1,0:T(8,128)(2,1)S(1)} %pad_maximum_fusion.1.b0) | copy-start | bytes 3096580
  88.0 37.6 %collective-permute-start.20 = (bf16[4,21,16,384]{3,2,1,0:T(8,128)(2,1)S(1)}, bf16[4,21,16,384]{3,2,1,0:T(8,128)(2,1)S(1)}, u32[]{:S(2)}, u32[]{:S(2)}) collective-permute-start(bf16[4,21,16,384]{3,2,1,0:T(8,128)(2,1)S(1)} %pad_maximum_fusion.1.b0), channel_id=1, source_target_pairs={{16,0},{65,1},{18,2},{67,3},{20,4},{69,5},{22,6},{71,7},{24,8},{73... | collective-permute-start | bytes 3096584 | tf_op jit(solution)/shard_map/ppermute | solution.py:39
  90.7 37.3 %collective-permute-start.22 = (bf16[4,21,16,384]{3,2,1,0:T(8,128)(2,1)S(1)}, bf16[4,21,16,384]{3,2,1,0:T(8,128)(2,1)}, u32[]{:S(2)}, u32[]{:S(2)}) collective-permute-start(bf16[4,21,16,384]{3,2,1,0:T(8,128)(2,1)S(1)} %pad_maximum_fusion.1.b0), channel_id=1, source_target_pairs={{48,0},{193,1},{50,2},{195,3},{52,4},{197,5},{54,6},{199,7},{56,8}... | collective-permute-start | bytes 3096584 | tf_op jit(solution)/shard_map/ppermute | solution.py:39
  122.6 6.7 %copy-start.12 = (f32[384]{0:T(512)S(1)}, f32[384]{0:T(512)}, u32[]{:S(2)}) copy-start(f32[384]{0:T(512)} %param.10) | copy-start | bytes 4612
  122.6 7.2 %copy-start.13 = (f32[384]{0:T(512)S(1)}, f32[384]{0:T(512)}, u32[]{:S(2)}) copy-start(f32[384]{0:T(512)} %param.11) | copy-start | bytes 4612
  122.6 7.8 %collective-permute-start.14 = (bf16[6,10,24,384]{3,2,1,0:T(8,128)(2,1)}, bf16[6,10,24,384]{3,2,1,0:T(8,128)(2,1)S(1)}, u32[]{:S(2)}, u32[]{:S(2)}) collective-permute-start(bf16[6,10,24,384]{3,2,1,0:T(8,128)(2,1)} %get-tuple-element.10), channel_id=1, source_target_pairs={{1,0},{0,1},{3,2},{2,3},{5,4},{4,5},{7,6},{6,7},{9,8},{8,9},{11,10... | collective-permute-start | bytes 3317768 | tf_op jit(solution)/shard_map/ppermute | solution.py:39
  125.6 13.6 %copy-start.2 = (bf16[4,21,16,384]{3,2,1,0:T(8,128)(2,1)}, bf16[4,21,16,384]{3,2,1,0:T(8,128)(2,1)S(1)}, u32[]{:S(2)}) copy-start(bf16[4,21,16,384]{3,2,1,0:T(8,128)(2,1)S(1)} %collective-permute-done.20.b1) | copy-start | bytes 3096580
  125.7 13.5 %collective-permute-start.21 = (bf16[2,21,16,384]{3,2,1,0:T(8,128)(2,1)S(1)}, bf16[2,21,16,384]{3,2,1,0:T(8,128)(2,1)S(1)}, u32[]{:S(2)}, u32[]{:S(2)}) collective-permute-start(bf16[2,21,16,384]{3,2,1,0:T(8,128)(2,1)S(1)} %slice.36), channel_id=1, source_target_pairs={{16,0},{65,1},{18,2},{67,3},{20,4},{69,5},{22,6},{71,7},{24,8},{73... | collective-permute-start | bytes 1548296 | tf_op jit(solution)/shard_map/ppermute | solution.py:39
  129.2 10.1 %collective-permute-start.23 = (bf16[2,21,16,384]{3,2,1,0:T(8,128)(2,1)S(1)}, bf16[2,21,16,384]{3,2,1,0:T(8,128)(2,1)S(1)}, u32[]{:S(2)}, u32[]{:S(2)}) collective-permute-start(bf16[2,21,16,384]{3,2,1,0:T(8,128)(2,1)S(1)} %slice.37), channel_id=1, source_target_pairs={{48,0},{193,1},{50,2},{195,3},{52,4},{197,5},{54,6},{199,7},{56,8}... | collective-permute-start | bytes 1548296 | tf_op jit(solution)/shard_map/ppermute | solution.py:39
  130.4 1.0 copy-start.4
  139.2 16.2 %copy-start.10 = (f32[384]{0:T(512)S(1)}, f32[384]{0:T(512)}, u32[]{:S(2)}) copy-start(f32[384]{0:T(512)} %param.13) | copy-start | bytes 4612
  139.2 0.8 copy-start.7
  140.0 0.8 copy-start.8
  151.5 3.8 %copy-start.5 = (f32[4,8,10,384]{3,2,1,0:T(8,128)S(1)}, f32[4,8,10,384]{3,2,1,0:T(8,128)}, u32[]{:S(2)}) copy-start(f32[4,8,10,384]{3,2,1,0:T(8,128)} %get-tuple-element.11) | copy-start | bytes 1474564
  152.9 2.5 %collective-permute-start.24 = (f32[4,8,10,384]{3,1,2,0:T(8,128)S(1)}, f32[4,8,10,384]{3,1,2,0:T(8,128)S(1)}, u32[]{:S(2)}, u32[]{:S(2)}) collective-permute-start(f32[4,8,10,384]{3,1,2,0:T(8,128)S(1)} %copy.21), channel_id=1, source_target_pairs={{1,0},{0,1},{3,2},{2,3},{5,4},{4,5},{7,6},{6,7},{9,8},{8,9},{11,10... | collective-permute-start | bytes 1474568 | tf_op jit(solution)/shard_map/ppermute | solution.py:39

commit v2 on v1

v2 whole, which is shorter than its diff:
```python
import jax
import jax.numpy as jnp
from jax import lax
from jax.experimental import pallas as pl
from jax.experimental.pallas import tpu as pltpu
from jax.sharding import Mesh, PartitionSpec as P

AXES = ("t", "h", "z", "c")
SHIFT = ((0, 1, -1, 2), (0, -1, 1, 2))
MAIN = tuple(t for t in range(27) if t % 3 != 1)
PAIRED = (1, 4, 7, 10, 13, 16)
ALONE = (19, 22, 25)
GROUPS = len(MAIN) + len(ALONE)
CHANS = 384
LANES = 256
BF = jnp.bfloat16
F32 = jnp.float32
VMEM = pltpu.CompilerParams(vmem_limit_bytes=32 * 2**20)
whole = pl.BlockSpec(memory_space=pltpu.VMEM)


def move(x, sizes, source):
    def place(at):
        index = 0
        for coordinate, size in zip(at, sizes):
            index = index * size + coordinate % size
        return index

    pairs = []
    for index in range(sizes[0] * sizes[1] * sizes[2] * sizes[3]):
        rest, c = divmod(index, sizes[3])
        rest, z = divmod(rest, sizes[2])
        t, h = divmod(rest, sizes[1])
        at = source(t, h, z, c)
        if at is not None:
            pairs.append((place(at), index))
    return lax.ppermute(x, AXES, pairs)


def take(rows_ref, start, count, stride):
    return jnp.concatenate(
        [rows_ref[part, pl.ds(start, count, stride=stride)] for part in range(3)], axis=1
    )


def fold_kernel(k1_ref, k2_ref, out_ref, rows_ref):
    for which, k_ref in enumerate((k1_ref, k2_ref)):
        for r in range(6):
            for part in range(3):
                values = k_ref[r, :, 128 * part : 128 * part + 128]
                rows_ref[part, 32 * r : 32 * r + 27] = values.astype(F32)
        for g in range(GROUPS):
            if g < len(MAIN):
                low = take(rows_ref, MAIN[g], 6, 32)
                high = take(rows_ref, 64 * (g % 3) + PAIRED[g // 3], 2, 32)
            else:
                low = take(rows_ref, ALONE[g - len(MAIN)], 6, 32)
                high = jnp.zeros((2, CHANS), F32)
            out_ref[which, g] = jnp.concatenate([low, high], axis=0).astype(BF)


def fold(kernel_1, kernel_2):
    return pl.pallas_call(
        fold_kernel,
        out_shape=jax.ShapeDtypeStruct((2, GROUPS, 8, CHANS), BF),
        in_specs=[whole] * 2,
        out_specs=whole,
        scratch_shapes=[pltpu.VMEM((3, 192, 128), F32)],
        compiler_params=VMEM,
        name="fold",
    )(jnp.transpose(kernel_1, (1, 0, 2)), jnp.transpose(kernel_2, (1, 0, 2)))


def spread(spread_ref):
    t, h, z, c = (lax.axis_index(a) for a in AXES)
    lane = lax.broadcasted_iota(jnp.int32, (1, LANES), 1)
    j = lane & 7
    p = lane >> 3
    outer, inner, far = p >> 3, (p >> 1) & 3, p & 1
    t_of = (t + jnp.where(c == 0, inner, outer)) & 3
    h_of = (h + jnp.where(c == 0, outer, inner)) & 3
    sides = jnp.where((t_of == 1) == (c == 0), 1, 7)
    shift = jnp.where(t_of == 0, 0, jnp.where(t_of == 3, 2, sides))
    z_of = (z + shift + 4 * far) & 7
    base = 96 * h_of + 12 * z_of + 6 * c
    chan = lax.broadcasted_iota(jnp.int32, (CHANS, LANES), 0)
    spread_ref[0] = jnp.where(chan == jnp.where(j < 6, base + j, -1), 1.0, 0.0).astype(BF)
    for k in range(3):
        wanted = jnp.where(j >= 6, base + 2 * k + j - 6, -1)
        spread_ref[k + 1] = jnp.where(chan == wanted, 1.0, 0.0).astype(BF)


def activated(values, gain):
    square_mean = jnp.mean(values * values, axis=-1, keepdims=True)
    normed = values * lax.rsqrt(square_mean + 1e-06) * gain
    return normed * jax.nn.sigmoid(normed)


def lay_out(active, spread_ref, out_ref):
    count = active.shape[0]

    def put(slot, value, matrix):
        laid = jnp.dot(value, spread_ref[matrix], preferred_element_type=F32)
        out_ref[slot, 0] = laid.astype(BF)

    put(0, active.astype(BF), 0)
    one = pltpu.roll(active, count - 1, 0).astype(BF)
    put(1, one, 0)
    for k in range(3):
        put(3 + k, one, 1 + k)
    put(2, pltpu.roll(active, count - 2, 0).astype(BF), 0)


def first_layout_kernel(x_ref, gain_ref, out_ref, spread_ref):
    @pl.when(pl.program_id(0) == 0)
    def _():
        spread(spread_ref)

    values = x_ref[0].astype(F32).reshape(12 * 24, CHANS)
    lay_out(activated(values, gain_ref[...]), spread_ref, out_ref)


def first_layout(features, gain):
    return pl.pallas_call(
        first_layout_kernel,
        grid=(8,),
        out_shape=jax.ShapeDtypeStruct((6, 8, 12 * 24, LANES), BF),
        in_specs=[
            pl.BlockSpec((1, 12, 24, CHANS), lambda f: (f, 0, 0, 0)),
            pl.BlockSpec((1, CHANS), lambda f: (0, 0)),
        ],
        out_specs=pl.BlockSpec((6, 1, 12 * 24, LANES), lambda f: (0, f, 0, 0)),
        scratch_shapes=[pltpu.VMEM((4, CHANS, LANES), BF)],
        compiler_params=VMEM,
        name="first_layout",
    )(features, gain)


def second_layout_kernel(mine_ref, other_ref, bias_ref, gain_ref, out_ref, spread_ref):
    @pl.when(pl.program_id(0) == 0)
    def _():
        spread(spread_ref)

    t, h, z = (lax.axis_index(a) for a in AXES[:3])
    frame = pl.program_id(0) - 2 + 4 * t
    total = mine_ref[0] + other_ref[0].astype(F32) + bias_ref[...]
    active = activated(total.astype(BF).astype(F32), gain_ref[...])
    row = lax.broadcasted_iota(jnp.int32, (10, 24, 1), 0) + 8 * h - 1
    col = lax.broadcasted_iota(jnp.int32, (10, 24, 1), 1) + 20 * z - 1
    inside = (row >= 0) & (row < 32) & (col >= 0) & (col < 160) & (frame >= 0)
    active = active.reshape(10, 24, CHANS) * jnp.where(inside, 1.0, 0.0)
    lay_out(active.reshape(10 * 24, CHANS), spread_ref, out_ref)


def second_layout(mine, other, bias, gain):
    return pl.pallas_call(
        second_layout_kernel,
        grid=(6,),
        out_shape=jax.ShapeDtypeStruct((6, 6, 10 * 24, LANES), BF),
        in_specs=[
            pl.BlockSpec((1, 10 * 24, CHANS), lambda f: (f, 0, 0)),
            pl.BlockSpec((1, 10 * 24, CHANS), lambda f: (f, 0, 0)),
            pl.BlockSpec((1, CHANS), lambda f: (0, 0)),
            pl.BlockSpec((1, CHANS), lambda f: (0, 0)),
        ],
        out_specs=pl.BlockSpec((6, 1, 10 * 24, LANES), lambda f: (0, f, 0, 0)),
        scratch_shapes=[pltpu.VMEM((4, CHANS, LANES), BF)],
        compiler_params=VMEM,
        name="second_layout",
    )(mine, other, bias, gain)


def tap_sum(laid_ref, blocks, first, frames, count):
    def window(slot, tap):
        dt, start = tap // 9, 24 * (tap % 9 // 3)
        return jnp.concatenate(
            [laid_ref[slot, first + dt + i, start : start + count] for i in range(frames)], axis=0
        )

    total = None
    for g in range(GROUPS):
        if g < len(MAIN):
            left = window(MAIN[g] % 3, MAIN[g]) + window(3 + g % 3, PAIRED[g // 3])
        else:
            left = window(1, ALONE[g - len(MAIN)])
        right = jnp.concatenate([b[i, g] for b in blocks for i in range(b.shape[0])], axis=0)
        term = jnp.dot(left, right, preferred_element_type=F32)
        total = term if total is None else total + term
    return total


def first_conv_kernel(laid_ref, *refs):
    *blocks, mine_ref, sent_ref = refs
    total = tap_sum(laid_ref, blocks, 2 * pl.program_id(0), 2, 10 * 24)
    total = total.reshape(2, 10 * 24, CHANS)
    mine_ref[...] = total
    sent_ref[...] = total.astype(BF)


def first_conv(laid, blocks):
    out = pl.BlockSpec((2, 10 * 24, CHANS), lambda f: (f, 0, 0))
    return pl.pallas_call(
        first_conv_kernel,
        grid=(3,),
        out_shape=(
            jax.ShapeDtypeStruct((6, 10 * 24, CHANS), F32),
            jax.ShapeDtypeStruct((6, 10 * 24, CHANS), BF),
        ),
        in_specs=[whole] * (1 + len(blocks)),
        out_specs=(out, out),
        compiler_params=VMEM,
        name="first_conv",
    )(laid, *blocks)


def second_conv_kernel(laid_ref, *refs):
    *blocks, mine_ref, sent_ref, total_ref = refs
    total = tap_sum(laid_ref, blocks, 2 * pl.program_id(0), 2, 8 * 24)
    for part in range(3):
        total_ref[part] = total[:, 128 * part : 128 * part + 128]
    own = 10 * lax.axis_index("c")
    for f in range(2):
        for w in range(10):
            at = 192 * f + w
            mine_ref[f, w] = take(total_ref, at + own, 8, 24)
            sent_ref[f, w] = take(total_ref, at + 10 - own, 8, 24)


def second_conv(laid, blocks):
    out = pl.BlockSpec((2, 10, 8, CHANS), lambda f: (f, 0, 0, 0))
    return pl.pallas_call(
        second_conv_kernel,
        grid=(2,),
        out_shape=(
            jax.ShapeDtypeStruct((4, 10, 8, CHANS), F32),
            jax.ShapeDtypeStruct((4, 10, 8, CHANS), F32),
        ),
        in_specs=[whole] * (1 + len(blocks)),
        out_specs=(out, out),
        scratch_shapes=[pltpu.VMEM((3, 2 * 192, 128), F32)],
        compiler_params=VMEM,
        name="second_conv",
    )(laid, *blocks)


def solution(mesh):
    sizes = (mesh.shape["tm"], mesh.shape["height"], mesh.shape["width"] // 2, 2)
    split = Mesh(mesh.devices.reshape(sizes), AXES)

    def sent(x, source):
        return move(x, sizes, source)

    def along(first, step):
        def source(t, h, z, c):
            return (t + step, h, z, c) if (c == 0) == first else (t, h + step, z, c)

        return source

    def z_near(x):
        return sent(x, lambda t, h, z, c: (t, h, z + SHIFT[c][t], c))

    def z_far(x):
        return sent(x, lambda t, h, z, c: (t, h, z + SHIFT[c][t] + 4, c))

    def first_ring(x):
        up, down = sent(x, along(True, 1)), sent(x, along(True, -1))
        far = sent(x, along(True, 2))
        return [jnp.stack([x[i], up[i], far[i], down[i]]) for i in range(2)]

    def second_ring(x):
        return sent(x, along(False, 1)), sent(x, along(False, -1))

    def passed_on(up, down):
        return sent(up[:2], along(False, 1)), sent(down[2:], along(False, -1))

    def swapped(x):
        return sent(x, lambda t, h, z, c: (t, h, z, 1 - c))

    def inner(at, d):
        return at if all(0 <= a < s for a, s in zip(at, sizes)) else None

    def taller(x):
        earlier = sent(x, lambda t, h, z, c: inner((t - 1, h, z, c), 0))
        return jnp.concatenate([earlier, x], axis=0)

    def higher(x):
        above = sent(x[:, -2:], lambda t, h, z, c: inner((t, h - 1, z, c), 0))
        below = sent(x[:, :2], lambda t, h, z, c: inner((t, h + 1, z, c), 0))
        return jnp.concatenate([above, x, below], axis=1)

    def wider(x, core):
        edge = jnp.where(core == 0, x[:, :, :2], x[:, :, -2:])
        beside = sent(edge, lambda t, h, z, c: inner((t, h, z + 2 * c - 1, 1 - c), 0))
        return jnp.where(
            core == 0,
            jnp.concatenate([beside, x], axis=2),
            jnp.concatenate([x, beside], axis=2),
        )

    def joined(mine, core):
        other = swapped(mine)
        return jnp.where(
            core == 0,
            jnp.concatenate([mine, other], axis=2),
            jnp.concatenate([other, mine], axis=2),
        )

    def at_once(*values):
        return lax.optimization_barrier(values)

    def on_device(features, gain_1, kernel_1, bias_1, gain_2, kernel_2, bias_2):
        core = lax.axis_index("c")
        gains = [v.reshape(1, CHANS) for v in (gain_1, gain_2, bias_1)]
        both = fold(kernel_1, kernel_2)
        both = jnp.concatenate([z_near(both), z_far(both)], axis=2)
        both, wide = at_once(both, taller(features))
        one, two, wide = at_once(*first_ring(both), higher(wide))
        up, down = second_ring(one)
        up, down, wide, two = at_once(up, down, wider(wide, core), two)
        far = passed_on(up, down)
        next_up, next_down = second_ring(two)
        laid = first_layout(joined(wide, core), gains[0])
        mine, passed = first_conv(laid, (one, up, *far, down))
        next_up, next_down, passed = at_once(next_up, next_down, passed)
        far = passed_on(next_up, next_down)
        laid = second_layout(mine, swapped(passed), gains[2], gains[1])
        mine, passed = second_conv(laid, (two, next_up, *far, next_down))
        own = jnp.transpose(features, (0, 2, 1, 3)).astype(F32)
        total = mine + swapped(passed) + bias_2 + own
        return jnp.transpose(total.astype(BF), (0, 2, 1, 3))

    volume = P("t", "h", ("z", "c"), None)
    weights = P(None, ("h", "z", "c"), None)
    return jax.shard_map(
        on_device,
        mesh=split,
        in_specs=(volume, P(), weights, P(), P(), weights, P()),
        out_specs=volume,
        check_vma=False,
    )
```

time: 157 us -> 119 us (0.76)
  Pallas kernels: 48.4 us -> 25.5 us
  starting transfers between devices: 56.6 us -> 42.9 us
  local copies, waits for them, and re-layouts: 17.7 us -> 5.05 us
  waiting for transfers between devices: 27.3 us -> 37.1 us
  other arithmetic: 5.99 us -> 8.13 us
    ppermute x25 -> x20, starting transfers between devices: 56.6 us -> 42.9 us  [move(): return lax.ppermute(x, AXES, pairs)]
    ppermute x25 -> x20, waiting for transfers between devices: 27.3 us -> 37.1 us  [move(): return lax.ppermute(x, AXES, pairs)]
    pallas_call x1, Pallas kernels: 17.1 us -> 9.85 us  [first_conv(): pl.pallas_call(first_conv_kernel, grid=(3,), out_shape=(jax.ShapeDtypeStr...]
    pallas_call x1, Pallas kernels: 10.8 us -> 4.81 us  [second_conv(): pl.pallas_call(second_conv_kernel, grid=(2,), out_shape=(jax.ShapeDtypeSt...]
    slice x5 -> x9, local copies, waits for them, and re-layouts: 4.96 us -> 1.5 us  [the longest x4 1.25 us: passed_on(): return (sent(up[:2], along(False, 1)), sent(down[2:], along(False, -1)))]
    pallas_call x1, Pallas kernels: 9.61 us -> 6.16 us  [first_layout(): pl.pallas_call(first_layout_kernel, grid=(8,), out_shape=jax.ShapeDtypeSt...]
    pallas_call x1, Pallas kernels: 7.79 us -> 4.39 us  [second_layout(): pl.pallas_call(second_layout_kernel, grid=(6,), out_shape=jax.ShapeDtypeS...]
    unnamed x34 -> x15, local copies, waits for them, and re-layouts: 6.01 us -> 2.84 us
  transfers between devices with their start and end apart: 25 -> 20, of which waited for: 7 -> 11; matrix products, arithmetic and copies ran while one was open for 11% -> 7% of each run, Pallas kernels for 23% -> 17%
where the time goes in v2:
time: 119 us
  starting transfers between devices  42.9 us (36%)
  waiting for transfers between devices  37.1 us (31%)
  Pallas kernels  25.5 us (21%)
  other arithmetic  8.13 us (7%)
  local copies, waits for them, and re-layouts  5.05 us (4%)
    ppermute x20, starting transfers between devices, move(): return lax.ppermute(x, AXES, pairs)  42.9 us
    ppermute x20, waiting for transfers between devices, move(): return lax.ppermute(x, AXES, pairs)  37.1 us
    pallas_call x1, Pallas kernels, first_conv(): pl.pallas_call(first_conv_kernel, grid=(3,), out_shape=(jax.ShapeDtypeStr...  9.85 us
    pallas_call x1, Pallas kernels, first_layout(): pl.pallas_call(first_layout_kernel, grid=(8,), out_shape=jax.ShapeDtypeSt...  6.16 us
    pallas_call x1, Pallas kernels, second_conv(): pl.pallas_call(second_conv_kernel, grid=(2,), out_shape=(jax.ShapeDtypeSt...  4.81 us
    pallas_call x1, Pallas kernels, second_layout(): pl.pallas_call(second_layout_kernel, grid=(6,), out_shape=jax.ShapeDtypeS...  4.39 us
    unnamed x15, local copies, waits for them, and re-layouts  2.84 us
    select_n x1, other arithmetic, wider(): jnp.where(core == 0, jnp.concatenate([beside, x], axis=2), jnp.concatenat...  2.67 us
  transfers between devices with their start and end apart: 20, of which 11 were waited for; matrix products, arithmetic and copies ran while one was open for 7% of the time, Pallas kernels for 17%

profile of v2, /device:TPU:1, one launch (start us, length us, event | category | flops | bytes accessed | tf_op | source)
XLA Modules:
  0.0 119.0 jit_solution(15728596232638681640)
XLA Ops:
  0.0 1.0 copy.10
  1.0 4.1 %collective-permute-start.2 = (bf16[4,8,10,384]{3,2,1,0:T(8,128)(2,1)S(1)}, bf16[4,8,10,384]{3,2,1,0:T(8,128)(2,1)S(1)}, u32[]{:S(2)}, u32[]{:S(2)}) collective-permute-start(bf16[4,8,10,384]{3,2,1,0:T(8,128)(2,1)S(1)} %copy.10), channel_id=1, source_target_pairs={{0,64},{1,65},{2,66},{3,67},{4,68},{5,69},{6,70},{7,71},{8,72},{9,... | collective-permute-start | bytes 737288 | tf_op jit(solution)/shard_map/ppermute | solution.py:37
  5.1 0.0 copy-start
  5.1 0.9 copy-done
  6.0 0.9 copy-done.1
  6.9 0.3 fold.1
  7.2 0.7 collective-permute-start
  7.9 7.0 %collective-permute-start.1 = (bf16[2,21,8,384]{3,2,1,0:T(8,128)(2,1)S(1)}, bf16[2,21,8,384]{3,2,1,0:T(8,128)(2,1)S(1)}, u32[]{:S(2)}, u32[]{:S(2)}) collective-permute-start(bf16[2,21,8,384]{3,2,1,0:T(8,128)(2,1)S(1)} %fold.1), channel_id=1, source_target_pairs={{8,0},{9,1},{10,2},{11,3},{12,4},{13,5},{14,6},{15,7},{0,8},{1,9},... | collective-permute-start | bytes 774152 | tf_op jit(solution)/shard_map/ppermute | solution.py:37
  14.9 0.0 collective-permute-done.2
  14.9 0.1 pad_maximum_fusion.3
  15.1 6.5 %collective-permute-done.1 = bf16[2,21,8,384]{3,2,1,0:T(8,128)(2,1)S(1)} collective-permute-done((bf16[2,21,8,384]{3,2,1,0:T(8,128)(2,1)S(1)}, bf16[2,21,8,384]{3,2,1,0:T(8,128)(2,1)S(1)}, u32[]{:S(2)}, u32[]{:S(2)}) %collective-permute-start.1) | collective-permute-done | bytes 258080 | tf_op jit(solution)/shard_map/ppermute | solution.py:37
  21.5 0.1 pad_maximum_fusion.4
  21.6 2.6 %collective-permute-start.3 = (bf16[2,21,16,384]{3,2,1,0:T(8,128)(2,1)S(1)}, bf16[2,21,16,384]{3,2,1,0:T(8,128)(2,1)S(1)}, u32[]{:S(2)}, u32[]{:S(2)}) collective-permute-start(bf16[2,21,16,384]{3,2,1,0:T(8,128)(2,1)S(1)} %pad_maximum_fusion.4), channel_id=1, source_target_pairs={{64,0},{17,1},{66,2},{19,3},{68,4},{21,5},{70,6},{23,7},{72,8},{25... | collective-permute-start | bytes 1548296 | tf_op jit(solution)/shard_map/ppermute | solution.py:37
  24.1 0.5 collective-permute-start.4
  24.6 0.6 collective-permute-start.5
  25.3 3.4 %collective-permute-start.6 = (bf16[8,2,10,384]{3,2,1,0:T(8,128)(2,1)S(1)}, bf16[8,2,10,384]{3,2,1,0:T(8,128)(2,1)S(1)}, u32[]{:S(2)}, u32[]{:S(2)}) collective-permute-start(bf16[8,2,10,384]{3,2,1,0:T(8,128)(2,1)S(1)} %get-tuple-element.37), channel_id=1, source_target_pairs={{0,16},{1,17},{2,18},{3,19},{4,20},{5,21},{6,22},{7,23},{8,24},{9,... | collective-permute-start | bytes 368648 | tf_op jit(solution)/shard_map/ppermute | solution.py:37
  28.7 1.3 %collective-permute-start.7 = (bf16[8,2,10,384]{3,2,1,0:T(8,128)(2,1)S(1)}, bf16[8,2,10,384]{3,2,1,0:T(8,128)(2,1)S(1)}, u32[]{:S(2)}, u32[]{:S(2)}) collective-permute-start(bf16[8,2,10,384]{3,2,1,0:T(8,128)(2,1)S(1)} %get-tuple-element.38), channel_id=1, source_target_pairs={{16,0},{17,1},{18,2},{19,3},{20,4},{21,5},{22,6},{23,7},{24,8},{25... | collective-permute-start | bytes 368648 | tf_op jit(solution)/shard_map/ppermute | solution.py:37
  30.0 0.1 fusion.3
  30.1 9.2 %collective-permute-done.6 = bf16[8,2,10,384]{3,2,1,0:T(8,128)(2,1)S(1)} collective-permute-done((bf16[8,2,10,384]{3,2,1,0:T(8,128)(2,1)S(1)}, bf16[8,2,10,384]{3,2,1,0:T(8,128)(2,1)S(1)}, u32[]{:S(2)}, u32[]{:S(2)}) %collective-permute-start.6) | collective-permute-done | bytes 122912 | tf_op jit(solution)/shard_map/ppermute | solution.py:37
  39.3 1.3 %pad_maximum_fusion = bf16[8,12,10,384]{3,2,1,0:T(8,128)(2,1)} fusion(bf16[8,2,10,384]{3,2,1,0:T(8,128)(2,1)S(1)} %collective-permute-done.7, bf16[8,8,10,384]{3,2,1,0:T(8,128)(2,1)S(1)} %pad_maximum_fusion.3, bf16[8,2,10,384]{3,2,1,0:T(8,128)(2,1)S(1)} %collective-permute-done.6), kind=kLoop, calls=%fused_computation.1 | loop fusion | flops 737280 | bytes 1474560 | tf_op jit(solution)/shard_map/concatenate | solution.py:289
  40.6 0.1 fusion.4
  40.7 0.1 fusion.5
  40.7 0.1 fusion.6
  40.8 0.4 pad_maximum_fusion.1
  41.2 6.2 %collective-permute-start.8 = (bf16[4,21,16,384]{3,2,1,0:T(8,128)(2,1)S(1)}, bf16[4,21,16,384]{3,2,1,0:T(8,128)(2,1)S(1)}, u32[]{:S(2)}, u32[]{:S(2)}) collective-permute-start(bf16[4,21,16,384]{3,2,1,0:T(8,128)(2,1)S(1)} %get-tuple-element.23.refs_0_), channel_id=1, source_target_pairs={{16,0},{65,1},{18,2},{67,3},{20,4},{69,5},{22,6},{71,7},{24,8},{73... | collective-permute-start | bytes 3096584 | tf_op jit(solution)/shard_map/ppermute | solution.py:37
  47.4 2.6 %collective-permute-start.9 = (bf16[4,21,16,384]{3,2,1,0:T(8,128)(2,1)S(1)}, bf16[4,21,16,384]{3,2,1,0:T(8,128)(2,1)}, u32[]{:S(2)}, u32[]{:S(2)}) collective-permute-start(bf16[4,21,16,384]{3,2,1,0:T(8,128)(2,1)S(1)} %get-tuple-element.23.refs_0_), channel_id=1, source_target_pairs={{48,0},{193,1},{50,2},{195,3},{52,4},{197,5},{54,6},{199,7},{56,8}... | collective-permute-start | bytes 3096584 | tf_op jit(solution)/shard_map/ppermute | solution.py:37
  50.0 1.3 %broadcast_select_fusion = bf16[8,12,2,384]{3,2,1,0:T(2,128)(2,1)S(1)} fusion(pred[]{:T(512)S(6)} %eq.2, bf16[8,12,10,384]{3,2,1,0:T(8,128)(2,1)} %pad_maximum_fusion), kind=kLoop, calls=%fused_computation.9 | loop fusion | flops 73728 | bytes 442369 | tf_op jit(solution)/shard_map/jit(_where)/select_n | solution.py:292
  51.3 4.5 %collective-permute-start.10 = (bf16[8,12,2,384]{3,2,1,0:T(2,128)(2,1)S(1)}, bf16[8,12,2,384]{3,2,1,0:T(2,128)(2,1)S(1)}, u32[]{:S(2)}, u32[]{:S(2)}) collective-permute-start(bf16[8,12,2,384]{3,2,1,0:T(2,128)(2,1)S(1)} %broadcast_select_fusion), channel_id=1, source_target_pairs={{2,1},{1,2},{4,3},{3,4},{6,5},{5,6},{8,7},{7,8},{10,9},{9,10},{12,... | collective-permute-start | bytes 442376 | tf_op jit(solution)/shard_map/ppermute | solution.py:37
  55.8 3.2 %collective-permute-done.10 = bf16[8,12,2,384]{3,2,1,0:T(2,128)(2,1)S(1)} collective-permute-done((bf16[8,12,2,384]{3,2,1,0:T(2,128)(2,1)S(1)}, bf16[8,12,2,384]{3,2,1,0:T(2,128)(2,1)S(1)}, u32[]{:S(2)}, u32[]{:S(2)}) %collective-permute-start.10) | collective-permute-done | bytes 147488 | tf_op jit(solution)/shard_map/ppermute | solution.py:37
  59.0 2.7 %maximum_select_fusion.1 = bf16[8,12,12,384]{3,2,1,0:T(8,128)(2,1)S(1)} fusion(bf16[8,12,10,384]{3,2,1,0:T(8,128)(2,1)} %pad_maximum_fusion, bf16[8,12,2,384]{3,2,1,0:T(2,128)(2,1)S(1)} %collective-permute-done.10, pred[]{:T(512)S(6)} %eq.2), kind=kLoop, calls=%fused_computation.2 | loop fusion | flops 3981312 | bytes 1769473 | tf_op jit(solution)/shard_map/jit(_where)/select_n | solution.py:294
  61.7 0.0 copy-start.4
  61.7 0.6 collective-permute-done.8.refs_1_
  62.3 2.7 %collective-permute-done.9.refs_4_ = bf16[4,21,16,384]{3,2,1,0:T(8,128)(2,1)} collective-permute-done((bf16[4,21,16,384]{3,2,1,0:T(8,128)(2,1)S(1)}, bf16[4,21,16,384]{3,2,1,0:T(8,128)(2,1)}, u32[]{:S(2)}, u32[]{:S(2)}) %collective-permute-start.9) | collective-permute-done | bytes 1032224 | tf_op jit(solution)/shard_map/ppermute | solution.py:37
  65.0 0.5 copy.12
  65.5 2.5 %collective-permute-start.11 = (bf16[8,12,12,384]{3,0,2,1:T(8,128)(2,1)S(1)}, bf16[8,12,12,384]{3,0,2,1:T(8,128)(2,1)S(1)}, u32[]{:S(2)}, u32[]{:S(2)}) collective-permute-start(bf16[8,12,12,384]{3,0,2,1:T(8,128)(2,1)S(1)} %copy.12), channel_id=1, source_target_pairs={{1,0},{0,1},{3,2},{2,3},{5,4},{4,5},{7,6},{6,7},{9,8},{8,9},{11,10... | collective-permute-start | bytes 2654216 | tf_op jit(solution)/shard_map/ppermute | solution.py:37
  67.9 0.6 collective-permute-start.14
  68.6 0.8 collective-permute-start.15
  69.4 0.1 slice.60
  69.5 1.9 %collective-permute-start.12 = (bf16[2,21,16,384]{3,2,1,0:T(8,128)(2,1)S(1)}, bf16[2,21,16,384]{3,2,1,0:T(8,128)(2,1)S(1)}, u32[]{:S(2)}, u32[]{:S(2)}) collective-permute-start(bf16[2,21,16,384]{3,2,1,0:T(8,128)(2,1)S(1)} %slice.60), channel_id=1, source_target_pairs={{16,0},{65,1},{18,2},{67,3},{20,4},{69,5},{22,6},{71,7},{24,8},{73... | collective-permute-start | bytes 1548296 | tf_op jit(solution)/shard_map/ppermute | solution.py:37
  71.4 1.1 slice.61
  72.5 0.3 collective-permute-start.13
  72.8 0.2 copy.13
  72.9 1.5 %maximum_select_fusion.x_ref = bf16[8,12,24,384]{3,2,1,0:T(8,128)(2,1)S(1)} fusion(bf16[8,12,12,384]{3,2,1,0:T(8,128)(2,1)S(1)} %copy.13, bf16[8,12,12,384]{3,2,1,0:T(8,128)(2,1)S(1)} %maximum_select_fusion.1, pred[]{:T(512)S(6)} %eq.2), kind=kLoop, calls=%fused_computation | loop fusion | flops 7962624 | bytes 3538945 | tf_op jit(solution)/shard_map/jit(_where)/select_n | solution.py:302
  74.4 6.2 %first_layout.1.laid_ref = bf16[6,8,288,256]{3,2,1,0:T(8,128)(2,1)S(1)} custom-call(bf16[8,12,24,384]{3,2,1,0:T(8,128)(2,1)S(1)} %maximum_select_fusion.x_ref, f32[1,384]{1,0:T(1,128)S(1)} %reshape.10.gain_ref), custom_call_target="tpu_custom_call" | custom-call | tf_op jit(solution)/shard_map/first_layout/pallas_call | solution.py:124
  80.6 6.6 %collective-permute-done.12.refs_2_ = bf16[2,21,16,384]{3,2,1,0:T(8,128)(2,1)S(1)} collective-permute-done((bf16[2,21,16,384]{3,2,1,0:T(8,128)(2,1)S(1)}, bf16[2,21,16,384]{3,2,1,0:T(8,128)(2,1)S(1)}, u32[]{:S(2)}, u32[]{:S(2)}) %collective-permute-start.12) | collective-permute-done | bytes 516128 | tf_op jit(solution)/shard_map/ppermute | solution.py:37
  87.2 1.8 %collective-permute-done.13.refs_3_ = bf16[2,21,16,384]{3,2,1,0:T(8,128)(2,1)S(1)} collective-permute-done((bf16[2,21,16,384]{3,2,1,0:T(8,128)(2,1)S(1)}, bf16[2,21,16,384]{3,2,1,0:T(8,128)(2,1)S(1)}, u32[]{:S(2)}, u32[]{:S(2)}) %collective-permute-start.13) | collective-permute-done | bytes 516128 | tf_op jit(solution)/shard_map/ppermute | solution.py:37
  89.1 9.8 %first_conv.1 = (f32[6,240,384]{2,1,0:T(8,128)S(1)}, bf16[6,240,384]{2,1,0:T(8,128)(2,1)S(1)}) custom-call(bf16[6,8,288,256]{3,2,1,0:T(8,128)(2,1)S(1)} %first_layout.1.laid_ref, bf16[4,21,16,384]{3,2,1,0:T(8,128)(2,1)S(1)} %get-tuple-element.23.refs_0_, bf16[4,21,16,384]{3,2,1,0:T(8,128)(2,1)S(1)} %collective-permute-done.8.refs_1_, ...), custom_call_target="tpu_custom_call" | custom-call | tf_op jit(solution)/shard_map/first_conv/pallas_call | solution.py:202
  98.9 0.0 copy-start.5
  98.9 0.0 copy-start.6
  99.0 1.6 %collective-permute-start.16 = (bf16[6,240,384]{2,1,0:T(8,128)(2,1)S(1)}, bf16[6,240,384]{2,1,0:T(8,128)(2,1)S(1)}, u32[]{:S(2)}, u32[]{:S(2)}) collective-permute-start(bf16[6,240,384]{2,1,0:T(8,128)(2,1)S(1)} %get-tuple-element.32), channel_id=1, source_target_pairs={{1,0},{0,1},{3,2},{2,3},{5,4},{4,5},{7,6},{6,7},{9,8},{8,9},{11,10... | collective-permute-start | bytes 3317768 | tf_op jit(solution)/shard_map/ppermute | solution.py:37
  100.6 0.1 slice.62
  100.6 1.5 %collective-permute-start.17 = (bf16[2,21,16,384]{3,2,1,0:T(8,128)(2,1)S(1)}, bf16[2,21,16,384]{3,2,1,0:T(8,128)(2,1)S(1)}, u32[]{:S(2)}, u32[]{:S(2)}) collective-permute-start(bf16[2,21,16,384]{3,2,1,0:T(8,128)(2,1)S(1)} %slice.62), channel_id=1, source_target_pairs={{16,0},{65,1},{18,2},{67,3},{20,4},{69,5},{22,6},{71,7},{24,8},{73... | collective-permute-start | bytes 1548296 | tf_op jit(solution)/shard_map/ppermute | solution.py:37
  102.2 0.1 slice.63
  102.2 0.1 collective-permute-start.18
  102.4 0.6 collective-permute-done.16.other_ref
  103.0 4.4 %second_layout.1.laid_ref = bf16[6,6,240,256]{3,2,1,0:T(8,128)(2,1)S(1)} custom-call(f32[6,240,384]{2,1,0:T(8,128)S(1)} %get-tuple-element.29.mine_ref, bf16[6,240,384]{2,1,0:T(8,128)(2,1)S(1)} %collective-permute-done.16.other_ref, f32[1,384]{1,0:T(1,128)S(1)} %reshape.11.bias_ref, f32[1,384]{1,0:T(1,128)S(1)} %reshape.12.gain_ref), custom_call_target="tpu_custom_call" | custom-call | tf_op jit(solution)/shard_map/second_layout/pallas_call | solution.py:156
  107.4 0.0 copy-start.2
  107.4 0.0 copy-start.3
  107.4 1.6 %collective-permute-done.17.refs_2_ = bf16[2,21,16,384]{3,2,1,0:T(8,128)(2,1)S(1)} collective-permute-done((bf16[2,21,16,384]{3,2,1,0:T(8,128)(2,1)S(1)}, bf16[2,21,16,384]{3,2,1,0:T(8,128)(2,1)S(1)}, u32[]{:S(2)}, u32[]{:S(2)}) %collective-permute-start.17) | collective-permute-done | bytes 516128 | tf_op jit(solution)/shard_map/ppermute | solution.py:37
  109.0 2.5 %collective-permute-done.18.refs_3_ = bf16[2,21,16,384]{3,2,1,0:T(8,128)(2,1)S(1)} collective-permute-done((bf16[2,21,16,384]{3,2,1,0:T(8,128)(2,1)S(1)}, bf16[2,21,16,384]{3,2,1,0:T(8,128)(2,1)S(1)}, u32[]{:S(2)}, u32[]{:S(2)}) %collective-permute-start.18) | collective-permute-done | bytes 516128 | tf_op jit(solution)/shard_map/ppermute | solution.py:37
  111.5 4.8 %second_conv.1 = (f32[4,10,8,384]{3,2,1,0:T(8,128)S(1)}, f32[4,10,8,384]{3,2,1,0:T(8,128)S(1)}) custom-call(bf16[6,6,240,256]{3,2,1,0:T(8,128)(2,1)S(1)} %second_layout.1.laid_ref, bf16[4,21,16,384]{3,2,1,0:T(8,128)(2,1)S(1)} %get-tuple-element.30.refs_0_, bf16[4,21,16,384]{3,2,1,0:T(8,128)(2,1)S(1)} %collective-permute-done.14.refs_1_, ...), custom_call_target="tpu_custom_call" | custom-call | tf_op jit(solution)/shard_map/second_conv/pallas_call | solution.py:231
  116.3 0.2 collective-permute-start.19
  116.5 1.8 %collective-permute-done.19 = f32[4,10,8,384]{3,2,1,0:T(8,128)S(1)} collective-permute-done((f32[4,10,8,384]{3,2,1,0:T(8,128)S(1)}, f32[4,10,8,384]{3,2,1,0:T(8,128)S(1)}, u32[]{:S(2)}, u32[]{:S(2)}) %collective-permute-start.19) | collective-permute-done | bytes 491552 | tf_op jit(solution)/shard_map/ppermute | solution.py:37
  118.2 0.8 fusion.1
  (18 shorter events, 0.1 us)
Async XLA Ops:
  1.0 13.9 %collective-permute-start.2 = (bf16[4,8,10,384]{3,2,1,0:T(8,128)(2,1)S(1)}, bf16[4,8,10,384]{3,2,1,0:T(8,128)(2,1)S(1)}, u32[]{:S(2)}, u32[]{:S(2)}) collective-permute-start(bf16[4,8,10,384]{3,2,1,0:T(8,128)(2,1)S(1)} %copy.10), channel_id=1, source_target_pairs={{0,64},{1,65},{2,66},{3,67},{4,68},{5,69},{6,70},{7,71},{8,72},{9,... | collective-permute-start | bytes 737288 | tf_op jit(solution)/shard_map/ppermute | solution.py:37
  5.1 0.9 copy-start
  6.0 0.9 copy-start.1
  7.2 7.8 %collective-permute-start = (bf16[2,21,8,384]{3,2,1,0:T(8,128)(2,1)S(1)}, bf16[2,21,8,384]{3,2,1,0:T(8,128)(2,1)S(1)}, u32[]{:S(2)}, u32[]{:S(2)}) collective-permute-start(bf16[2,21,8,384]{3,2,1,0:T(8,128)(2,1)S(1)} %fold.1), channel_id=1, source_target_pairs={{0,0},{1,1},{2,2},{3,3},{4,4},{5,5},{6,6},{7,7},{8,8},{9,9},{10,10... | collective-permute-start | bytes 774152 | tf_op jit(solution)/shard_map/ppermute | solution.py:37
  7.9 13.6 %collective-permute-start.1 = (bf16[2,21,8,384]{3,2,1,0:T(8,128)(2,1)S(1)}, bf16[2,21,8,384]{3,2,1,0:T(8,128)(2,1)S(1)}, u32[]{:S(2)}, u32[]{:S(2)}) collective-permute-start(bf16[2,21,8,384]{3,2,1,0:T(8,128)(2,1)S(1)} %fold.1), channel_id=1, source_target_pairs={{8,0},{9,1},{10,2},{11,3},{12,4},{13,5},{14,6},{15,7},{0,8},{1,9},... | collective-permute-start | bytes 774152 | tf_op jit(solution)/shard_map/ppermute | solution.py:37
  21.6 19.0 %collective-permute-start.3 = (bf16[2,21,16,384]{3,2,1,0:T(8,128)(2,1)S(1)}, bf16[2,21,16,384]{3,2,1,0:T(8,128)(2,1)S(1)}, u32[]{:S(2)}, u32[]{:S(2)}) collective-permute-start(bf16[2,21,16,384]{3,2,1,0:T(8,128)(2,1)S(1)} %pad_maximum_fusion.4), channel_id=1, source_target_pairs={{64,0},{17,1},{66,2},{19,3},{68,4},{21,5},{70,6},{23,7},{72,8},{25... | collective-permute-start | bytes 1548296 | tf_op jit(solution)/shard_map/ppermute | solution.py:37
  24.1 16.5 %collective-permute-start.4 = (bf16[2,21,16,384]{3,2,1,0:T(8,128)(2,1)S(1)}, bf16[2,21,16,384]{3,2,1,0:T(8,128)(2,1)S(1)}, u32[]{:S(2)}, u32[]{:S(2)}) collective-permute-start(bf16[2,21,16,384]{3,2,1,0:T(8,128)(2,1)S(1)} %pad_maximum_fusion.4), channel_id=1, source_target_pairs={{128,0},{33,1},{130,2},{35,3},{132,4},{37,5},{134,6},{39,7},{136,8... | collective-permute-start | bytes 1548296 | tf_op jit(solution)/shard_map/ppermute | solution.py:37
  24.6 16.1 %collective-permute-start.5 = (bf16[2,21,16,384]{3,2,1,0:T(8,128)(2,1)S(1)}, bf16[2,21,16,384]{3,2,1,0:T(8,128)(2,1)S(1)}, u32[]{:S(2)}, u32[]{:S(2)}) collective-permute-start(bf16[2,21,16,384]{3,2,1,0:T(8,128)(2,1)S(1)} %pad_maximum_fusion.4), channel_id=1, source_target_pairs={{192,0},{49,1},{194,2},{51,3},{196,4},{53,5},{198,6},{55,7},{200,8... | collective-permute-start | bytes 1548296 | tf_op jit(solution)/shard_map/ppermute | solution.py:37
  25.3 14.0 %collective-permute-start.6 = (bf16[8,2,10,384]{3,2,1,0:T(8,128)(2,1)S(1)}, bf16[8,2,10,384]{3,2,1,0:T(8,128)(2,1)S(1)}, u32[]{:S(2)}, u32[]{:S(2)}) collective-permute-start(bf16[8,2,10,384]{3,2,1,0:T(8,128)(2,1)S(1)} %get-tuple-element.37), channel_id=1, source_target_pairs={{0,16},{1,17},{2,18},{3,19},{4,20},{5,21},{6,22},{7,23},{8,24},{9,... | collective-permute-start | bytes 368648 | tf_op jit(solution)/shard_map/ppermute | solution.py:37
  28.7 10.6 %collective-permute-start.7 = (bf16[8,2,10,384]{3,2,1,0:T(8,128)(2,1)S(1)}, bf16[8,2,10,384]{3,2,1,0:T(8,128)(2,1)S(1)}, u32[]{:S(2)}, u32[]{:S(2)}) collective-permute-start(bf16[8,2,10,384]{3,2,1,0:T(8,128)(2,1)S(1)} %get-tuple-element.38), channel_id=1, source_target_pairs={{16,0},{17,1},{18,2},{19,3},{20,4},{21,5},{22,6},{23,7},{24,8},{25... | collective-permute-start | bytes 368648 | tf_op jit(solution)/shard_map/ppermute | solution.py:37
  41.2 21.1 %collective-permute-start.8 = (bf16[4,21,16,384]{3,2,1,0:T(8,128)(2,1)S(1)}, bf16[4,21,16,384]{3,2,1,0:T(8,128)(2,1)S(1)}, u32[]{:S(2)}, u32[]{:S(2)}) collective-permute-start(bf16[4,21,16,384]{3,2,1,0:T(8,128)(2,1)S(1)} %get-tuple-element.23.refs_0_), channel_id=1, source_target_pairs={{16,0},{65,1},{18,2},{67,3},{20,4},{69,5},{22,6},{71,7},{24,8},{73... | collective-permute-start | bytes 3096584 | tf_op jit(solution)/shard_map/ppermute | solution.py:37
  47.4 17.6 %collective-permute-start.9 = (bf16[4,21,16,384]{3,2,1,0:T(8,128)(2,1)S(1)}, bf16[4,21,16,384]{3,2,1,0:T(8,128)(2,1)}, u32[]{:S(2)}, u32[]{:S(2)}) collective-permute-start(bf16[4,21,16,384]{3,2,1,0:T(8,128)(2,1)S(1)} %get-tuple-element.23.refs_0_), channel_id=1, source_target_pairs={{48,0},{193,1},{50,2},{195,3},{52,4},{197,5},{54,6},{199,7},{56,8}... | collective-permute-start | bytes 3096584 | tf_op jit(solution)/shard_map/ppermute | solution.py:37
  51.3 7.7 %collective-permute-start.10 = (bf16[8,12,2,384]{3,2,1,0:T(2,128)(2,1)S(1)}, bf16[8,12,2,384]{3,2,1,0:T(2,128)(2,1)S(1)}, u32[]{:S(2)}, u32[]{:S(2)}) collective-permute-start(bf16[8,12,2,384]{3,2,1,0:T(2,128)(2,1)S(1)} %broadcast_select_fusion), channel_id=1, source_target_pairs={{2,1},{1,2},{4,3},{3,4},{6,5},{5,6},{8,7},{7,8},{10,9},{9,10},{12,... | collective-permute-start | bytes 442376 | tf_op jit(solution)/shard_map/ppermute | solution.py:37
  61.7 11.1 %copy-start.4 = (f32[384]{0:T(512)S(1)}, f32[384]{0:T(512)}, u32[]{:S(2)}) copy-start(f32[384]{0:T(512)} %param.8) | copy-start | bytes 4612
  65.5 7.3 %collective-permute-start.11 = (bf16[8,12,12,384]{3,0,2,1:T(8,128)(2,1)S(1)}, bf16[8,12,12,384]{3,0,2,1:T(8,128)(2,1)S(1)}, u32[]{:S(2)}, u32[]{:S(2)}) collective-permute-start(bf16[8,12,12,384]{3,0,2,1:T(8,128)(2,1)S(1)} %copy.12), channel_id=1, source_target_pairs={{1,0},{0,1},{3,2},{2,3},{5,4},{4,5},{7,6},{6,7},{9,8},{8,9},{11,10... | collective-permute-start | bytes 2654216 | tf_op jit(solution)/shard_map/ppermute | solution.py:37
  67.9 31.0 %collective-permute-start.14 = (bf16[4,21,16,384]{3,2,1,0:T(8,128)(2,1)S(1)}, bf16[4,21,16,384]{3,2,1,0:T(8,128)(2,1)S(1)}, u32[]{:S(2)}, u32[]{:S(2)}) collective-permute-start(bf16[4,21,16,384]{3,2,1,0:T(8,128)(2,1)S(1)} %get-tuple-element.30.refs_0_), channel_id=1, source_target_pairs={{16,0},{65,1},{18,2},{67,3},{20,4},{69,5},{22,6},{71,7},{24,8},{73... | collective-permute-start | bytes 3096584 | tf_op jit(solution)/shard_map/ppermute | solution.py:37
  68.6 30.4 %collective-permute-start.15 = (bf16[4,21,16,384]{3,2,1,0:T(8,128)(2,1)S(1)}, bf16[4,21,16,384]{3,2,1,0:T(8,128)(2,1)S(1)}, u32[]{:S(2)}, u32[]{:S(2)}) collective-permute-start(bf16[4,21,16,384]{3,2,1,0:T(8,128)(2,1)S(1)} %get-tuple-element.30.refs_0_), channel_id=1, source_target_pairs={{48,0},{193,1},{50,2},{195,3},{52,4},{197,5},{54,6},{199,7},{56,8}... | collective-permute-start | bytes 3096584 | tf_op jit(solution)/shard_map/ppermute | solution.py:37
  69.5 17.8 %collective-permute-start.12 = (bf16[2,21,16,384]{3,2,1,0:T(8,128)(2,1)S(1)}, bf16[2,21,16,384]{3,2,1,0:T(8,128)(2,1)S(1)}, u32[]{:S(2)}, u32[]{:S(2)}) collective-permute-start(bf16[2,21,16,384]{3,2,1,0:T(8,128)(2,1)S(1)} %slice.60), channel_id=1, source_target_pairs={{16,0},{65,1},{18,2},{67,3},{20,4},{69,5},{22,6},{71,7},{24,8},{73... | collective-permute-start | bytes 1548296 | tf_op jit(solution)/shard_map/ppermute | solution.py:37
  72.5 16.6 %collective-permute-start.13 = (bf16[2,21,16,384]{3,2,1,0:T(8,128)(2,1)S(1)}, bf16[2,21,16,384]{3,2,1,0:T(8,128)(2,1)S(1)}, u32[]{:S(2)}, u32[]{:S(2)}) collective-permute-start(bf16[2,21,16,384]{3,2,1,0:T(8,128)(2,1)S(1)} %slice.61), channel_id=1, source_target_pairs={{48,0},{193,1},{50,2},{195,3},{52,4},{197,5},{54,6},{199,7},{56,8}... | collective-permute-start | bytes 1548296 | tf_op jit(solution)/shard_map/ppermute | solution.py:37
  98.9 3.4 %copy-start.5 = (f32[384]{0:T(512)S(1)}, f32[384]{0:T(512)}, u32[]{:S(2)}) copy-start(f32[384]{0:T(512)} %param.10) | copy-start | bytes 4612
  98.9 3.4 %copy-start.6 = (f32[384]{0:T(512)S(1)}, f32[384]{0:T(512)}, u32[]{:S(2)}) copy-start(f32[384]{0:T(512)} %param.11) | copy-start | bytes 4612
  99.0 4.0 %collective-permute-start.16 = (bf16[6,240,384]{2,1,0:T(8,128)(2,1)S(1)}, bf16[6,240,384]{2,1,0:T(8,128)(2,1)S(1)}, u32[]{:S(2)}, u32[]{:S(2)}) collective-permute-start(bf16[6,240,384]{2,1,0:T(8,128)(2,1)S(1)} %get-tuple-element.32), channel_id=1, source_target_pairs={{1,0},{0,1},{3,2},{2,3},{5,4},{4,5},{7,6},{6,7},{9,8},{8,9},{11,10... | collective-permute-start | bytes 3317768 | tf_op jit(solution)/shard_map/ppermute | solution.py:37
  100.6 8.3 %collective-permute-start.17 = (bf16[2,21,16,384]{3,2,1,0:T(8,128)(2,1)S(1)}, bf16[2,21,16,384]{3,2,1,0:T(8,128)(2,1)S(1)}, u32[]{:S(2)}, u32[]{:S(2)}) collective-permute-start(bf16[2,21,16,384]{3,2,1,0:T(8,128)(2,1)S(1)} %slice.62), channel_id=1, source_target_pairs={{16,0},{65,1},{18,2},{67,3},{20,4},{69,5},{22,6},{71,7},{24,8},{73... | collective-permute-start | bytes 1548296 | tf_op jit(solution)/shard_map/ppermute | solution.py:37
  102.2 9.2 %collective-permute-start.18 = (bf16[2,21,16,384]{3,2,1,0:T(8,128)(2,1)S(1)}, bf16[2,21,16,384]{3,2,1,0:T(8,128)(2,1)S(1)}, u32[]{:S(2)}, u32[]{:S(2)}) collective-permute-start(bf16[2,21,16,384]{3,2,1,0:T(8,128)(2,1)S(1)} %slice.63), channel_id=1, source_target_pairs={{48,0},{193,1},{50,2},{195,3},{52,4},{197,5},{54,6},{199,7},{56,8}... | collective-permute-start | bytes 1548296 | tf_op jit(solution)/shard_map/ppermute | solution.py:37
  107.4 10.9 %copy-start.2 = (bf16[4,8,10,384]{3,1,2,0:T(8,128)(2,1)S(1)}, bf16[4,8,10,384]{3,1,2,0:T(8,128)(2,1)}, u32[]{:S(2)}) copy-start(bf16[4,8,10,384]{3,1,2,0:T(8,128)(2,1)} %param.7) | copy-start | bytes 737284
  107.4 10.9 %copy-start.3 = (f32[384]{0:T(512)S(1)}, f32[384]{0:T(512)}, u32[]{:S(2)}) copy-start(f32[384]{0:T(512)} %param.13) | copy-start | bytes 4612
  116.3 2.0 %collective-permute-start.19 = (f32[4,10,8,384]{3,2,1,0:T(8,128)S(1)}, f32[4,10,8,384]{3,2,1,0:T(8,128)S(1)}, u32[]{:S(2)}, u32[]{:S(2)}) collective-permute-start(f32[4,10,8,384]{3,2,1,0:T(8,128)S(1)} %get-tuple-element.36), channel_id=1, source_target_pairs={{1,0},{0,1},{3,2},{2,3},{5,4},{4,5},{7,6},{6,7},{9,8},{8,9},{11,10... | collective-permute-start | bytes 1474568 | tf_op jit(solution)/shard_map/ppermute | solution.py:37

commit v3 on v2

--- a/solution.py
+++ b/solution.py
@@ -1,3 +1,5 @@
+import functools
+
 import jax
 import jax.numpy as jnp
 from jax import lax
@@ -170,34 +172,71 @@
     )(mine, other, bias, gain)
 
 
-def tap_sum(laid_ref, blocks, first, frames, count):
+def left_of(laid_ref, g, first, frames, count, lanes):
     def window(slot, tap):
         dt, start = tap // 9, 24 * (tap % 9 // 3)
+        at = slice(start, start + count)
         return jnp.concatenate(
-            [laid_ref[slot, first + dt + i, start : start + count] for i in range(frames)], axis=0
+            [laid_ref[slot, first + dt + i, at, lanes] for i in range(frames)], axis=0
         )
 
+    if g < len(MAIN):
+        return window(MAIN[g] % 3, MAIN[g]) + window(3 + g % 3, PAIRED[g // 3])
+    return window(1, ALONE[g - len(MAIN)])
+
+
+def near_sum(laid_ref, blocks, first, frames, count):
+    zeros = jnp.zeros((LANES // 4, CHANS), BF)
     total = None
     for g in range(GROUPS):
-        if g < len(MAIN):
-            left = window(MAIN[g] % 3, MAIN[g]) + window(3 + g % 3, PAIRED[g // 3])
-        else:
-            left = window(1, ALONE[g - len(MAIN)])
-        right = jnp.concatenate([b[i, g] for b in blocks for i in range(b.shape[0])], axis=0)
+        rows = [b[i, g] for b in blocks for i in range(2)]
+        right = jnp.concatenate(rows[:8] + [zeros] + rows[8:], axis=0)
+        left = left_of(laid_ref, g, first, frames, count, slice(0, LANES))
         term = jnp.dot(left, right, preferred_element_type=F32)
         total = term if total is None else total + term
     return total
 
 
-def first_conv_kernel(laid_ref, *refs):
-    *blocks, mine_ref, sent_ref = refs
-    total = tap_sum(laid_ref, blocks, 2 * pl.program_id(0), 2, 10 * 24)
-    total = total.reshape(2, 10 * 24, CHANS)
+def far_sum(laid_ref, blocks, first, frames, count):
+    total = None
+    for base in range(0, GROUPS, 4):
+        groups = range(base, min(base + 4, GROUPS))
+        left, right = [], []
+        for g in groups:
+            left.append(left_of(laid_ref, g, first, frames, count, slice(128, 256))[:, :64])
+            right += [b[i, g] for b in blocks for i in range(2)]
+        left, right = jnp.concatenate(left, axis=1), jnp.concatenate(right, axis=0)
+        term = jnp.dot(left, right, preferred_element_type=F32)
+        total = term if total is None else total + term
+    return total
+
+
+def near_kernel(frames, count, laid_ref, *refs):
+    *blocks, out_ref = refs
+    total = near_sum(laid_ref, blocks, 2 * pl.program_id(0), 2, count)
+    out_ref[...] = total.reshape(2, count, CHANS)
+
+
+def near_conv(laid, blocks, frames, count):
+    return pl.pallas_call(
+        functools.partial(near_kernel, frames, count),
+        grid=(frames // 2,),
+        out_shape=jax.ShapeDtypeStruct((frames, count, CHANS), F32),
+        in_specs=[whole] * (1 + len(blocks)),
+        out_specs=pl.BlockSpec((2, count, CHANS), lambda f: (f, 0, 0)),
+        compiler_params=VMEM,
+        name="near_conv",
+    )(laid, *blocks)
+
+
+def first_conv_kernel(laid_ref, b0, b1, near_ref, mine_ref, sent_ref):
+    total = far_sum(laid_ref, (b0, b1), 2 * pl.program_id(0), 2, 10 * 24)
+    total = near_ref[...] + total.reshape(2, 10 * 24, CHANS)
     mine_ref[...] = total
     sent_ref[...] = total.astype(BF)
 
 
-def first_conv(laid, blocks):
+def first_conv(laid, blocks, near):
     out = pl.BlockSpec((2, 10 * 24, CHANS), lambda f: (f, 0, 0))
     return pl.pallas_call(
         first_conv_kernel,
@@ -206,16 +245,16 @@
             jax.ShapeDtypeStruct((6, 10 * 24, CHANS), F32),
             jax.ShapeDtypeStruct((6, 10 * 24, CHANS), BF),
         ),
-        in_specs=[whole] * (1 + len(blocks)),
+        in_specs=[whole] * 3 + [out],
         out_specs=(out, out),
         compiler_params=VMEM,
         name="first_conv",
-    )(laid, *blocks)
-
-
-def second_conv_kernel(laid_ref, *refs):
-    *blocks, mine_ref, sent_ref, total_ref = refs
-    total = tap_sum(laid_ref, blocks, 2 * pl.program_id(0), 2, 8 * 24)
+    )(laid, *blocks, near)
+
+
+def second_conv_kernel(laid_ref, b0, b1, near_ref, mine_ref, sent_ref, total_ref):
+    total = far_sum(laid_ref, (b0, b1), 2 * pl.program_id(0), 2, 8 * 24)
+    total = near_ref[...].reshape(2 * 192, CHANS) + total
     for part in range(3):
         total_ref[part] = total[:, 128 * part : 128 * part + 128]
     own = 10 * lax.axis_index("c")
@@ -226,7 +265,7 @@
             sent_ref[f, w] = take(total_ref, at + 10 - own, 8, 24)
 
 
-def second_conv(laid, blocks):
+def second_conv(laid, blocks, near):
     out = pl.BlockSpec((2, 10, 8, CHANS), lambda f: (f, 0, 0, 0))
     return pl.pallas_call(
         second_conv_kernel,
@@ -235,12 +274,12 @@
             jax.ShapeDtypeStruct((4, 10, 8, CHANS), F32),
             jax.ShapeDtypeStruct((4, 10, 8, CHANS), F32),
         ),
-        in_specs=[whole] * (1 + len(blocks)),
+        in_specs=[whole] * 3 + [pl.BlockSpec((2, 8 * 24, CHANS), lambda f: (f, 0, 0))],
         out_specs=(out, out),
         scratch_shapes=[pltpu.VMEM((3, 2 * 192, 128), F32)],
         compiler_params=VMEM,
         name="second_conv",
-    )(laid, *blocks)
+    )(laid, *blocks, near)
 
 
 def solution(mesh):
@@ -265,13 +304,19 @@
     def first_ring(x):
         up, down = sent(x, along(True, 1)), sent(x, along(True, -1))
         far = sent(x, along(True, 2))
-        return [jnp.stack([x[i], up[i], far[i], down[i]]) for i in range(2)]
+        return [(jnp.stack([x[i], up[i]]), jnp.stack([far[i], down[i]])) for i in range(2)]
 
     def second_ring(x):
-        return sent(x, along(False, 1)), sent(x, along(False, -1))
-
-    def passed_on(up, down):
-        return sent(up[:2], along(False, 1)), sent(down[2:], along(False, -1))
+        return sent(x[0], along(False, 1)), sent(x[1], along(False, -1))
+
+    def second_ring_rest(x):
+        return sent(x[1], along(False, 1)), sent(x[0], along(False, -1))
+
+    def passed_on(first_up, last_down):
+        return sent(first_up, along(False, 1)), sent(last_down, along(False, -1))
+
+    def in_order(x, first_up, last_down, last_up, first_down):
+        return (*x, first_up, last_up, first_down, last_down)
 
     def swapped(x):
         return sent(x, lambda t, h, z, c: (t, h, z, 1 - c))
@@ -313,18 +358,23 @@
         gains = [v.reshape(1, CHANS) for v in (gain_1, gain_2, bias_1)]
         both = fold(kernel_1, kernel_2)
         both = jnp.concatenate([z_near(both), z_far(both)], axis=2)
-        both, wide = at_once(both, taller(features))
-        one, two, wide = at_once(*first_ring(both), higher(wide))
-        up, down = second_ring(one)
-        up, down, wide, two = at_once(up, down, wider(wide, core), two)
-        far = passed_on(up, down)
-        next_up, next_down = second_ring(two)
+        both, wide = at_once(both, higher(taller(features)))
+        one, two = first_ring(both)
+        (one, two), wide = at_once((one, two), wider(wide, core))
+        ends, rest = second_ring(one), second_ring_rest(one)
         laid = first_layout(joined(wide, core), gains[0])
-        mine, passed = first_conv(laid, (one, up, *far, down))
-        next_up, next_down, passed = at_once(next_up, next_down, passed)
-        far = passed_on(next_up, next_down)
+        ends, laid, two = at_once(ends, laid, two)
+        far = passed_on(*ends)
+        rest = at_once(*rest)
+        next_ends = second_ring(two)
+        near = near_conv(laid, in_order(one, *ends, *rest), 6, 10 * 24)
+        far, near, next_ends = at_once(far, near, next_ends)
+        mine, passed = first_conv(laid, far, near)
+        next_rest = second_ring_rest(two)
+        far = passed_on(*next_ends)
         laid = second_layout(mine, swapped(passed), gains[2], gains[1])
-        mine, passed = second_conv(laid, (two, next_up, *far, next_down))
+        near = near_conv(laid, in_order(two, *next_ends, *next_rest), 4, 8 * 24)
+        mine, passed = second_conv(laid, far, near)
         own = jnp.transpose(features, (0, 2, 1, 3)).astype(F32)
         total = mine + swapped(passed) + bias_2 + own
         return jnp.transpose(total.astype(BF), (0, 2, 1, 3))

time: 119 us -> 104 us (0.87)
  waiting for transfers between devices: 37.1 us -> 16.9 us
  starting transfers between devices: 42.9 us -> 49.6 us
  other arithmetic: 8.13 us -> 3.75 us
  Pallas kernels: 25.5 us -> 28.9 us
    ppermute x20 -> x24, waiting for transfers between devices: 37.1 us -> 16.9 us  [move(): return lax.ppermute(x, AXES, pairs)]
    pallas_call x0 -> x2, Pallas kernels: none -> 13.1 us  [near_conv(): pl.pallas_call(functools.partial(near_kernel, frames, count), grid=(frame...]
    pallas_call x1, Pallas kernels: 9.85 us -> 2.96 us  [first_conv(): pl.pallas_call(first_conv_kernel, grid=(3,), out_shape=(jax.ShapeDtypeStr...]
    ppermute x20 -> x24, starting transfers between devices: 42.9 us -> 49.6 us  [move(): return lax.ppermute(x, AXES, pairs)]
    pallas_call x1, Pallas kernels: 4.81 us -> 1.85 us  [second_conv(): pl.pallas_call(second_conv_kernel, grid=(2,), out_shape=(jax.ShapeDtypeSt...]
    select_n x1, other arithmetic: 2.67 us -> 0.83 us  [wider(): jnp.where(core == 0, jnp.concatenate([beside, x], axis=2), jnp.concatenat...]
    slice x8 -> x4, local copies, waits for them, and re-layouts: 1.46 us -> 0.22 us  [the longest x1 0.05 us: first_ring(): x[i]]
    select_n x1, other arithmetic: 1.35 us -> 0.11 us  [wider(): edge = jnp.where(core == 0, x[:, :, :2], x[:, :, -2:])]
  transfers between devices with their start and end apart: 20 -> 24, of which waited for: 11 -> 8; matrix products, arithmetic and copies ran while one was open for 7% -> 3% of each run, Pallas kernels for 17% -> 23%
where the time goes in v3:
time: 104 us
  starting transfers between devices  49.6 us (48%)
  Pallas kernels  28.9 us (28%)
  waiting for transfers between devices  16.9 us (16%)
  local copies, waits for them, and re-layouts  3.99 us (4%)
  other arithmetic  3.75 us (4%)
    ppermute x24, starting transfers between devices, move(): return lax.ppermute(x, AXES, pairs)  49.6 us
    ppermute x24, waiting for transfers between devices, move(): return lax.ppermute(x, AXES, pairs)  16.9 us
    pallas_call x2, Pallas kernels, near_conv(): pl.pallas_call(functools.partial(near_kernel, frames, count), grid=(frame...  13.1 us
    pallas_call x1, Pallas kernels, first_layout(): pl.pallas_call(first_layout_kernel, grid=(8,), out_shape=jax.ShapeDtypeSt...  6.16 us
    pallas_call x1, Pallas kernels, second_layout(): pl.pallas_call(second_layout_kernel, grid=(6,), out_shape=jax.ShapeDtypeS...  4.42 us
    pallas_call x1, Pallas kernels, first_conv(): pl.pallas_call(first_conv_kernel, grid=(3,), out_shape=(jax.ShapeDtypeStr...  2.96 us
    unnamed x16, local copies, waits for them, and re-layouts  2.95 us
  transfers between devices with their start and end apart: 24, of which 8 were waited for; matrix products, arithmetic and copies ran while one was open for 3% of the time, Pallas kernels for 23%

profile of v3, /device:TPU:1, one launch (start us, length us, event | category | flops | bytes accessed | tf_op | source)
XLA Modules:
  0.0 103.5 jit_solution(16573989451539252721)
XLA Ops:
  0.0 1.1 %copy.10 = bf16[4,8,10,384]{3,2,1,0:T(8,128)(2,1)S(1)} copy(bf16[4,8,10,384]{3,1,2,0:T(8,128)(2,1)} %param.7) | data formatting | bytes 491520 | tf_op args[0]
  1.1 4.1 %collective-permute-start.2 = (bf16[4,8,10,384]{3,2,1,0:T(8,128)(2,1)S(1)}, bf16[4,8,10,384]{3,2,1,0:T(8,128)(2,1)S(1)}, u32[]{:S(2)}, u32[]{:S(2)}) collective-permute-start(bf16[4,8,10,384]{3,2,1,0:T(8,128)(2,1)S(1)} %copy.10), channel_id=1, source_target_pairs={{0,64},{1,65},{2,66},{3,67},{4,68},{5,69},{6,70},{7,71},{8,72},{9,... | collective-permute-start | bytes 737288 | tf_op jit(solution)/shard_map/ppermute | solution.py:39
  5.1 0.0 copy-start
  5.1 0.9 copy-done
  6.1 0.9 copy-done.1
  7.0 0.3 fold.1
  7.3 0.7 collective-permute-start
  8.0 7.0 %collective-permute-start.1 = (bf16[2,21,8,384]{3,2,1,0:T(8,128)(2,1)S(1)}, bf16[2,21,8,384]{3,2,1,0:T(8,128)(2,1)S(1)}, u32[]{:S(2)}, u32[]{:S(2)}) collective-permute-start(bf16[2,21,8,384]{3,2,1,0:T(8,128)(2,1)S(1)} %fold.1), channel_id=1, source_target_pairs={{8,0},{9,1},{10,2},{11,3},{12,4},{13,5},{14,6},{15,7},{0,8},{1,9},... | collective-permute-start | bytes 774152 | tf_op jit(solution)/shard_map/ppermute | solution.py:39
  15.0 0.1 copy_dynamic-update-slice_fusion
  15.2 3.1 %collective-permute-start.3 = (bf16[8,2,10,384]{3,2,1,0:T(8,128)(2,1)S(1)}, bf16[8,2,10,384]{3,2,1,0:T(8,128)(2,1)S(1)}, u32[]{:S(2)}, u32[]{:S(2)}) collective-permute-start(bf16[8,2,10,384]{3,2,1,0:T(8,128)(2,1)S(1)} %get-tuple-element.51), channel_id=1, source_target_pairs={{0,16},{1,17},{2,18},{3,19},{4,20},{5,21},{6,22},{7,23},{8,24},{9,... | collective-permute-start | bytes 368648 | tf_op jit(solution)/shard_map/ppermute | solution.py:39
  18.3 1.3 %collective-permute-start.4 = (bf16[8,2,10,384]{3,2,1,0:T(8,128)(2,1)S(1)}, bf16[8,2,10,384]{3,2,1,0:T(8,128)(2,1)S(1)}, u32[]{:S(2)}, u32[]{:S(2)}) collective-permute-start(bf16[8,2,10,384]{3,2,1,0:T(8,128)(2,1)S(1)} %get-tuple-element.52), channel_id=1, source_target_pairs={{16,0},{17,1},{18,2},{19,3},{20,4},{21,5},{22,6},{23,7},{24,8},{25... | collective-permute-start | bytes 368648 | tf_op jit(solution)/shard_map/ppermute | solution.py:39
  19.6 0.0 collective-permute-done
  19.6 2.0 %collective-permute-done.1 = bf16[2,21,8,384]{3,2,1,0:T(8,128)(2,1)S(1)} collective-permute-done((bf16[2,21,8,384]{3,2,1,0:T(8,128)(2,1)S(1)}, bf16[2,21,8,384]{3,2,1,0:T(8,128)(2,1)S(1)}, u32[]{:S(2)}, u32[]{:S(2)}) %collective-permute-start.1) | collective-permute-done | bytes 258080 | tf_op jit(solution)/shard_map/ppermute | solution.py:39
  21.6 0.1 pad_maximum_fusion.1
  21.6 0.0 collective-permute-done.3
  21.7 3.4 %collective-permute-done.4 = bf16[8,2,10,384]{3,2,1,0:T(8,128)(2,1)S(1)} collective-permute-done((bf16[8,2,10,384]{3,2,1,0:T(8,128)(2,1)S(1)}, bf16[8,2,10,384]{3,2,1,0:T(8,128)(2,1)S(1)}, u32[]{:S(2)}, u32[]{:S(2)}) %collective-permute-start.4) | collective-permute-done | bytes 122912 | tf_op jit(solution)/shard_map/ppermute | solution.py:39
  25.1 0.3 pad_maximum_fusion
  25.3 2.5 %collective-permute-start.6 = (bf16[2,21,16,384]{3,2,1,0:T(8,128)(2,1)S(1)}, bf16[2,21,16,384]{3,2,1,0:T(8,128)(2,1)S(1)}, u32[]{:S(2)}, u32[]{:S(2)}) collective-permute-start(bf16[2,21,16,384]{3,2,1,0:T(8,128)(2,1)S(1)} %pad_maximum_fusion.1), channel_id=1, source_target_pairs={{128,0},{33,1},{130,2},{35,3},{132,4},{37,5},{134,6},{39,7},{136,8... | collective-permute-start | bytes 1548296 | tf_op jit(solution)/shard_map/ppermute | solution.py:39
  27.8 0.0 collective-permute-start.7
  27.8 2.7 %collective-permute-start.5 = (bf16[2,21,16,384]{3,2,1,0:T(8,128)(2,1)S(1)}, bf16[2,21,16,384]{3,2,1,0:T(8,128)(2,1)S(1)}, u32[]{:S(2)}, u32[]{:S(2)}) collective-permute-start(bf16[2,21,16,384]{3,2,1,0:T(8,128)(2,1)S(1)} %pad_maximum_fusion.1), channel_id=1, source_target_pairs={{64,0},{17,1},{66,2},{19,3},{68,4},{21,5},{70,6},{23,7},{72,8},{25... | collective-permute-start | bytes 1548296 | tf_op jit(solution)/shard_map/ppermute | solution.py:39
  30.5 0.1 broadcast_select_fusion
  30.6 7.6 %collective-permute-start.8 = (bf16[8,12,2,384]{3,2,1,0:T(2,128)(2,1)S(1)}, bf16[8,12,2,384]{3,2,1,0:T(2,128)(2,1)S(1)}, u32[]{:S(2)}, u32[]{:S(2)}) collective-permute-start(bf16[8,12,2,384]{3,2,1,0:T(2,128)(2,1)S(1)} %broadcast_select_fusion), channel_id=1, source_target_pairs={{2,1},{1,2},{4,3},{3,4},{6,5},{5,6},{8,7},{7,8},{10,9},{9,10},{12,... | collective-permute-start | bytes 442376 | tf_op jit(solution)/shard_map/ppermute | solution.py:39
  38.3 0.1 fusion.5
  38.4 3.0 %collective-permute-done.8 = bf16[8,12,2,384]{3,2,1,0:T(2,128)(2,1)S(1)} collective-permute-done((bf16[8,12,2,384]{3,2,1,0:T(2,128)(2,1)S(1)}, bf16[8,12,2,384]{3,2,1,0:T(2,128)(2,1)S(1)}, u32[]{:S(2)}, u32[]{:S(2)}) %collective-permute-start.8) | collective-permute-done | bytes 147488 | tf_op jit(solution)/shard_map/ppermute | solution.py:39
  41.4 0.8 maximum_select_fusion.1
  42.2 0.0 collective-permute-done.6
  42.2 0.1 fusion.3
  42.3 0.0 collective-permute-done.7
  42.3 0.1 fusion.4
  42.4 0.1 pad_maximum_fusion.3
  42.5 0.1 fusion.6
  42.6 0.0 copy-start.4
  42.6 0.1 pad_maximum_fusion.2
  42.7 0.5 copy.12
  43.3 3.7 %collective-permute-start.11 = (bf16[8,12,12,384]{3,0,2,1:T(8,128)(2,1)S(1)}, bf16[8,12,12,384]{3,0,2,1:T(8,128)(2,1)S(1)}, u32[]{:S(2)}, u32[]{:S(2)}) collective-permute-start(bf16[8,12,12,384]{3,0,2,1:T(8,128)(2,1)S(1)} %copy.12), channel_id=1, source_target_pairs={{1,0},{0,1},{3,2},{2,3},{5,4},{4,5},{7,6},{6,7},{9,8},{8,9},{11,10... | collective-permute-start | bytes 2654216 | tf_op jit(solution)/shard_map/ppermute | solution.py:39
  47.0 0.9 collective-permute-start.10
  47.8 1.8 %collective-permute-start.9 = (bf16[2,21,16,384]{3,2,1,0:T(8,128)(2,1)S(1)}, bf16[2,21,16,384]{3,2,1,0:T(8,128)(2,1)S(1)}, u32[]{:S(2)}, u32[]{:S(2)}) collective-permute-start(bf16[2,21,16,384]{3,2,1,0:T(8,128)(2,1)S(1)} %get-tuple-element.30.refs_0_), channel_id=1, source_target_pairs={{16,0},{65,1},{18,2},{67,3},{20,4},{69,5},{22,6},{71,7},{24,8},{73... | collective-permute-start | bytes 1548296 | tf_op jit(solution)/shard_map/ppermute | solution.py:39
  49.6 1.1 %collective-permute-start.14 = (bf16[2,21,16,384]{3,2,1,0:T(8,128)(2,1)S(1)}, bf16[2,21,16,384]{3,2,1,0:T(8,128)(2,1)S(1)}, u32[]{:S(2)}, u32[]{:S(2)}) collective-permute-start(bf16[2,21,16,384]{3,2,1,0:T(8,128)(2,1)S(1)} %get-tuple-element.31.refs_1_), channel_id=1, source_target_pairs={{16,0},{65,1},{18,2},{67,3},{20,4},{69,5},{22,6},{71,7},{24,8},{73... | collective-permute-start | bytes 1548296 | tf_op jit(solution)/shard_map/ppermute | solution.py:39
  50.8 0.3 collective-permute-start.15
  51.1 0.0 collective-permute-done.11
  51.1 0.2 copy.13
  51.3 1.4 %maximum_select_fusion.x_ref = bf16[8,12,24,384]{3,2,1,0:T(8,128)(2,1)S(1)} fusion(bf16[8,12,12,384]{3,2,1,0:T(8,128)(2,1)S(1)} %copy.13, bf16[8,12,12,384]{3,2,1,0:T(8,128)(2,1)S(1)} %maximum_select_fusion.1, pred[]{:T(512)S(6)} %eq.2), kind=kLoop, calls=%fused_computation | loop fusion | flops 7962624 | bytes 3538945 | tf_op jit(solution)/shard_map/jit(_where)/select_n | solution.py:347
  52.8 6.2 %first_layout.1.laid_ref = bf16[6,8,288,256]{3,2,1,0:T(8,128)(2,1)S(1)} custom-call(bf16[8,12,24,384]{3,2,1,0:T(8,128)(2,1)S(1)} %maximum_select_fusion.x_ref, f32[1,384]{1,0:T(1,128)S(1)} %reshape.10.gain_ref), custom_call_target="tpu_custom_call" | custom-call | tf_op jit(solution)/shard_map/first_layout/pallas_call | solution.py:126
  58.9 2.4 %collective-permute-start.12 = (bf16[2,21,16,384]{3,2,1,0:T(8,128)(2,1)S(1)}, bf16[2,21,16,384]{3,2,1,0:T(8,128)(2,1)S(1)}, u32[]{:S(2)}, u32[]{:S(2)}) collective-permute-start(bf16[2,21,16,384]{3,2,1,0:T(8,128)(2,1)S(1)} %collective-permute-done.9.refs_2_), channel_id=1, source_target_pairs={{16,0},{65,1},{18,2},{67,3},{20,4},{69,5},{22,6},{71,7},{24,8},{73... | collective-permute-start | bytes 1548296 | tf_op jit(solution)/shard_map/ppermute | solution.py:39
  61.4 2.7 %collective-permute-start.16 = (bf16[2,21,16,384]{3,2,1,0:T(8,128)(2,1)S(1)}, bf16[2,21,16,384]{3,2,1,0:T(8,128)(2,1)S(1)}, u32[]{:S(2)}, u32[]{:S(2)}) collective-permute-start(bf16[2,21,16,384]{3,2,1,0:T(8,128)(2,1)S(1)} %get-tuple-element.40.refs_0_), channel_id=1, source_target_pairs={{16,0},{65,1},{18,2},{67,3},{20,4},{69,5},{22,6},{71,7},{24,8},{73... | collective-permute-start | bytes 1548296 | tf_op jit(solution)/shard_map/ppermute | solution.py:39
  64.1 8.5 %near_conv.2.near_ref = f32[6,240,384]{2,1,0:T(8,128)S(1)} custom-call(bf16[6,8,288,256]{3,2,1,0:T(8,128)(2,1)S(1)} %first_layout.1.laid_ref, bf16[2,21,16,384]{3,2,1,0:T(8,128)(2,1)S(1)} %get-tuple-element.30.refs_0_, bf16[2,21,16,384]{3,2,1,0:T(8,128)(2,1)S(1)} %get-tuple-element.31.refs_1_, bf16[2,21,16,384]{3,2,1,0:T(8,128)(2,1)S(1)} %collective-permute-done.9.refs_2_, ...), custom_call_target="tpu_custom_call" | custom-call | tf_op jit(solution)/shard_map/near_conv/pallas_call | solution.py:221
  72.6 0.0 copy-start.5
  72.6 0.0 copy-start.6
  72.6 0.3 collective-permute-done.16.refs_2_
  72.9 3.4 %collective-permute-done.17.refs_5_ = bf16[2,21,16,384]{3,2,1,0:T(8,128)(2,1)S(1)} collective-permute-done((bf16[2,21,16,384]{3,2,1,0:T(8,128)(2,1)S(1)}, bf16[2,21,16,384]{3,2,1,0:T(8,128)(2,1)S(1)}, u32[]{:S(2)}, u32[]{:S(2)}) %collective-permute-start.17) | collective-permute-done | bytes 516128 | tf_op jit(solution)/shard_map/ppermute | solution.py:39
  76.3 3.0 %first_conv.1 = (f32[6,240,384]{2,1,0:T(8,128)S(1)}, bf16[6,240,384]{2,1,0:T(8,128)(2,1)S(1)}) custom-call(bf16[6,8,288,256]{3,2,1,0:T(8,128)(2,1)S(1)} %first_layout.1.laid_ref, bf16[2,21,16,384]{3,2,1,0:T(8,128)(2,1)S(1)} %collective-permute-done.12.b0, bf16[2,21,16,384]{3,2,1,0:T(8,128)(2,1)S(1)} %collective-permute-done.13.b1, ...), custom_call_target="tpu_custom_call" | custom-call | tf_op jit(solution)/shard_map/first_conv/pallas_call | solution.py:241
  79.3 2.6 %collective-permute-start.18 = (bf16[6,240,384]{2,1,0:T(8,128)(2,1)S(1)}, bf16[6,240,384]{2,1,0:T(8,128)(2,1)S(1)}, u32[]{:S(2)}, u32[]{:S(2)}) collective-permute-start(bf16[6,240,384]{2,1,0:T(8,128)(2,1)S(1)} %get-tuple-element.46), channel_id=1, source_target_pairs={{1,0},{0,1},{3,2},{2,3},{5,4},{4,5},{7,6},{6,7},{9,8},{8,9},{11,10... | collective-permute-start | bytes 3317768 | tf_op jit(solution)/shard_map/ppermute | solution.py:39
  81.9 2.3 %collective-permute-start.21 = (bf16[2,21,16,384]{3,2,1,0:T(8,128)(2,1)S(1)}, bf16[2,21,16,384]{3,2,1,0:T(8,128)(2,1)S(1)}, u32[]{:S(2)}, u32[]{:S(2)}) collective-permute-start(bf16[2,21,16,384]{3,2,1,0:T(8,128)(2,1)S(1)} %get-tuple-element.41.refs_1_), channel_id=1, source_target_pairs={{16,0},{65,1},{18,2},{67,3},{20,4},{69,5},{22,6},{71,7},{24,8},{73... | collective-permute-start | bytes 1548296 | tf_op jit(solution)/shard_map/ppermute | solution.py:39
  84.2 2.7 %collective-permute-start.19 = (bf16[2,21,16,384]{3,2,1,0:T(8,128)(2,1)S(1)}, bf16[2,21,16,384]{3,2,1,0:T(8,128)(2,1)S(1)}, u32[]{:S(2)}, u32[]{:S(2)}) collective-permute-start(bf16[2,21,16,384]{3,2,1,0:T(8,128)(2,1)S(1)} %collective-permute-done.16.refs_2_), channel_id=1, source_target_pairs={{16,0},{65,1},{18,2},{67,3},{20,4},{69,5},{22,6},{71,7},{24,8},{73... | collective-permute-start | bytes 1548296 | tf_op jit(solution)/shard_map/ppermute | solution.py:39
  86.9 0.0 collective-permute-start.20
  86.9 4.4 %second_layout.1.laid_ref = bf16[6,6,240,256]{3,2,1,0:T(8,128)(2,1)S(1)} custom-call(f32[6,240,384]{2,1,0:T(8,128)S(1)} %get-tuple-element.45.mine_ref, bf16[6,240,384]{2,1,0:T(8,128)(2,1)S(1)} %collective-permute-done.18.other_ref, f32[1,384]{1,0:T(1,128)S(1)} %reshape.11.bias_ref, f32[1,384]{1,0:T(1,128)S(1)} %reshape.12.gain_ref), custom_call_target="tpu_custom_call" | custom-call | tf_op jit(solution)/shard_map/second_layout/pallas_call | solution.py:158
  91.4 2.3 %collective-permute-done.22.refs_4_ = bf16[2,21,16,384]{3,2,1,0:T(8,128)(2,1)S(1)} collective-permute-done((bf16[2,21,16,384]{3,2,1,0:T(8,128)(2,1)S(1)}, bf16[2,21,16,384]{3,2,1,0:T(8,128)(2,1)S(1)}, u32[]{:S(2)}, u32[]{:S(2)}) %collective-permute-start.22) | collective-permute-done | bytes 516128 | tf_op jit(solution)/shard_map/ppermute | solution.py:39
  93.7 4.6 %near_conv.3.near_ref = f32[4,192,384]{2,1,0:T(8,128)S(1)} custom-call(bf16[6,6,240,256]{3,2,1,0:T(8,128)(2,1)S(1)} %second_layout.1.laid_ref, bf16[2,21,16,384]{3,2,1,0:T(8,128)(2,1)S(1)} %get-tuple-element.40.refs_0_, bf16[2,21,16,384]{3,2,1,0:T(8,128)(2,1)S(1)} %get-tuple-element.41.refs_1_, bf16[2,21,16,384]{3,2,1,0:T(8,128)(2,1)S(1)} %collective-permute-done.16.refs_2_, ...), custom_call_target="tpu_custom_call" | custom-call | tf_op jit(solution)/shard_map/near_conv/pallas_call | solution.py:221
  98.3 0.0 copy-start.3
  98.3 0.6 collective-permute-done.20.b1
  98.9 1.8 %second_conv.1 = (f32[4,10,8,384]{3,2,1,0:T(8,128)S(1)}, f32[4,10,8,384]{3,2,1,0:T(8,128)S(1)}) custom-call(bf16[6,6,240,256]{3,2,1,0:T(8,128)(2,1)S(1)} %second_layout.1.laid_ref, bf16[2,21,16,384]{3,2,1,0:T(8,128)(2,1)S(1)} %collective-permute-done.19.b0, bf16[2,21,16,384]{3,2,1,0:T(8,128)(2,1)S(1)} %collective-permute-done.20.b1, ...), custom_call_target="tpu_custom_call" | custom-call | tf_op jit(solution)/shard_map/second_conv/pallas_call | solution.py:270
  100.8 0.1 collective-permute-start.23
  100.9 1.9 %collective-permute-done.23 = f32[4,10,8,384]{3,2,1,0:T(8,128)S(1)} collective-permute-done((f32[4,10,8,384]{3,2,1,0:T(8,128)S(1)}, f32[4,10,8,384]{3,2,1,0:T(8,128)S(1)}, u32[]{:S(2)}, u32[]{:S(2)}) %collective-permute-start.23) | collective-permute-done | bytes 491552 | tf_op jit(solution)/shard_map/ppermute | solution.py:39
  102.7 0.8 fusion.1
  (26 shorter events, 0.1 us)
Async XLA Ops:
  0.0 15.0 %copy-start.2 = (bf16[4,8,10,384]{3,1,2,0:T(8,128)(2,1)S(1)}, bf16[4,8,10,384]{3,1,2,0:T(8,128)(2,1)}, u32[]{:S(2)}) copy-start(bf16[4,8,10,384]{3,1,2,0:T(8,128)(2,1)} %param.7) | copy-start | bytes 737284
  1.1 13.9 %collective-permute-start.2 = (bf16[4,8,10,384]{3,2,1,0:T(8,128)(2,1)S(1)}, bf16[4,8,10,384]{3,2,1,0:T(8,128)(2,1)S(1)}, u32[]{:S(2)}, u32[]{:S(2)}) collective-permute-start(bf16[4,8,10,384]{3,2,1,0:T(8,128)(2,1)S(1)} %copy.10), channel_id=1, source_target_pairs={{0,64},{1,65},{2,66},{3,67},{4,68},{5,69},{6,70},{7,71},{8,72},{9,... | collective-permute-start | bytes 737288 | tf_op jit(solution)/shard_map/ppermute | solution.py:39
  5.1 0.9 copy-start
  6.0 0.9 copy-start.1
  7.3 12.3 %collective-permute-start = (bf16[2,21,8,384]{3,2,1,0:T(8,128)(2,1)S(1)}, bf16[2,21,8,384]{3,2,1,0:T(8,128)(2,1)S(1)}, u32[]{:S(2)}, u32[]{:S(2)}) collective-permute-start(bf16[2,21,8,384]{3,2,1,0:T(8,128)(2,1)S(1)} %fold.1), channel_id=1, source_target_pairs={{0,0},{1,1},{2,2},{3,3},{4,4},{5,5},{6,6},{7,7},{8,8},{9,9},{10,10... | collective-permute-start | bytes 774152 | tf_op jit(solution)/shard_map/ppermute | solution.py:39
  8.0 13.6 %collective-permute-start.1 = (bf16[2,21,8,384]{3,2,1,0:T(8,128)(2,1)S(1)}, bf16[2,21,8,384]{3,2,1,0:T(8,128)(2,1)S(1)}, u32[]{:S(2)}, u32[]{:S(2)}) collective-permute-start(bf16[2,21,8,384]{3,2,1,0:T(8,128)(2,1)S(1)} %fold.1), channel_id=1, source_target_pairs={{8,0},{9,1},{10,2},{11,3},{12,4},{13,5},{14,6},{15,7},{0,8},{1,9},... | collective-permute-start | bytes 774152 | tf_op jit(solution)/shard_map/ppermute | solution.py:39
  15.2 6.5 %collective-permute-start.3 = (bf16[8,2,10,384]{3,2,1,0:T(8,128)(2,1)S(1)}, bf16[8,2,10,384]{3,2,1,0:T(8,128)(2,1)S(1)}, u32[]{:S(2)}, u32[]{:S(2)}) collective-permute-start(bf16[8,2,10,384]{3,2,1,0:T(8,128)(2,1)S(1)} %get-tuple-element.51), channel_id=1, source_target_pairs={{0,16},{1,17},{2,18},{3,19},{4,20},{5,21},{6,22},{7,23},{8,24},{9,... | collective-permute-start | bytes 368648 | tf_op jit(solution)/shard_map/ppermute | solution.py:39
  18.3 6.8 %collective-permute-start.4 = (bf16[8,2,10,384]{3,2,1,0:T(8,128)(2,1)S(1)}, bf16[8,2,10,384]{3,2,1,0:T(8,128)(2,1)S(1)}, u32[]{:S(2)}, u32[]{:S(2)}) collective-permute-start(bf16[8,2,10,384]{3,2,1,0:T(8,128)(2,1)S(1)} %get-tuple-element.52), channel_id=1, source_target_pairs={{16,0},{17,1},{18,2},{19,3},{20,4},{21,5},{22,6},{23,7},{24,8},{25... | collective-permute-start | bytes 368648 | tf_op jit(solution)/shard_map/ppermute | solution.py:39
  25.3 16.9 %collective-permute-start.6 = (bf16[2,21,16,384]{3,2,1,0:T(8,128)(2,1)S(1)}, bf16[2,21,16,384]{3,2,1,0:T(8,128)(2,1)S(1)}, u32[]{:S(2)}, u32[]{:S(2)}) collective-permute-start(bf16[2,21,16,384]{3,2,1,0:T(8,128)(2,1)S(1)} %pad_maximum_fusion.1), channel_id=1, source_target_pairs={{128,0},{33,1},{130,2},{35,3},{132,4},{37,5},{134,6},{39,7},{136,8... | collective-permute-start | bytes 1548296 | tf_op jit(solution)/shard_map/ppermute | solution.py:39
  27.8 14.5 %collective-permute-start.7 = (bf16[2,21,16,384]{3,2,1,0:T(8,128)(2,1)S(1)}, bf16[2,21,16,384]{3,2,1,0:T(8,128)(2,1)S(1)}, u32[]{:S(2)}, u32[]{:S(2)}) collective-permute-start(bf16[2,21,16,384]{3,2,1,0:T(8,128)(2,1)S(1)} %pad_maximum_fusion.1), channel_id=1, source_target_pairs={{192,0},{49,1},{194,2},{51,3},{196,4},{53,5},{198,6},{55,7},{200,8... | collective-permute-start | bytes 1548296 | tf_op jit(solution)/shard_map/ppermute | solution.py:39
  27.8 14.7 %collective-permute-start.5 = (bf16[2,21,16,384]{3,2,1,0:T(8,128)(2,1)S(1)}, bf16[2,21,16,384]{3,2,1,0:T(8,128)(2,1)S(1)}, u32[]{:S(2)}, u32[]{:S(2)}) collective-permute-start(bf16[2,21,16,384]{3,2,1,0:T(8,128)(2,1)S(1)} %pad_maximum_fusion.1), channel_id=1, source_target_pairs={{64,0},{17,1},{66,2},{19,3},{68,4},{21,5},{70,6},{23,7},{72,8},{25... | collective-permute-start | bytes 1548296 | tf_op jit(solution)/shard_map/ppermute | solution.py:39
  30.6 10.8 %collective-permute-start.8 = (bf16[8,12,2,384]{3,2,1,0:T(2,128)(2,1)S(1)}, bf16[8,12,2,384]{3,2,1,0:T(2,128)(2,1)S(1)}, u32[]{:S(2)}, u32[]{:S(2)}) collective-permute-start(bf16[8,12,2,384]{3,2,1,0:T(2,128)(2,1)S(1)} %broadcast_select_fusion), channel_id=1, source_target_pairs={{2,1},{1,2},{4,3},{3,4},{6,5},{5,6},{8,7},{7,8},{10,9},{9,10},{12,... | collective-permute-start | bytes 442376 | tf_op jit(solution)/shard_map/ppermute | solution.py:39
  42.6 8.2 %copy-start.4 = (f32[384]{0:T(512)S(1)}, f32[384]{0:T(512)}, u32[]{:S(2)}) copy-start(f32[384]{0:T(512)} %param.8) | copy-start | bytes 4612
  43.3 7.8 %collective-permute-start.11 = (bf16[8,12,12,384]{3,0,2,1:T(8,128)(2,1)S(1)}, bf16[8,12,12,384]{3,0,2,1:T(8,128)(2,1)S(1)}, u32[]{:S(2)}, u32[]{:S(2)}) collective-permute-start(bf16[8,12,12,384]{3,0,2,1:T(8,128)(2,1)S(1)} %copy.12), channel_id=1, source_target_pairs={{1,0},{0,1},{3,2},{2,3},{5,4},{4,5},{7,6},{6,7},{9,8},{8,9},{11,10... | collective-permute-start | bytes 2654216 | tf_op jit(solution)/shard_map/ppermute | solution.py:39
  47.0 12.0 %collective-permute-start.10 = (bf16[2,21,16,384]{3,2,1,0:T(8,128)(2,1)S(1)}, bf16[2,21,16,384]{3,2,1,0:T(8,128)(2,1)S(1)}, u32[]{:S(2)}, u32[]{:S(2)}) collective-permute-start(bf16[2,21,16,384]{3,2,1,0:T(8,128)(2,1)S(1)} %get-tuple-element.31.refs_1_), channel_id=1, source_target_pairs={{48,0},{193,1},{50,2},{195,3},{52,4},{197,5},{54,6},{199,7},{56,8}... | collective-permute-start | bytes 1548296 | tf_op jit(solution)/shard_map/ppermute | solution.py:39
  47.8 11.1 %collective-permute-start.9 = (bf16[2,21,16,384]{3,2,1,0:T(8,128)(2,1)S(1)}, bf16[2,21,16,384]{3,2,1,0:T(8,128)(2,1)S(1)}, u32[]{:S(2)}, u32[]{:S(2)}) collective-permute-start(bf16[2,21,16,384]{3,2,1,0:T(8,128)(2,1)S(1)} %get-tuple-element.30.refs_0_), channel_id=1, source_target_pairs={{16,0},{65,1},{18,2},{67,3},{20,4},{69,5},{22,6},{71,7},{24,8},{73... | collective-permute-start | bytes 1548296 | tf_op jit(solution)/shard_map/ppermute | solution.py:39
  49.6 14.4 %collective-permute-start.14 = (bf16[2,21,16,384]{3,2,1,0:T(8,128)(2,1)S(1)}, bf16[2,21,16,384]{3,2,1,0:T(8,128)(2,1)S(1)}, u32[]{:S(2)}, u32[]{:S(2)}) collective-permute-start(bf16[2,21,16,384]{3,2,1,0:T(8,128)(2,1)S(1)} %get-tuple-element.31.refs_1_), channel_id=1, source_target_pairs={{16,0},{65,1},{18,2},{67,3},{20,4},{69,5},{22,6},{71,7},{24,8},{73... | collective-permute-start | bytes 1548296 | tf_op jit(solution)/shard_map/ppermute | solution.py:39
  50.8 13.3 %collective-permute-start.15 = (bf16[2,21,16,384]{3,2,1,0:T(8,128)(2,1)S(1)}, bf16[2,21,16,384]{3,2,1,0:T(8,128)(2,1)S(1)}, u32[]{:S(2)}, u32[]{:S(2)}) collective-permute-start(bf16[2,21,16,384]{3,2,1,0:T(8,128)(2,1)S(1)} %get-tuple-element.30.refs_0_), channel_id=1, source_target_pairs={{48,0},{193,1},{50,2},{195,3},{52,4},{197,5},{54,6},{199,7},{56,8}... | collective-permute-start | bytes 1548296 | tf_op jit(solution)/shard_map/ppermute | solution.py:39
  58.9 13.7 %collective-permute-start.12 = (bf16[2,21,16,384]{3,2,1,0:T(8,128)(2,1)S(1)}, bf16[2,21,16,384]{3,2,1,0:T(8,128)(2,1)S(1)}, u32[]{:S(2)}, u32[]{:S(2)}) collective-permute-start(bf16[2,21,16,384]{3,2,1,0:T(8,128)(2,1)S(1)} %collective-permute-done.9.refs_2_), channel_id=1, source_target_pairs={{16,0},{65,1},{18,2},{67,3},{20,4},{69,5},{22,6},{71,7},{24,8},{73... | collective-permute-start | bytes 1548296 | tf_op jit(solution)/shard_map/ppermute | solution.py:39
  61.4 11.2 %collective-permute-start.13 = (bf16[2,21,16,384]{3,2,1,0:T(8,128)(2,1)S(1)}, bf16[2,21,16,384]{3,2,1,0:T(8,128)(2,1)S(1)}, u32[]{:S(2)}, u32[]{:S(2)}) collective-permute-start(bf16[2,21,16,384]{3,2,1,0:T(8,128)(2,1)S(1)} %collective-permute-done.10.refs_5_), channel_id=1, source_target_pairs={{48,0},{193,1},{50,2},{195,3},{52,4},{197,5},{54,6},{199,7},{56,8}... | collective-permute-start | bytes 1548296 | tf_op jit(solution)/shard_map/ppermute | solution.py:39
  61.4 11.6 %collective-permute-start.16 = (bf16[2,21,16,384]{3,2,1,0:T(8,128)(2,1)S(1)}, bf16[2,21,16,384]{3,2,1,0:T(8,128)(2,1)S(1)}, u32[]{:S(2)}, u32[]{:S(2)}) collective-permute-start(bf16[2,21,16,384]{3,2,1,0:T(8,128)(2,1)S(1)} %get-tuple-element.40.refs_0_), channel_id=1, source_target_pairs={{16,0},{65,1},{18,2},{67,3},{20,4},{69,5},{22,6},{71,7},{24,8},{73... | collective-permute-start | bytes 1548296 | tf_op jit(solution)/shard_map/ppermute | solution.py:39
  64.0 12.3 %collective-permute-start.17 = (bf16[2,21,16,384]{3,2,1,0:T(8,128)(2,1)S(1)}, bf16[2,21,16,384]{3,2,1,0:T(8,128)(2,1)S(1)}, u32[]{:S(2)}, u32[]{:S(2)}) collective-permute-start(bf16[2,21,16,384]{3,2,1,0:T(8,128)(2,1)S(1)} %get-tuple-element.41.refs_1_), channel_id=1, source_target_pairs={{48,0},{193,1},{50,2},{195,3},{52,4},{197,5},{54,6},{199,7},{56,8}... | collective-permute-start | bytes 1548296 | tf_op jit(solution)/shard_map/ppermute | solution.py:39
  72.6 14.3 %copy-start.5 = (f32[384]{0:T(512)S(1)}, f32[384]{0:T(512)}, u32[]{:S(2)}) copy-start(f32[384]{0:T(512)} %param.10) | copy-start | bytes 4612
  72.6 14.3 %copy-start.6 = (f32[384]{0:T(512)S(1)}, f32[384]{0:T(512)}, u32[]{:S(2)}) copy-start(f32[384]{0:T(512)} %param.11) | copy-start | bytes 4612
  79.3 7.6 %collective-permute-start.18 = (bf16[6,240,384]{2,1,0:T(8,128)(2,1)S(1)}, bf16[6,240,384]{2,1,0:T(8,128)(2,1)S(1)}, u32[]{:S(2)}, u32[]{:S(2)}) collective-permute-start(bf16[6,240,384]{2,1,0:T(8,128)(2,1)S(1)} %get-tuple-element.46), channel_id=1, source_target_pairs={{1,0},{0,1},{3,2},{2,3},{5,4},{4,5},{7,6},{6,7},{9,8},{8,9},{11,10... | collective-permute-start | bytes 3317768 | tf_op jit(solution)/shard_map/ppermute | solution.py:39
  81.9 9.5 %collective-permute-start.21 = (bf16[2,21,16,384]{3,2,1,0:T(8,128)(2,1)S(1)}, bf16[2,21,16,384]{3,2,1,0:T(8,128)(2,1)S(1)}, u32[]{:S(2)}, u32[]{:S(2)}) collective-permute-start(bf16[2,21,16,384]{3,2,1,0:T(8,128)(2,1)S(1)} %get-tuple-element.41.refs_1_), channel_id=1, source_target_pairs={{16,0},{65,1},{18,2},{67,3},{20,4},{69,5},{22,6},{71,7},{24,8},{73... | collective-permute-start | bytes 1548296 | tf_op jit(solution)/shard_map/ppermute | solution.py:39
  84.2 9.4 %collective-permute-start.22 = (bf16[2,21,16,384]{3,2,1,0:T(8,128)(2,1)S(1)}, bf16[2,21,16,384]{3,2,1,0:T(8,128)(2,1)S(1)}, u32[]{:S(2)}, u32[]{:S(2)}) collective-permute-start(bf16[2,21,16,384]{3,2,1,0:T(8,128)(2,1)S(1)} %get-tuple-element.40.refs_0_), channel_id=1, source_target_pairs={{48,0},{193,1},{50,2},{195,3},{52,4},{197,5},{54,6},{199,7},{56,8}... | collective-permute-start | bytes 1548296 | tf_op jit(solution)/shard_map/ppermute | solution.py:39
  84.2 14.1 %collective-permute-start.19 = (bf16[2,21,16,384]{3,2,1,0:T(8,128)(2,1)S(1)}, bf16[2,21,16,384]{3,2,1,0:T(8,128)(2,1)S(1)}, u32[]{:S(2)}, u32[]{:S(2)}) collective-permute-start(bf16[2,21,16,384]{3,2,1,0:T(8,128)(2,1)S(1)} %collective-permute-done.16.refs_2_), channel_id=1, source_target_pairs={{16,0},{65,1},{18,2},{67,3},{20,4},{69,5},{22,6},{71,7},{24,8},{73... | collective-permute-start | bytes 1548296 | tf_op jit(solution)/shard_map/ppermute | solution.py:39
  86.9 12.0 %collective-permute-start.20 = (bf16[2,21,16,384]{3,2,1,0:T(8,128)(2,1)S(1)}, bf16[2,21,16,384]{3,2,1,0:T(8,128)(2,1)S(1)}, u32[]{:S(2)}, u32[]{:S(2)}) collective-permute-start(bf16[2,21,16,384]{3,2,1,0:T(8,128)(2,1)S(1)} %collective-permute-done.17.refs_5_), channel_id=1, source_target_pairs={{48,0},{193,1},{50,2},{195,3},{52,4},{197,5},{54,6},{199,7},{56,8}... | collective-permute-start | bytes 1548296 | tf_op jit(solution)/shard_map/ppermute | solution.py:39
  98.3 4.4 %copy-start.3 = (f32[384]{0:T(512)S(1)}, f32[384]{0:T(512)}, u32[]{:S(2)}) copy-start(f32[384]{0:T(512)} %param.13) | copy-start | bytes 4612
  100.8 2.0 %collective-permute-start.23 = (f32[4,10,8,384]{3,2,1,0:T(8,128)S(1)}, f32[4,10,8,384]{3,2,1,0:T(8,128)S(1)}, u32[]{:S(2)}, u32[]{:S(2)}) collective-permute-start(f32[4,10,8,384]{3,2,1,0:T(8,128)S(1)} %get-tuple-element.50), channel_id=1, source_target_pairs={{1,0},{0,1},{3,2},{2,3},{5,4},{4,5},{7,6},{6,7},{9,8},{8,9},{11,10... | collective-permute-start | bytes 1474568 | tf_op jit(solution)/shard_map/ppermute | solution.py:39

commit v4 on v3

--- a/solution.py
+++ b/solution.py
@@ -86,10 +86,7 @@
     z_of = (z + shift + 4 * far) & 7
     base = 96 * h_of + 12 * z_of + 6 * c
     chan = lax.broadcasted_iota(jnp.int32, (CHANS, LANES), 0)
-    spread_ref[0] = jnp.where(chan == jnp.where(j < 6, base + j, -1), 1.0, 0.0).astype(BF)
-    for k in range(3):
-        wanted = jnp.where(j >= 6, base + 2 * k + j - 6, -1)
-        spread_ref[k + 1] = jnp.where(chan == wanted, 1.0, 0.0).astype(BF)
+    spread_ref[...] = jnp.where(chan == jnp.where(j < 6, base + j, -1), 1.0, 0.0).astype(BF)
 
 
 def activated(values, gain):
@@ -100,17 +97,16 @@
 
 def lay_out(active, spread_ref, out_ref):
     count = active.shape[0]
-
-    def put(slot, value, matrix):
-        laid = jnp.dot(value, spread_ref[matrix], preferred_element_type=F32)
-        out_ref[slot, 0] = laid.astype(BF)
-
-    put(0, active.astype(BF), 0)
-    one = pltpu.roll(active, count - 1, 0).astype(BF)
-    put(1, one, 0)
+    laid = jnp.dot(active.astype(BF), spread_ref[...], preferred_element_type=F32)
+    one = pltpu.roll(laid, count - 1, 0)
+    out_ref[0, 0] = laid.astype(BF)
+    out_ref[1, 0] = one.astype(BF)
+    out_ref[2, 0] = pltpu.roll(laid, count - 2, 0).astype(BF)
+    last = (lax.broadcasted_iota(jnp.int32, (count, 128), 1) & 7) >= 6
     for k in range(3):
-        put(3 + k, one, 1 + k)
-    put(2, pltpu.roll(active, count - 2, 0).astype(BF), 0)
+        for part in (slice(0, 128), slice(128, 256)):
+            pair = pltpu.roll(one[:, part], 6 - 2 * k, 1)
+            out_ref[3 + k, 0, :, part] = jnp.where(last, pair, 0.0).astype(BF)
 
 
 def first_layout_kernel(x_ref, gain_ref, out_ref, spread_ref):
@@ -132,7 +128,7 @@
             pl.BlockSpec((1, CHANS), lambda f: (0, 0)),
         ],
         out_specs=pl.BlockSpec((6, 1, 12 * 24, LANES), lambda f: (0, f, 0, 0)),
-        scratch_shapes=[pltpu.VMEM((4, CHANS, LANES), BF)],
+        scratch_shapes=[pltpu.VMEM((CHANS, LANES), BF)],
         compiler_params=VMEM,
         name="first_layout",
     )(features, gain)
@@ -166,7 +162,7 @@
             pl.BlockSpec((1, CHANS), lambda f: (0, 0)),
         ],
         out_specs=pl.BlockSpec((6, 1, 10 * 24, LANES), lambda f: (0, f, 0, 0)),
-        scratch_shapes=[pltpu.VMEM((4, CHANS, LANES), BF)],
+        scratch_shapes=[pltpu.VMEM((CHANS, LANES), BF)],
         compiler_params=VMEM,
         name="second_layout",
     )(mine, other, bias, gain)
@@ -360,14 +356,12 @@
         both = jnp.concatenate([z_near(both), z_far(both)], axis=2)
         both, wide = at_once(both, higher(taller(features)))
         one, two = first_ring(both)
-        (one, two), wide = at_once((one, two), wider(wide, core))
+        (one, two), wide = at_once((one, two), joined(wider(wide, core), core))
         ends, rest = second_ring(one), second_ring_rest(one)
-        laid = first_layout(joined(wide, core), gains[0])
-        ends, laid, two = at_once(ends, laid, two)
+        ends, laid, two = at_once(ends, first_layout(wide, gains[0]), two)
         far = passed_on(*ends)
-        rest = at_once(*rest)
         next_ends = second_ring(two)
-        near = near_conv(laid, in_order(one, *ends, *rest), 6, 10 * 24)
+        near = near_conv(laid, in_order(one, *ends, *at_once(*rest)), 6, 10 * 24)
         far, near, next_ends = at_once(far, near, next_ends)
         mine, passed = first_conv(laid, far, near)
         next_rest = second_ring_rest(two)

time: 104 us -> 103 us (level)
  waiting for transfers between devices: 16.9 us -> 22.3 us
  Pallas kernels: 28.9 us -> 25.4 us
  starting transfers between devices: 49.6 us -> 46.6 us
    ppermute x24, waiting for transfers between devices: 16.9 us -> 22.3 us  [move(): return lax.ppermute(x, AXES, pairs)]
    ppermute x24, starting transfers between devices: 49.6 us -> 46.6 us  [move(): return lax.ppermute(x, AXES, pairs)]
    pallas_call x1, Pallas kernels: 6.16 us -> 4.06 us  [first_layout(): pl.pallas_call(first_layout_kernel, grid=(8,), out_shape=jax.ShapeDtypeSt...]
    pallas_call x1, Pallas kernels: 4.42 us -> 3.01 us  [second_layout(): pl.pallas_call(second_layout_kernel, grid=(6,), out_shape=jax.ShapeDtypeS...]
  transfers between devices with their start and end apart: 24 -> 24, of which waited for: 8 -> 13; matrix products, arithmetic and copies ran while one was open for 3% -> 2% of each run, Pallas kernels for 23% -> 20%
where the time goes in v4:
time: 103 us; the launch traced here: 102 us
  starting transfers between devices  46.6 us (45%)
  Pallas kernels  25.4 us (25%)
  waiting for transfers between devices  22.3 us (22%)
  local copies, waits for them, and re-layouts  3.99 us (4%)
  other arithmetic  3.75 us (4%)
    ppermute x24, starting transfers between devices, move(): return lax.ppermute(x, AXES, pairs)  46.6 us
    ppermute x24, waiting for transfers between devices, move(): return lax.ppermute(x, AXES, pairs)  22.3 us
    pallas_call x2, Pallas kernels, near_conv(): pl.pallas_call(functools.partial(near_kernel, frames, count), grid=(frame...  13.1 us
    pallas_call x1, Pallas kernels, first_layout(): pl.pallas_call(first_layout_kernel, grid=(8,), out_shape=jax.ShapeDtypeSt...  4.06 us
    pallas_call x1, Pallas kernels, second_layout(): pl.pallas_call(second_layout_kernel, grid=(6,), out_shape=jax.ShapeDtypeS...  3.01 us
    pallas_call x1, Pallas kernels, first_conv(): pl.pallas_call(first_conv_kernel, grid=(3,), out_shape=(jax.ShapeDtypeStr...  2.98 us
    unnamed x16, local copies, waits for them, and re-layouts  2.95 us
  transfers between devices with their start and end apart: 24, of which 13 were waited for; matrix products, arithmetic and copies ran while one was open for 2% of the time, Pallas kernels for 20%

profile of v4, /device:TPU:1, one launch (start us, length us, event | category | flops | bytes accessed | tf_op | source)
XLA Modules:
  0.0 102.4 jit_solution(6253744325832772812)
XLA Ops:
  0.0 1.1 %copy.10 = bf16[4,8,10,384]{3,2,1,0:T(8,128)(2,1)S(1)} copy(bf16[4,8,10,384]{3,1,2,0:T(8,128)(2,1)} %param.7) | data formatting | bytes 491520 | tf_op args[0]
  1.1 4.1 %collective-permute-start.2 = (bf16[4,8,10,384]{3,2,1,0:T(8,128)(2,1)S(1)}, bf16[4,8,10,384]{3,2,1,0:T(8,128)(2,1)S(1)}, u32[]{:S(2)}, u32[]{:S(2)}) collective-permute-start(bf16[4,8,10,384]{3,2,1,0:T(8,128)(2,1)S(1)} %copy.10), channel_id=1, source_target_pairs={{0,64},{1,65},{2,66},{3,67},{4,68},{5,69},{6,70},{7,71},{8,72},{9,... | collective-permute-start | bytes 737288 | tf_op jit(solution)/shard_map/ppermute | solution.py:39
  5.1 0.0 copy-start
  5.1 0.9 copy-done
  6.1 0.9 copy-done.1
  7.0 0.3 fold.1
  7.3 0.7 collective-permute-start
  8.0 7.0 %collective-permute-start.1 = (bf16[2,21,8,384]{3,2,1,0:T(8,128)(2,1)S(1)}, bf16[2,21,8,384]{3,2,1,0:T(8,128)(2,1)S(1)}, u32[]{:S(2)}, u32[]{:S(2)}) collective-permute-start(bf16[2,21,8,384]{3,2,1,0:T(8,128)(2,1)S(1)} %fold.1), channel_id=1, source_target_pairs={{8,0},{9,1},{10,2},{11,3},{12,4},{13,5},{14,6},{15,7},{0,8},{1,9},... | collective-permute-start | bytes 774152 | tf_op jit(solution)/shard_map/ppermute | solution.py:39
  15.0 0.0 collective-permute-done.2
  15.0 0.1 copy_dynamic-update-slice_fusion
  15.2 3.1 %collective-permute-start.3 = (bf16[8,2,10,384]{3,2,1,0:T(8,128)(2,1)S(1)}, bf16[8,2,10,384]{3,2,1,0:T(8,128)(2,1)S(1)}, u32[]{:S(2)}, u32[]{:S(2)}) collective-permute-start(bf16[8,2,10,384]{3,2,1,0:T(8,128)(2,1)S(1)} %get-tuple-element.51), channel_id=1, source_target_pairs={{0,16},{1,17},{2,18},{3,19},{4,20},{5,21},{6,22},{7,23},{8,24},{9,... | collective-permute-start | bytes 368648 | tf_op jit(solution)/shard_map/ppermute | solution.py:39
  18.3 1.3 %collective-permute-start.4 = (bf16[8,2,10,384]{3,2,1,0:T(8,128)(2,1)S(1)}, bf16[8,2,10,384]{3,2,1,0:T(8,128)(2,1)S(1)}, u32[]{:S(2)}, u32[]{:S(2)}) collective-permute-start(bf16[8,2,10,384]{3,2,1,0:T(8,128)(2,1)S(1)} %get-tuple-element.52), channel_id=1, source_target_pairs={{16,0},{17,1},{18,2},{19,3},{20,4},{21,5},{22,6},{23,7},{24,8},{25... | collective-permute-start | bytes 368648 | tf_op jit(solution)/shard_map/ppermute | solution.py:39
  19.6 0.0 collective-permute-done
  19.6 2.0 %collective-permute-done.1 = bf16[2,21,8,384]{3,2,1,0:T(8,128)(2,1)S(1)} collective-permute-done((bf16[2,21,8,384]{3,2,1,0:T(8,128)(2,1)S(1)}, bf16[2,21,8,384]{3,2,1,0:T(8,128)(2,1)S(1)}, u32[]{:S(2)}, u32[]{:S(2)}) %collective-permute-start.1) | collective-permute-done | bytes 258080 | tf_op jit(solution)/shard_map/ppermute | solution.py:39
  21.6 0.1 pad_maximum_fusion.1
  21.7 3.4 %collective-permute-done.4 = bf16[8,2,10,384]{3,2,1,0:T(8,128)(2,1)S(1)} collective-permute-done((bf16[8,2,10,384]{3,2,1,0:T(8,128)(2,1)S(1)}, bf16[8,2,10,384]{3,2,1,0:T(8,128)(2,1)S(1)}, u32[]{:S(2)}, u32[]{:S(2)}) %collective-permute-start.4) | collective-permute-done | bytes 122912 | tf_op jit(solution)/shard_map/ppermute | solution.py:39
  25.1 0.3 pad_maximum_fusion
  25.3 2.5 %collective-permute-start.6 = (bf16[2,21,16,384]{3,2,1,0:T(8,128)(2,1)S(1)}, bf16[2,21,16,384]{3,2,1,0:T(8,128)(2,1)S(1)}, u32[]{:S(2)}, u32[]{:S(2)}) collective-permute-start(bf16[2,21,16,384]{3,2,1,0:T(8,128)(2,1)S(1)} %pad_maximum_fusion.1), channel_id=1, source_target_pairs={{128,0},{33,1},{130,2},{35,3},{132,4},{37,5},{134,6},{39,7},{136,8... | collective-permute-start | bytes 1548296 | tf_op jit(solution)/shard_map/ppermute | solution.py:39
  27.8 2.7 %collective-permute-start.5 = (bf16[2,21,16,384]{3,2,1,0:T(8,128)(2,1)S(1)}, bf16[2,21,16,384]{3,2,1,0:T(8,128)(2,1)S(1)}, u32[]{:S(2)}, u32[]{:S(2)}) collective-permute-start(bf16[2,21,16,384]{3,2,1,0:T(8,128)(2,1)S(1)} %pad_maximum_fusion.1), channel_id=1, source_target_pairs={{64,0},{17,1},{66,2},{19,3},{68,4},{21,5},{70,6},{23,7},{72,8},{25... | collective-permute-start | bytes 1548296 | tf_op jit(solution)/shard_map/ppermute | solution.py:39
  30.5 0.1 broadcast_select_fusion
  30.6 7.6 %collective-permute-start.8 = (bf16[8,12,2,384]{3,2,1,0:T(2,128)(2,1)S(1)}, bf16[8,12,2,384]{3,2,1,0:T(2,128)(2,1)S(1)}, u32[]{:S(2)}, u32[]{:S(2)}) collective-permute-start(bf16[8,12,2,384]{3,2,1,0:T(2,128)(2,1)S(1)} %broadcast_select_fusion), channel_id=1, source_target_pairs={{2,1},{1,2},{4,3},{3,4},{6,5},{5,6},{8,7},{7,8},{10,9},{9,10},{12,... | collective-permute-start | bytes 442376 | tf_op jit(solution)/shard_map/ppermute | solution.py:39
  38.3 0.1 fusion.5
  38.4 3.0 %collective-permute-done.8 = bf16[8,12,2,384]{3,2,1,0:T(2,128)(2,1)S(1)} collective-permute-done((bf16[8,12,2,384]{3,2,1,0:T(2,128)(2,1)S(1)}, bf16[8,12,2,384]{3,2,1,0:T(2,128)(2,1)S(1)}, u32[]{:S(2)}, u32[]{:S(2)}) %collective-permute-start.8) | collective-permute-done | bytes 147488 | tf_op jit(solution)/shard_map/ppermute | solution.py:39
  41.4 0.8 maximum_select_fusion.1
  42.2 0.5 copy.12
  42.8 0.1 collective-permute-start.9
  42.9 0.1 fusion.3
  42.9 0.1 fusion.4
  43.0 0.1 pad_maximum_fusion.3
  43.2 0.1 fusion.6
  43.2 0.1 pad_maximum_fusion.2
  43.4 1.9 %collective-permute-done.9 = bf16[8,12,12,384]{3,0,2,1:T(8,128)(2,1)S(1)} collective-permute-done((bf16[8,12,12,384]{3,0,2,1:T(8,128)(2,1)S(1)}, bf16[8,12,12,384]{3,0,2,1:T(8,128)(2,1)S(1)}, u32[]{:S(2)}, u32[]{:S(2)}) %collective-permute-start.9) | collective-permute-done | bytes 884768 | tf_op jit(solution)/shard_map/ppermute | solution.py:39
  45.3 0.2 copy.13
  45.5 0.0 copy-start.4
  45.5 1.4 %maximum_select_fusion.x_ref = bf16[8,12,24,384]{3,2,1,0:T(8,128)(2,1)S(1)} fusion(bf16[8,12,12,384]{3,2,1,0:T(8,128)(2,1)S(1)} %copy.13, bf16[8,12,12,384]{3,2,1,0:T(8,128)(2,1)S(1)} %maximum_select_fusion.1, pred[]{:T(512)S(6)} %eq.2), kind=kLoop, calls=%fused_computation | loop fusion | flops 7962624 | bytes 3538945 | tf_op jit(solution)/shard_map/jit(_where)/select_n | solution.py:343
  46.9 0.1 collective-permute-start.10
  47.0 1.5 %collective-permute-start.11 = (bf16[2,21,16,384]{3,2,1,0:T(8,128)(2,1)S(1)}, bf16[2,21,16,384]{3,2,1,0:T(8,128)(2,1)S(1)}, u32[]{:S(2)}, u32[]{:S(2)}) collective-permute-start(bf16[2,21,16,384]{3,2,1,0:T(8,128)(2,1)S(1)} %get-tuple-element.31.refs_1_), channel_id=1, source_target_pairs={{48,0},{193,1},{50,2},{195,3},{52,4},{197,5},{54,6},{199,7},{56,8}... | collective-permute-start | bytes 1548296 | tf_op jit(solution)/shard_map/ppermute | solution.py:39
  48.5 1.6 %collective-permute-start.14 = (bf16[2,21,16,384]{3,2,1,0:T(8,128)(2,1)S(1)}, bf16[2,21,16,384]{3,2,1,0:T(8,128)(2,1)S(1)}, u32[]{:S(2)}, u32[]{:S(2)}) collective-permute-start(bf16[2,21,16,384]{3,2,1,0:T(8,128)(2,1)S(1)} %get-tuple-element.31.refs_1_), channel_id=1, source_target_pairs={{16,0},{65,1},{18,2},{67,3},{20,4},{69,5},{22,6},{71,7},{24,8},{73... | collective-permute-start | bytes 1548296 | tf_op jit(solution)/shard_map/ppermute | solution.py:39
  50.0 4.1 %first_layout.1.laid_ref = bf16[6,8,288,256]{3,2,1,0:T(8,128)(2,1)S(1)} custom-call(bf16[8,12,24,384]{3,2,1,0:T(8,128)(2,1)S(1)} %maximum_select_fusion.x_ref, f32[1,384]{1,0:T(1,128)S(1)} %reshape.10.gain_ref), custom_call_target="tpu_custom_call" | custom-call | tf_op jit(solution)/shard_map/first_layout/pallas_call | solution.py:122
  54.1 1.1 %collective-permute-done.10.refs_2_ = bf16[2,21,16,384]{3,2,1,0:T(8,128)(2,1)S(1)} collective-permute-done((bf16[2,21,16,384]{3,2,1,0:T(8,128)(2,1)S(1)}, bf16[2,21,16,384]{3,2,1,0:T(8,128)(2,1)S(1)}, u32[]{:S(2)}, u32[]{:S(2)}) %collective-permute-start.10) | collective-permute-done | bytes 516128 | tf_op jit(solution)/shard_map/ppermute | solution.py:39
  55.2 1.6 %collective-permute-done.11.refs_5_ = bf16[2,21,16,384]{3,2,1,0:T(8,128)(2,1)S(1)} collective-permute-done((bf16[2,21,16,384]{3,2,1,0:T(8,128)(2,1)S(1)}, bf16[2,21,16,384]{3,2,1,0:T(8,128)(2,1)S(1)}, u32[]{:S(2)}, u32[]{:S(2)}) %collective-permute-start.11) | collective-permute-done | bytes 516128 | tf_op jit(solution)/shard_map/ppermute | solution.py:39
  56.8 1.5 %collective-permute-start.12 = (bf16[2,21,16,384]{3,2,1,0:T(8,128)(2,1)S(1)}, bf16[2,21,16,384]{3,2,1,0:T(8,128)(2,1)S(1)}, u32[]{:S(2)}, u32[]{:S(2)}) collective-permute-start(bf16[2,21,16,384]{3,2,1,0:T(8,128)(2,1)S(1)} %collective-permute-done.10.refs_2_), channel_id=1, source_target_pairs={{16,0},{65,1},{18,2},{67,3},{20,4},{69,5},{22,6},{71,7},{24,8},{73... | collective-permute-start | bytes 1548296 | tf_op jit(solution)/shard_map/ppermute | solution.py:39
  58.3 2.7 %collective-permute-start.16 = (bf16[2,21,16,384]{3,2,1,0:T(8,128)(2,1)S(1)}, bf16[2,21,16,384]{3,2,1,0:T(8,128)(2,1)S(1)}, u32[]{:S(2)}, u32[]{:S(2)}) collective-permute-start(bf16[2,21,16,384]{3,2,1,0:T(8,128)(2,1)S(1)} %get-tuple-element.40.refs_0_), channel_id=1, source_target_pairs={{16,0},{65,1},{18,2},{67,3},{20,4},{69,5},{22,6},{71,7},{24,8},{73... | collective-permute-start | bytes 1548296 | tf_op jit(solution)/shard_map/ppermute | solution.py:39
  60.9 0.8 collective-permute-start.17
  61.7 0.6 collective-permute-done.15.refs_4_
  62.3 8.5 %near_conv.2.near_ref = f32[6,240,384]{2,1,0:T(8,128)S(1)} custom-call(bf16[6,8,288,256]{3,2,1,0:T(8,128)(2,1)S(1)} %first_layout.1.laid_ref, bf16[2,21,16,384]{3,2,1,0:T(8,128)(2,1)S(1)} %get-tuple-element.30.refs_0_, bf16[2,21,16,384]{3,2,1,0:T(8,128)(2,1)S(1)} %get-tuple-element.31.refs_1_, bf16[2,21,16,384]{3,2,1,0:T(8,128)(2,1)S(1)} %collective-permute-done.10.refs_2_, ...), custom_call_target="tpu_custom_call" | custom-call | tf_op jit(solution)/shard_map/near_conv/pallas_call | solution.py:217
  70.9 0.0 copy-start.5
  70.9 0.0 copy-start.6
  70.9 0.9 collective-permute-done.16.refs_2_
  71.8 1.6 %collective-permute-done.17.refs_5_ = bf16[2,21,16,384]{3,2,1,0:T(8,128)(2,1)S(1)} collective-permute-done((bf16[2,21,16,384]{3,2,1,0:T(8,128)(2,1)S(1)}, bf16[2,21,16,384]{3,2,1,0:T(8,128)(2,1)S(1)}, u32[]{:S(2)}, u32[]{:S(2)}) %collective-permute-start.17) | collective-permute-done | bytes 516128 | tf_op jit(solution)/shard_map/ppermute | solution.py:39
  73.4 3.0 %first_conv.1 = (f32[6,240,384]{2,1,0:T(8,128)S(1)}, bf16[6,240,384]{2,1,0:T(8,128)(2,1)S(1)}) custom-call(bf16[6,8,288,256]{3,2,1,0:T(8,128)(2,1)S(1)} %first_layout.1.laid_ref, bf16[2,21,16,384]{3,2,1,0:T(8,128)(2,1)S(1)} %collective-permute-done.12.b0, bf16[2,21,16,384]{3,2,1,0:T(8,128)(2,1)S(1)} %collective-permute-done.13.b1, ...), custom_call_target="tpu_custom_call" | custom-call | tf_op jit(solution)/shard_map/first_conv/pallas_call | solution.py:237
  76.4 4.4 %collective-permute-start.18 = (bf16[6,240,384]{2,1,0:T(8,128)(2,1)S(1)}, bf16[6,240,384]{2,1,0:T(8,128)(2,1)S(1)}, u32[]{:S(2)}, u32[]{:S(2)}) collective-permute-start(bf16[6,240,384]{2,1,0:T(8,128)(2,1)S(1)} %get-tuple-element.46), channel_id=1, source_target_pairs={{1,0},{0,1},{3,2},{2,3},{5,4},{4,5},{7,6},{6,7},{9,8},{8,9},{11,10... | collective-permute-start | bytes 3317768 | tf_op jit(solution)/shard_map/ppermute | solution.py:39
  80.8 2.4 %collective-permute-start.21 = (bf16[2,21,16,384]{3,2,1,0:T(8,128)(2,1)S(1)}, bf16[2,21,16,384]{3,2,1,0:T(8,128)(2,1)S(1)}, u32[]{:S(2)}, u32[]{:S(2)}) collective-permute-start(bf16[2,21,16,384]{3,2,1,0:T(8,128)(2,1)S(1)} %get-tuple-element.41.refs_1_), channel_id=1, source_target_pairs={{16,0},{65,1},{18,2},{67,3},{20,4},{69,5},{22,6},{71,7},{24,8},{73... | collective-permute-start | bytes 1548296 | tf_op jit(solution)/shard_map/ppermute | solution.py:39
  83.1 2.7 %collective-permute-start.19 = (bf16[2,21,16,384]{3,2,1,0:T(8,128)(2,1)S(1)}, bf16[2,21,16,384]{3,2,1,0:T(8,128)(2,1)S(1)}, u32[]{:S(2)}, u32[]{:S(2)}) collective-permute-start(bf16[2,21,16,384]{3,2,1,0:T(8,128)(2,1)S(1)} %collective-permute-done.16.refs_2_), channel_id=1, source_target_pairs={{16,0},{65,1},{18,2},{67,3},{20,4},{69,5},{22,6},{71,7},{24,8},{73... | collective-permute-start | bytes 1548296 | tf_op jit(solution)/shard_map/ppermute | solution.py:39
  85.9 3.0 %second_layout.1.laid_ref = bf16[6,6,240,256]{3,2,1,0:T(8,128)(2,1)S(1)} custom-call(f32[6,240,384]{2,1,0:T(8,128)S(1)} %get-tuple-element.45.mine_ref, bf16[6,240,384]{2,1,0:T(8,128)(2,1)S(1)} %collective-permute-done.18.other_ref, f32[1,384]{1,0:T(1,128)S(1)} %reshape.11.bias_ref, f32[1,384]{1,0:T(1,128)S(1)} %reshape.12.gain_ref), custom_call_target="tpu_custom_call" | custom-call | tf_op jit(solution)/shard_map/second_layout/pallas_call | solution.py:154
  88.9 0.3 collective-permute-done.21.refs_3_
  89.2 3.4 %collective-permute-done.22.refs_4_ = bf16[2,21,16,384]{3,2,1,0:T(8,128)(2,1)S(1)} collective-permute-done((bf16[2,21,16,384]{3,2,1,0:T(8,128)(2,1)S(1)}, bf16[2,21,16,384]{3,2,1,0:T(8,128)(2,1)S(1)}, u32[]{:S(2)}, u32[]{:S(2)}) %collective-permute-start.22) | collective-permute-done | bytes 516128 | tf_op jit(solution)/shard_map/ppermute | solution.py:39
  92.6 4.6 %near_conv.3.near_ref = f32[4,192,384]{2,1,0:T(8,128)S(1)} custom-call(bf16[6,6,240,256]{3,2,1,0:T(8,128)(2,1)S(1)} %second_layout.1.laid_ref, bf16[2,21,16,384]{3,2,1,0:T(8,128)(2,1)S(1)} %get-tuple-element.40.refs_0_, bf16[2,21,16,384]{3,2,1,0:T(8,128)(2,1)S(1)} %get-tuple-element.41.refs_1_, bf16[2,21,16,384]{3,2,1,0:T(8,128)(2,1)S(1)} %collective-permute-done.16.refs_2_, ...), custom_call_target="tpu_custom_call" | custom-call | tf_op jit(solution)/shard_map/near_conv/pallas_call | solution.py:217
  97.2 0.0 copy-start.3
  97.2 0.6 collective-permute-done.20.b1
  97.8 1.8 %second_conv.1 = (f32[4,10,8,384]{3,2,1,0:T(8,128)S(1)}, f32[4,10,8,384]{3,2,1,0:T(8,128)S(1)}) custom-call(bf16[6,6,240,256]{3,2,1,0:T(8,128)(2,1)S(1)} %second_layout.1.laid_ref, bf16[2,21,16,384]{3,2,1,0:T(8,128)(2,1)S(1)} %collective-permute-done.19.b0, bf16[2,21,16,384]{3,2,1,0:T(8,128)(2,1)S(1)} %collective-permute-done.20.b1, ...), custom_call_target="tpu_custom_call" | custom-call | tf_op jit(solution)/shard_map/second_conv/pallas_call | solution.py:266
  99.7 0.1 collective-permute-start.23
  99.8 1.9 %collective-permute-done.23 = f32[4,10,8,384]{3,2,1,0:T(8,128)S(1)} collective-permute-done((f32[4,10,8,384]{3,2,1,0:T(8,128)S(1)}, f32[4,10,8,384]{3,2,1,0:T(8,128)S(1)}, u32[]{:S(2)}, u32[]{:S(2)}) %collective-permute-start.23) | collective-permute-done | bytes 491552 | tf_op jit(solution)/shard_map/ppermute | solution.py:39
  101.6 0.8 fusion.1
  (26 shorter events, 0.1 us)
Async XLA Ops:
  0.0 15.0 %copy-start.2 = (bf16[4,8,10,384]{3,1,2,0:T(8,128)(2,1)S(1)}, bf16[4,8,10,384]{3,1,2,0:T(8,128)(2,1)}, u32[]{:S(2)}) copy-start(bf16[4,8,10,384]{3,1,2,0:T(8,128)(2,1)} %param.7) | copy-start | bytes 737284
  1.1 13.9 %collective-permute-start.2 = (bf16[4,8,10,384]{3,2,1,0:T(8,128)(2,1)S(1)}, bf16[4,8,10,384]{3,2,1,0:T(8,128)(2,1)S(1)}, u32[]{:S(2)}, u32[]{:S(2)}) collective-permute-start(bf16[4,8,10,384]{3,2,1,0:T(8,128)(2,1)S(1)} %copy.10), channel_id=1, source_target_pairs={{0,64},{1,65},{2,66},{3,67},{4,68},{5,69},{6,70},{7,71},{8,72},{9,... | collective-permute-start | bytes 737288 | tf_op jit(solution)/shard_map/ppermute | solution.py:39
  5.1 0.9 copy-start
  6.0 0.9 copy-start.1
  7.3 12.3 %collective-permute-start = (bf16[2,21,8,384]{3,2,1,0:T(8,128)(2,1)S(1)}, bf16[2,21,8,384]{3,2,1,0:T(8,128)(2,1)S(1)}, u32[]{:S(2)}, u32[]{:S(2)}) collective-permute-start(bf16[2,21,8,384]{3,2,1,0:T(8,128)(2,1)S(1)} %fold.1), channel_id=1, source_target_pairs={{0,0},{1,1},{2,2},{3,3},{4,4},{5,5},{6,6},{7,7},{8,8},{9,9},{10,10... | collective-permute-start | bytes 774152 | tf_op jit(solution)/shard_map/ppermute | solution.py:39
  8.0 13.6 %collective-permute-start.1 = (bf16[2,21,8,384]{3,2,1,0:T(8,128)(2,1)S(1)}, bf16[2,21,8,384]{3,2,1,0:T(8,128)(2,1)S(1)}, u32[]{:S(2)}, u32[]{:S(2)}) collective-permute-start(bf16[2,21,8,384]{3,2,1,0:T(8,128)(2,1)S(1)} %fold.1), channel_id=1, source_target_pairs={{8,0},{9,1},{10,2},{11,3},{12,4},{13,5},{14,6},{15,7},{0,8},{1,9},... | collective-permute-start | bytes 774152 | tf_op jit(solution)/shard_map/ppermute | solution.py:39
  15.2 6.5 %collective-permute-start.3 = (bf16[8,2,10,384]{3,2,1,0:T(8,128)(2,1)S(1)}, bf16[8,2,10,384]{3,2,1,0:T(8,128)(2,1)S(1)}, u32[]{:S(2)}, u32[]{:S(2)}) collective-permute-start(bf16[8,2,10,384]{3,2,1,0:T(8,128)(2,1)S(1)} %get-tuple-element.51), channel_id=1, source_target_pairs={{0,16},{1,17},{2,18},{3,19},{4,20},{5,21},{6,22},{7,23},{8,24},{9,... | collective-permute-start | bytes 368648 | tf_op jit(solution)/shard_map/ppermute | solution.py:39
  18.3 6.8 %collective-permute-start.4 = (bf16[8,2,10,384]{3,2,1,0:T(8,128)(2,1)S(1)}, bf16[8,2,10,384]{3,2,1,0:T(8,128)(2,1)S(1)}, u32[]{:S(2)}, u32[]{:S(2)}) collective-permute-start(bf16[8,2,10,384]{3,2,1,0:T(8,128)(2,1)S(1)} %get-tuple-element.52), channel_id=1, source_target_pairs={{16,0},{17,1},{18,2},{19,3},{20,4},{21,5},{22,6},{23,7},{24,8},{25... | collective-permute-start | bytes 368648 | tf_op jit(solution)/shard_map/ppermute | solution.py:39
  25.3 17.5 %collective-permute-start.6 = (bf16[2,21,16,384]{3,2,1,0:T(8,128)(2,1)S(1)}, bf16[2,21,16,384]{3,2,1,0:T(8,128)(2,1)S(1)}, u32[]{:S(2)}, u32[]{:S(2)}) collective-permute-start(bf16[2,21,16,384]{3,2,1,0:T(8,128)(2,1)S(1)} %pad_maximum_fusion.1), channel_id=1, source_target_pairs={{128,0},{33,1},{130,2},{35,3},{132,4},{37,5},{134,6},{39,7},{136,8... | collective-permute-start | bytes 1548296 | tf_op jit(solution)/shard_map/ppermute | solution.py:39
  27.8 15.1 %collective-permute-start.7 = (bf16[2,21,16,384]{3,2,1,0:T(8,128)(2,1)S(1)}, bf16[2,21,16,384]{3,2,1,0:T(8,128)(2,1)S(1)}, u32[]{:S(2)}, u32[]{:S(2)}) collective-permute-start(bf16[2,21,16,384]{3,2,1,0:T(8,128)(2,1)S(1)} %pad_maximum_fusion.1), channel_id=1, source_target_pairs={{192,0},{49,1},{194,2},{51,3},{196,4},{53,5},{198,6},{55,7},{200,8... | collective-permute-start | bytes 1548296 | tf_op jit(solution)/shard_map/ppermute | solution.py:39
  27.8 15.3 %collective-permute-start.5 = (bf16[2,21,16,384]{3,2,1,0:T(8,128)(2,1)S(1)}, bf16[2,21,16,384]{3,2,1,0:T(8,128)(2,1)S(1)}, u32[]{:S(2)}, u32[]{:S(2)}) collective-permute-start(bf16[2,21,16,384]{3,2,1,0:T(8,128)(2,1)S(1)} %pad_maximum_fusion.1), channel_id=1, source_target_pairs={{64,0},{17,1},{66,2},{19,3},{68,4},{21,5},{70,6},{23,7},{72,8},{25... | collective-permute-start | bytes 1548296 | tf_op jit(solution)/shard_map/ppermute | solution.py:39
  30.6 10.8 %collective-permute-start.8 = (bf16[8,12,2,384]{3,2,1,0:T(2,128)(2,1)S(1)}, bf16[8,12,2,384]{3,2,1,0:T(2,128)(2,1)S(1)}, u32[]{:S(2)}, u32[]{:S(2)}) collective-permute-start(bf16[8,12,2,384]{3,2,1,0:T(2,128)(2,1)S(1)} %broadcast_select_fusion), channel_id=1, source_target_pairs={{2,1},{1,2},{4,3},{3,4},{6,5},{5,6},{8,7},{7,8},{10,9},{9,10},{12,... | collective-permute-start | bytes 442376 | tf_op jit(solution)/shard_map/ppermute | solution.py:39
  42.8 2.5 %collective-permute-start.9 = (bf16[8,12,12,384]{3,0,2,1:T(8,128)(2,1)S(1)}, bf16[8,12,12,384]{3,0,2,1:T(8,128)(2,1)S(1)}, u32[]{:S(2)}, u32[]{:S(2)}) collective-permute-start(bf16[8,12,12,384]{3,0,2,1:T(8,128)(2,1)S(1)} %copy.12), channel_id=1, source_target_pairs={{1,0},{0,1},{3,2},{2,3},{5,4},{4,5},{7,6},{6,7},{9,8},{8,9},{11,10... | collective-permute-start | bytes 2654216 | tf_op jit(solution)/shard_map/ppermute | solution.py:39
  45.5 4.6 %copy-start.4 = (f32[384]{0:T(512)S(1)}, f32[384]{0:T(512)}, u32[]{:S(2)}) copy-start(f32[384]{0:T(512)} %param.8) | copy-start | bytes 4612
  46.9 8.3 %collective-permute-start.10 = (bf16[2,21,16,384]{3,2,1,0:T(8,128)(2,1)S(1)}, bf16[2,21,16,384]{3,2,1,0:T(8,128)(2,1)S(1)}, u32[]{:S(2)}, u32[]{:S(2)}) collective-permute-start(bf16[2,21,16,384]{3,2,1,0:T(8,128)(2,1)S(1)} %get-tuple-element.30.refs_0_), channel_id=1, source_target_pairs={{16,0},{65,1},{18,2},{67,3},{20,4},{69,5},{22,6},{71,7},{24,8},{73... | collective-permute-start | bytes 1548296 | tf_op jit(solution)/shard_map/ppermute | solution.py:39
  47.0 9.8 %collective-permute-start.11 = (bf16[2,21,16,384]{3,2,1,0:T(8,128)(2,1)S(1)}, bf16[2,21,16,384]{3,2,1,0:T(8,128)(2,1)S(1)}, u32[]{:S(2)}, u32[]{:S(2)}) collective-permute-start(bf16[2,21,16,384]{3,2,1,0:T(8,128)(2,1)S(1)} %get-tuple-element.31.refs_1_), channel_id=1, source_target_pairs={{48,0},{193,1},{50,2},{195,3},{52,4},{197,5},{54,6},{199,7},{56,8}... | collective-permute-start | bytes 1548296 | tf_op jit(solution)/shard_map/ppermute | solution.py:39
  48.5 12.5 %collective-permute-start.14 = (bf16[2,21,16,384]{3,2,1,0:T(8,128)(2,1)S(1)}, bf16[2,21,16,384]{3,2,1,0:T(8,128)(2,1)S(1)}, u32[]{:S(2)}, u32[]{:S(2)}) collective-permute-start(bf16[2,21,16,384]{3,2,1,0:T(8,128)(2,1)S(1)} %get-tuple-element.31.refs_1_), channel_id=1, source_target_pairs={{16,0},{65,1},{18,2},{67,3},{20,4},{69,5},{22,6},{71,7},{24,8},{73... | collective-permute-start | bytes 1548296 | tf_op jit(solution)/shard_map/ppermute | solution.py:39
  50.0 12.3 %collective-permute-start.15 = (bf16[2,21,16,384]{3,2,1,0:T(8,128)(2,1)S(1)}, bf16[2,21,16,384]{3,2,1,0:T(8,128)(2,1)S(1)}, u32[]{:S(2)}, u32[]{:S(2)}) collective-permute-start(bf16[2,21,16,384]{3,2,1,0:T(8,128)(2,1)S(1)} %get-tuple-element.30.refs_0_), channel_id=1, source_target_pairs={{48,0},{193,1},{50,2},{195,3},{52,4},{197,5},{54,6},{199,7},{56,8}... | collective-permute-start | bytes 1548296 | tf_op jit(solution)/shard_map/ppermute | solution.py:39
  56.8 14.1 %collective-permute-start.12 = (bf16[2,21,16,384]{3,2,1,0:T(8,128)(2,1)S(1)}, bf16[2,21,16,384]{3,2,1,0:T(8,128)(2,1)S(1)}, u32[]{:S(2)}, u32[]{:S(2)}) collective-permute-start(bf16[2,21,16,384]{3,2,1,0:T(8,128)(2,1)S(1)} %collective-permute-done.10.refs_2_), channel_id=1, source_target_pairs={{16,0},{65,1},{18,2},{67,3},{20,4},{69,5},{22,6},{71,7},{24,8},{73... | collective-permute-start | bytes 1548296 | tf_op jit(solution)/shard_map/ppermute | solution.py:39
  58.3 12.6 %collective-permute-start.13 = (bf16[2,21,16,384]{3,2,1,0:T(8,128)(2,1)S(1)}, bf16[2,21,16,384]{3,2,1,0:T(8,128)(2,1)S(1)}, u32[]{:S(2)}, u32[]{:S(2)}) collective-permute-start(bf16[2,21,16,384]{3,2,1,0:T(8,128)(2,1)S(1)} %collective-permute-done.11.refs_5_), channel_id=1, source_target_pairs={{48,0},{193,1},{50,2},{195,3},{52,4},{197,5},{54,6},{199,7},{56,8}... | collective-permute-start | bytes 1548296 | tf_op jit(solution)/shard_map/ppermute | solution.py:39
  58.3 13.6 %collective-permute-start.16 = (bf16[2,21,16,384]{3,2,1,0:T(8,128)(2,1)S(1)}, bf16[2,21,16,384]{3,2,1,0:T(8,128)(2,1)S(1)}, u32[]{:S(2)}, u32[]{:S(2)}) collective-permute-start(bf16[2,21,16,384]{3,2,1,0:T(8,128)(2,1)S(1)} %get-tuple-element.40.refs_0_), channel_id=1, source_target_pairs={{16,0},{65,1},{18,2},{67,3},{20,4},{69,5},{22,6},{71,7},{24,8},{73... | collective-permute-start | bytes 1548296 | tf_op jit(solution)/shard_map/ppermute | solution.py:39
  60.9 12.4 %collective-permute-start.17 = (bf16[2,21,16,384]{3,2,1,0:T(8,128)(2,1)S(1)}, bf16[2,21,16,384]{3,2,1,0:T(8,128)(2,1)S(1)}, u32[]{:S(2)}, u32[]{:S(2)}) collective-permute-start(bf16[2,21,16,384]{3,2,1,0:T(8,128)(2,1)S(1)} %get-tuple-element.41.refs_1_), channel_id=1, source_target_pairs={{48,0},{193,1},{50,2},{195,3},{52,4},{197,5},{54,6},{199,7},{56,8}... | collective-permute-start | bytes 1548296 | tf_op jit(solution)/shard_map/ppermute | solution.py:39
  70.9 15.0 %copy-start.5 = (f32[384]{0:T(512)S(1)}, f32[384]{0:T(512)}, u32[]{:S(2)}) copy-start(f32[384]{0:T(512)} %param.10) | copy-start | bytes 4612
  70.9 15.0 %copy-start.6 = (f32[384]{0:T(512)S(1)}, f32[384]{0:T(512)}, u32[]{:S(2)}) copy-start(f32[384]{0:T(512)} %param.11) | copy-start | bytes 4612
  76.4 9.5 %collective-permute-start.18 = (bf16[6,240,384]{2,1,0:T(8,128)(2,1)S(1)}, bf16[6,240,384]{2,1,0:T(8,128)(2,1)S(1)}, u32[]{:S(2)}, u32[]{:S(2)}) collective-permute-start(bf16[6,240,384]{2,1,0:T(8,128)(2,1)S(1)} %get-tuple-element.46), channel_id=1, source_target_pairs={{1,0},{0,1},{3,2},{2,3},{5,4},{4,5},{7,6},{6,7},{9,8},{8,9},{11,10... | collective-permute-start | bytes 3317768 | tf_op jit(solution)/shard_map/ppermute | solution.py:39
  80.8 8.4 %collective-permute-start.21 = (bf16[2,21,16,384]{3,2,1,0:T(8,128)(2,1)S(1)}, bf16[2,21,16,384]{3,2,1,0:T(8,128)(2,1)S(1)}, u32[]{:S(2)}, u32[]{:S(2)}) collective-permute-start(bf16[2,21,16,384]{3,2,1,0:T(8,128)(2,1)S(1)} %get-tuple-element.41.refs_1_), channel_id=1, source_target_pairs={{16,0},{65,1},{18,2},{67,3},{20,4},{69,5},{22,6},{71,7},{24,8},{73... | collective-permute-start | bytes 1548296 | tf_op jit(solution)/shard_map/ppermute | solution.py:39
  83.1 9.4 %collective-permute-start.22 = (bf16[2,21,16,384]{3,2,1,0:T(8,128)(2,1)S(1)}, bf16[2,21,16,384]{3,2,1,0:T(8,128)(2,1)S(1)}, u32[]{:S(2)}, u32[]{:S(2)}) collective-permute-start(bf16[2,21,16,384]{3,2,1,0:T(8,128)(2,1)S(1)} %get-tuple-element.40.refs_0_), channel_id=1, source_target_pairs={{48,0},{193,1},{50,2},{195,3},{52,4},{197,5},{54,6},{199,7},{56,8}... | collective-permute-start | bytes 1548296 | tf_op jit(solution)/shard_map/ppermute | solution.py:39
  83.1 14.1 %collective-permute-start.19 = (bf16[2,21,16,384]{3,2,1,0:T(8,128)(2,1)S(1)}, bf16[2,21,16,384]{3,2,1,0:T(8,128)(2,1)S(1)}, u32[]{:S(2)}, u32[]{:S(2)}) collective-permute-start(bf16[2,21,16,384]{3,2,1,0:T(8,128)(2,1)S(1)} %collective-permute-done.16.refs_2_), channel_id=1, source_target_pairs={{16,0},{65,1},{18,2},{67,3},{20,4},{69,5},{22,6},{71,7},{24,8},{73... | collective-permute-start | bytes 1548296 | tf_op jit(solution)/shard_map/ppermute | solution.py:39
  85.8 12.0 %collective-permute-start.20 = (bf16[2,21,16,384]{3,2,1,0:T(8,128)(2,1)S(1)}, bf16[2,21,16,384]{3,2,1,0:T(8,128)(2,1)S(1)}, u32[]{:S(2)}, u32[]{:S(2)}) collective-permute-start(bf16[2,21,16,384]{3,2,1,0:T(8,128)(2,1)S(1)} %collective-permute-done.17.refs_5_), channel_id=1, source_target_pairs={{48,0},{193,1},{50,2},{195,3},{52,4},{197,5},{54,6},{199,7},{56,8}... | collective-permute-start | bytes 1548296 | tf_op jit(solution)/shard_map/ppermute | solution.py:39
  97.2 4.4 %copy-start.3 = (f32[384]{0:T(512)S(1)}, f32[384]{0:T(512)}, u32[]{:S(2)}) copy-start(f32[384]{0:T(512)} %param.13) | copy-start | bytes 4612
  99.7 2.0 %collective-permute-start.23 = (f32[4,10,8,384]{3,2,1,0:T(8,128)S(1)}, f32[4,10,8,384]{3,2,1,0:T(8,128)S(1)}, u32[]{:S(2)}, u32[]{:S(2)}) collective-permute-start(f32[4,10,8,384]{3,2,1,0:T(8,128)S(1)} %get-tuple-element.50), channel_id=1, source_target_pairs={{1,0},{0,1},{3,2},{2,3},{5,4},{4,5},{7,6},{6,7},{9,8},{8,9},{11,10... | collective-permute-start | bytes 1474568 | tf_op jit(solution)/shard_map/ppermute | solution.py:39

commit v5 on v4

--- a/solution.py
+++ b/solution.py
@@ -297,9 +297,12 @@
     def z_far(x):
         return sent(x, lambda t, h, z, c: (t, h, z + SHIFT[c][t] + 4, c))
 
+    def two_planes_on(t, h, z, c):
+        return (t, h, z + (-1, 1, 1, -1)[t], c) if c == 0 else (t, h + 2, z, c)
+
     def first_ring(x):
         up, down = sent(x, along(True, 1)), sent(x, along(True, -1))
-        far = sent(x, along(True, 2))
+        far = sent(x, two_planes_on)
         return [(jnp.stack([x[i], up[i]]), jnp.stack([far[i], down[i]])) for i in range(2)]
 
     def second_ring(x):

time: 103 us -> 99.1 us (0.962)
  starting transfers between devices: 46.6 us -> 43.4 us
    ppermute x24, starting transfers between devices: 46.6 us -> 43.4 us  [move(): return lax.ppermute(x, AXES, pairs)]
  transfers between devices with their start and end apart: 24 -> 24, of which waited for: 13 -> 13; matrix products, arithmetic and copies ran while one was open for 2% -> 2% of each run, Pallas kernels for 20% -> 21%
where the time goes in v5:
time: 99.1 us; the launch traced here: 98.8 us
  starting transfers between devices  43.4 us (44%)
  Pallas kernels  25.4 us (26%)
  waiting for transfers between devices  22 us (22%)
  local copies, waits for them, and re-layouts  3.99 us (4%)
  other arithmetic  3.75 us (4%)
    ppermute x24, starting transfers between devices, move(): return lax.ppermute(x, AXES, pairs)  43.4 us
    ppermute x24, waiting for transfers between devices, move(): return lax.ppermute(x, AXES, pairs)  22 us
    pallas_call x2, Pallas kernels, near_conv(): pl.pallas_call(functools.partial(near_kernel, frames, count), grid=(frame...  13.1 us
    pallas_call x1, Pallas kernels, first_layout(): pl.pallas_call(first_layout_kernel, grid=(8,), out_shape=jax.ShapeDtypeSt...  4.06 us
    pallas_call x1, Pallas kernels, second_layout(): pl.pallas_call(second_layout_kernel, grid=(6,), out_shape=jax.ShapeDtypeS...  3.01 us
    pallas_call x1, Pallas kernels, first_conv(): pl.pallas_call(first_conv_kernel, grid=(3,), out_shape=(jax.ShapeDtypeStr...  2.97 us
    unnamed x16, local copies, waits for them, and re-layouts  2.95 us
  transfers between devices with their start and end apart: 24, of which 13 were waited for; matrix products, arithmetic and copies ran while one was open for 2% of the time, Pallas kernels for 21%

profile of v5, /device:TPU:1, one launch (start us, length us, event | category | flops | bytes accessed | tf_op | source)
XLA Modules:
  0.0 98.8 jit_solution(15358952300197814586)
XLA Ops:
  0.0 1.1 %copy.10 = bf16[4,8,10,384]{3,2,1,0:T(8,128)(2,1)S(1)} copy(bf16[4,8,10,384]{3,1,2,0:T(8,128)(2,1)} %param.7) | data formatting | bytes 491520 | tf_op args[0]
  1.1 4.1 %collective-permute-start.2 = (bf16[4,8,10,384]{3,2,1,0:T(8,128)(2,1)S(1)}, bf16[4,8,10,384]{3,2,1,0:T(8,128)(2,1)S(1)}, u32[]{:S(2)}, u32[]{:S(2)}) collective-permute-start(bf16[4,8,10,384]{3,2,1,0:T(8,128)(2,1)S(1)} %copy.10), channel_id=1, source_target_pairs={{0,64},{1,65},{2,66},{3,67},{4,68},{5,69},{6,70},{7,71},{8,72},{9,... | collective-permute-start | bytes 737288 | tf_op jit(solution)/shard_map/ppermute | solution.py:39
  5.1 0.0 copy-start
  5.1 0.9 copy-done
  6.1 0.9 copy-done.1
  7.0 0.3 fold.1
  7.3 0.7 collective-permute-start
  8.0 7.0 %collective-permute-start.1 = (bf16[2,21,8,384]{3,2,1,0:T(8,128)(2,1)S(1)}, bf16[2,21,8,384]{3,2,1,0:T(8,128)(2,1)S(1)}, u32[]{:S(2)}, u32[]{:S(2)}) collective-permute-start(bf16[2,21,8,384]{3,2,1,0:T(8,128)(2,1)S(1)} %fold.1), channel_id=1, source_target_pairs={{8,0},{9,1},{10,2},{11,3},{12,4},{13,5},{14,6},{15,7},{0,8},{1,9},... | collective-permute-start | bytes 774152 | tf_op jit(solution)/shard_map/ppermute | solution.py:39
  15.0 0.1 copy_dynamic-update-slice_fusion
  15.2 3.1 %collective-permute-start.3 = (bf16[8,2,10,384]{3,2,1,0:T(8,128)(2,1)S(1)}, bf16[8,2,10,384]{3,2,1,0:T(8,128)(2,1)S(1)}, u32[]{:S(2)}, u32[]{:S(2)}) collective-permute-start(bf16[8,2,10,384]{3,2,1,0:T(8,128)(2,1)S(1)} %get-tuple-element.51), channel_id=1, source_target_pairs={{0,16},{1,17},{2,18},{3,19},{4,20},{5,21},{6,22},{7,23},{8,24},{9,... | collective-permute-start | bytes 368648 | tf_op jit(solution)/shard_map/ppermute | solution.py:39
  18.3 1.3 %collective-permute-start.4 = (bf16[8,2,10,384]{3,2,1,0:T(8,128)(2,1)S(1)}, bf16[8,2,10,384]{3,2,1,0:T(8,128)(2,1)S(1)}, u32[]{:S(2)}, u32[]{:S(2)}) collective-permute-start(bf16[8,2,10,384]{3,2,1,0:T(8,128)(2,1)S(1)} %get-tuple-element.52), channel_id=1, source_target_pairs={{16,0},{17,1},{18,2},{19,3},{20,4},{21,5},{22,6},{23,7},{24,8},{25... | collective-permute-start | bytes 368648 | tf_op jit(solution)/shard_map/ppermute | solution.py:39
  19.6 2.0 %collective-permute-done.1 = bf16[2,21,8,384]{3,2,1,0:T(8,128)(2,1)S(1)} collective-permute-done((bf16[2,21,8,384]{3,2,1,0:T(8,128)(2,1)S(1)}, bf16[2,21,8,384]{3,2,1,0:T(8,128)(2,1)S(1)}, u32[]{:S(2)}, u32[]{:S(2)}) %collective-permute-start.1) | collective-permute-done | bytes 258080 | tf_op jit(solution)/shard_map/ppermute | solution.py:39
  21.6 0.1 pad_maximum_fusion.1
  21.7 3.4 %collective-permute-done.4 = bf16[8,2,10,384]{3,2,1,0:T(8,128)(2,1)S(1)} collective-permute-done((bf16[8,2,10,384]{3,2,1,0:T(8,128)(2,1)S(1)}, bf16[8,2,10,384]{3,2,1,0:T(8,128)(2,1)S(1)}, u32[]{:S(2)}, u32[]{:S(2)}) %collective-permute-start.4) | collective-permute-done | bytes 122912 | tf_op jit(solution)/shard_map/ppermute | solution.py:39
  25.1 0.3 pad_maximum_fusion
  25.3 2.5 %collective-permute-start.6 = (bf16[2,21,16,384]{3,2,1,0:T(8,128)(2,1)S(1)}, bf16[2,21,16,384]{3,2,1,0:T(8,128)(2,1)S(1)}, u32[]{:S(2)}, u32[]{:S(2)}) collective-permute-start(bf16[2,21,16,384]{3,2,1,0:T(8,128)(2,1)S(1)} %pad_maximum_fusion.1), channel_id=1, source_target_pairs={{14,0},{33,1},{0,2},{35,3},{2,4},{37,5},{4,6},{39,7},{6,8},{41,9},... | collective-permute-start | bytes 1548296 | tf_op jit(solution)/shard_map/ppermute | solution.py:39
  27.8 2.7 %collective-permute-start.5 = (bf16[2,21,16,384]{3,2,1,0:T(8,128)(2,1)S(1)}, bf16[2,21,16,384]{3,2,1,0:T(8,128)(2,1)S(1)}, u32[]{:S(2)}, u32[]{:S(2)}) collective-permute-start(bf16[2,21,16,384]{3,2,1,0:T(8,128)(2,1)S(1)} %pad_maximum_fusion.1), channel_id=1, source_target_pairs={{64,0},{17,1},{66,2},{19,3},{68,4},{21,5},{70,6},{23,7},{72,8},{25... | collective-permute-start | bytes 1548296 | tf_op jit(solution)/shard_map/ppermute | solution.py:39
  30.5 0.1 broadcast_select_fusion
  30.6 5.1 %collective-permute-start.8 = (bf16[8,12,2,384]{3,2,1,0:T(2,128)(2,1)S(1)}, bf16[8,12,2,384]{3,2,1,0:T(2,128)(2,1)S(1)}, u32[]{:S(2)}, u32[]{:S(2)}) collective-permute-start(bf16[8,12,2,384]{3,2,1,0:T(2,128)(2,1)S(1)} %broadcast_select_fusion), channel_id=1, source_target_pairs={{2,1},{1,2},{4,3},{3,4},{6,5},{5,6},{8,7},{7,8},{10,9},{9,10},{12,... | collective-permute-start | bytes 442376 | tf_op jit(solution)/shard_map/ppermute | solution.py:39
  35.7 0.1 fusion.5
  35.8 3.0 %collective-permute-done.8 = bf16[8,12,2,384]{3,2,1,0:T(2,128)(2,1)S(1)} collective-permute-done((bf16[8,12,2,384]{3,2,1,0:T(2,128)(2,1)S(1)}, bf16[8,12,2,384]{3,2,1,0:T(2,128)(2,1)S(1)}, u32[]{:S(2)}, u32[]{:S(2)}) %collective-permute-start.8) | collective-permute-done | bytes 147488 | tf_op jit(solution)/shard_map/ppermute | solution.py:39
  38.8 0.8 maximum_select_fusion.1
  39.7 0.5 copy.12
  40.2 0.1 collective-permute-start.9
  40.3 0.1 fusion.3
  40.4 0.2 collective-permute-done.7
  40.6 0.1 fusion.4
  40.6 0.1 pad_maximum_fusion.3
  40.8 0.1 fusion.6
  40.8 0.1 pad_maximum_fusion.2
  41.0 1.7 %collective-permute-done.9 = bf16[8,12,12,384]{3,0,2,1:T(8,128)(2,1)S(1)} collective-permute-done((bf16[8,12,12,384]{3,0,2,1:T(8,128)(2,1)S(1)}, bf16[8,12,12,384]{3,0,2,1:T(8,128)(2,1)S(1)}, u32[]{:S(2)}, u32[]{:S(2)}) %collective-permute-start.9) | collective-permute-done | bytes 884768 | tf_op jit(solution)/shard_map/ppermute | solution.py:39
  42.7 0.2 copy.13
  42.9 0.0 copy-start.4
  42.9 1.4 %maximum_select_fusion.x_ref = bf16[8,12,24,384]{3,2,1,0:T(8,128)(2,1)S(1)} fusion(bf16[8,12,12,384]{3,2,1,0:T(8,128)(2,1)S(1)} %copy.13, bf16[8,12,12,384]{3,2,1,0:T(8,128)(2,1)S(1)} %maximum_select_fusion.1, pred[]{:T(512)S(6)} %eq.2), kind=kLoop, calls=%fused_computation | loop fusion | flops 7962624 | bytes 3538945 | tf_op jit(solution)/shard_map/jit(_where)/select_n | solution.py:346
  44.3 2.3 %collective-permute-start.10 = (bf16[2,21,16,384]{3,2,1,0:T(8,128)(2,1)S(1)}, bf16[2,21,16,384]{3,2,1,0:T(8,128)(2,1)S(1)}, u32[]{:S(2)}, u32[]{:S(2)}) collective-permute-start(bf16[2,21,16,384]{3,2,1,0:T(8,128)(2,1)S(1)} %get-tuple-element.30.refs_0_), channel_id=1, source_target_pairs={{16,0},{65,1},{18,2},{67,3},{20,4},{69,5},{22,6},{71,7},{24,8},{73... | collective-permute-start | bytes 1548296 | tf_op jit(solution)/shard_map/ppermute | solution.py:39
  46.7 1.0 collective-permute-start.11
  47.6 2.4 %collective-permute-start.14 = (bf16[2,21,16,384]{3,2,1,0:T(8,128)(2,1)S(1)}, bf16[2,21,16,384]{3,2,1,0:T(8,128)(2,1)S(1)}, u32[]{:S(2)}, u32[]{:S(2)}) collective-permute-start(bf16[2,21,16,384]{3,2,1,0:T(8,128)(2,1)S(1)} %get-tuple-element.31.refs_1_), channel_id=1, source_target_pairs={{16,0},{65,1},{18,2},{67,3},{20,4},{69,5},{22,6},{71,7},{24,8},{73... | collective-permute-start | bytes 1548296 | tf_op jit(solution)/shard_map/ppermute | solution.py:39
  50.0 0.0 collective-permute-start.15
  50.0 4.1 %first_layout.1.laid_ref = bf16[6,8,288,256]{3,2,1,0:T(8,128)(2,1)S(1)} custom-call(bf16[8,12,24,384]{3,2,1,0:T(8,128)(2,1)S(1)} %maximum_select_fusion.x_ref, f32[1,384]{1,0:T(1,128)S(1)} %reshape.10.gain_ref), custom_call_target="tpu_custom_call" | custom-call | tf_op jit(solution)/shard_map/first_layout/pallas_call | solution.py:122
  54.1 0.2 collective-permute-done.10.refs_2_
  54.3 2.5 %collective-permute-done.11.refs_5_ = bf16[2,21,16,384]{3,2,1,0:T(8,128)(2,1)S(1)} collective-permute-done((bf16[2,21,16,384]{3,2,1,0:T(8,128)(2,1)S(1)}, bf16[2,21,16,384]{3,2,1,0:T(8,128)(2,1)S(1)}, u32[]{:S(2)}, u32[]{:S(2)}) %collective-permute-start.11) | collective-permute-done | bytes 516128 | tf_op jit(solution)/shard_map/ppermute | solution.py:39
  56.8 1.5 %collective-permute-start.12 = (bf16[2,21,16,384]{3,2,1,0:T(8,128)(2,1)S(1)}, bf16[2,21,16,384]{3,2,1,0:T(8,128)(2,1)S(1)}, u32[]{:S(2)}, u32[]{:S(2)}) collective-permute-start(bf16[2,21,16,384]{3,2,1,0:T(8,128)(2,1)S(1)} %collective-permute-done.10.refs_2_), channel_id=1, source_target_pairs={{16,0},{65,1},{18,2},{67,3},{20,4},{69,5},{22,6},{71,7},{24,8},{73... | collective-permute-start | bytes 1548296 | tf_op jit(solution)/shard_map/ppermute | solution.py:39
  58.3 2.7 %collective-permute-start.16 = (bf16[2,21,16,384]{3,2,1,0:T(8,128)(2,1)S(1)}, bf16[2,21,16,384]{3,2,1,0:T(8,128)(2,1)S(1)}, u32[]{:S(2)}, u32[]{:S(2)}) collective-permute-start(bf16[2,21,16,384]{3,2,1,0:T(8,128)(2,1)S(1)} %get-tuple-element.40.refs_0_), channel_id=1, source_target_pairs={{16,0},{65,1},{18,2},{67,3},{20,4},{69,5},{22,6},{71,7},{24,8},{73... | collective-permute-start | bytes 1548296 | tf_op jit(solution)/shard_map/ppermute | solution.py:39
  60.9 0.8 collective-permute-start.17
  61.7 0.6 collective-permute-done.15.refs_4_
  62.3 8.5 %near_conv.2.near_ref = f32[6,240,384]{2,1,0:T(8,128)S(1)} custom-call(bf16[6,8,288,256]{3,2,1,0:T(8,128)(2,1)S(1)} %first_layout.1.laid_ref, bf16[2,21,16,384]{3,2,1,0:T(8,128)(2,1)S(1)} %get-tuple-element.30.refs_0_, bf16[2,21,16,384]{3,2,1,0:T(8,128)(2,1)S(1)} %get-tuple-element.31.refs_1_, bf16[2,21,16,384]{3,2,1,0:T(8,128)(2,1)S(1)} %collective-permute-done.10.refs_2_, ...), custom_call_target="tpu_custom_call" | custom-call | tf_op jit(solution)/shard_map/near_conv/pallas_call | solution.py:217
  70.8 0.0 copy-start.5
  70.9 0.0 copy-start.6
  70.9 0.0 collective-permute-done.16.refs_2_
  70.9 2.5 %collective-permute-done.17.refs_5_ = bf16[2,21,16,384]{3,2,1,0:T(8,128)(2,1)S(1)} collective-permute-done((bf16[2,21,16,384]{3,2,1,0:T(8,128)(2,1)S(1)}, bf16[2,21,16,384]{3,2,1,0:T(8,128)(2,1)S(1)}, u32[]{:S(2)}, u32[]{:S(2)}) %collective-permute-start.17) | collective-permute-done | bytes 516128 | tf_op jit(solution)/shard_map/ppermute | solution.py:39
  73.4 3.0 %first_conv.1 = (f32[6,240,384]{2,1,0:T(8,128)S(1)}, bf16[6,240,384]{2,1,0:T(8,128)(2,1)S(1)}) custom-call(bf16[6,8,288,256]{3,2,1,0:T(8,128)(2,1)S(1)} %first_layout.1.laid_ref, bf16[2,21,16,384]{3,2,1,0:T(8,128)(2,1)S(1)} %collective-permute-done.12.b0, bf16[2,21,16,384]{3,2,1,0:T(8,128)(2,1)S(1)} %collective-permute-done.13.b1, ...), custom_call_target="tpu_custom_call" | custom-call | tf_op jit(solution)/shard_map/first_conv/pallas_call | solution.py:237
  76.4 0.9 collective-permute-start.18
  77.3 2.3 %collective-permute-start.21 = (bf16[2,21,16,384]{3,2,1,0:T(8,128)(2,1)S(1)}, bf16[2,21,16,384]{3,2,1,0:T(8,128)(2,1)S(1)}, u32[]{:S(2)}, u32[]{:S(2)}) collective-permute-start(bf16[2,21,16,384]{3,2,1,0:T(8,128)(2,1)S(1)} %get-tuple-element.41.refs_1_), channel_id=1, source_target_pairs={{16,0},{65,1},{18,2},{67,3},{20,4},{69,5},{22,6},{71,7},{24,8},{73... | collective-permute-start | bytes 1548296 | tf_op jit(solution)/shard_map/ppermute | solution.py:39
  79.5 2.7 %collective-permute-start.19 = (bf16[2,21,16,384]{3,2,1,0:T(8,128)(2,1)S(1)}, bf16[2,21,16,384]{3,2,1,0:T(8,128)(2,1)S(1)}, u32[]{:S(2)}, u32[]{:S(2)}) collective-permute-start(bf16[2,21,16,384]{3,2,1,0:T(8,128)(2,1)S(1)} %collective-permute-done.16.refs_2_), channel_id=1, source_target_pairs={{16,0},{65,1},{18,2},{67,3},{20,4},{69,5},{22,6},{71,7},{24,8},{73... | collective-permute-start | bytes 1548296 | tf_op jit(solution)/shard_map/ppermute | solution.py:39
  82.2 3.0 %second_layout.1.laid_ref = bf16[6,6,240,256]{3,2,1,0:T(8,128)(2,1)S(1)} custom-call(f32[6,240,384]{2,1,0:T(8,128)S(1)} %get-tuple-element.45.mine_ref, bf16[6,240,384]{2,1,0:T(8,128)(2,1)S(1)} %collective-permute-done.18.other_ref, f32[1,384]{1,0:T(1,128)S(1)} %reshape.11.bias_ref, f32[1,384]{1,0:T(1,128)S(1)} %reshape.12.gain_ref), custom_call_target="tpu_custom_call" | custom-call | tf_op jit(solution)/shard_map/second_layout/pallas_call | solution.py:154
  85.3 0.3 collective-permute-done.21.refs_3_
  85.6 3.4 %collective-permute-done.22.refs_4_ = bf16[2,21,16,384]{3,2,1,0:T(8,128)(2,1)S(1)} collective-permute-done((bf16[2,21,16,384]{3,2,1,0:T(8,128)(2,1)S(1)}, bf16[2,21,16,384]{3,2,1,0:T(8,128)(2,1)S(1)}, u32[]{:S(2)}, u32[]{:S(2)}) %collective-permute-start.22) | collective-permute-done | bytes 516128 | tf_op jit(solution)/shard_map/ppermute | solution.py:39
  89.0 4.6 %near_conv.3.near_ref = f32[4,192,384]{2,1,0:T(8,128)S(1)} custom-call(bf16[6,6,240,256]{3,2,1,0:T(8,128)(2,1)S(1)} %second_layout.1.laid_ref, bf16[2,21,16,384]{3,2,1,0:T(8,128)(2,1)S(1)} %get-tuple-element.40.refs_0_, bf16[2,21,16,384]{3,2,1,0:T(8,128)(2,1)S(1)} %get-tuple-element.41.refs_1_, bf16[2,21,16,384]{3,2,1,0:T(8,128)(2,1)S(1)} %collective-permute-done.16.refs_2_, ...), custom_call_target="tpu_custom_call" | custom-call | tf_op jit(solution)/shard_map/near_conv/pallas_call | solution.py:217
  93.6 0.0 copy-start.3
  93.6 0.6 collective-permute-done.20.b1
  94.2 1.8 %second_conv.1 = (f32[4,10,8,384]{3,2,1,0:T(8,128)S(1)}, f32[4,10,8,384]{3,2,1,0:T(8,128)S(1)}) custom-call(bf16[6,6,240,256]{3,2,1,0:T(8,128)(2,1)S(1)} %second_layout.1.laid_ref, bf16[2,21,16,384]{3,2,1,0:T(8,128)(2,1)S(1)} %collective-permute-done.19.b0, bf16[2,21,16,384]{3,2,1,0:T(8,128)(2,1)S(1)} %collective-permute-done.20.b1, ...), custom_call_target="tpu_custom_call" | custom-call | tf_op jit(solution)/shard_map/second_conv/pallas_call | solution.py:266
  96.1 0.5 collective-permute-start.23
  96.5 1.5 %collective-permute-done.23 = f32[4,10,8,384]{3,2,1,0:T(8,128)S(1)} collective-permute-done((f32[4,10,8,384]{3,2,1,0:T(8,128)S(1)}, f32[4,10,8,384]{3,2,1,0:T(8,128)S(1)}, u32[]{:S(2)}, u32[]{:S(2)}) %collective-permute-start.23) | collective-permute-done | bytes 491552 | tf_op jit(solution)/shard_map/ppermute | solution.py:39
  98.0 0.8 fusion.1
  (26 shorter events, 0.1 us)
Async XLA Ops:
  0.0 15.0 %copy-start.2 = (bf16[4,8,10,384]{3,1,2,0:T(8,128)(2,1)S(1)}, bf16[4,8,10,384]{3,1,2,0:T(8,128)(2,1)}, u32[]{:S(2)}) copy-start(bf16[4,8,10,384]{3,1,2,0:T(8,128)(2,1)} %param.7) | copy-start | bytes 737284
  1.1 13.9 %collective-permute-start.2 = (bf16[4,8,10,384]{3,2,1,0:T(8,128)(2,1)S(1)}, bf16[4,8,10,384]{3,2,1,0:T(8,128)(2,1)S(1)}, u32[]{:S(2)}, u32[]{:S(2)}) collective-permute-start(bf16[4,8,10,384]{3,2,1,0:T(8,128)(2,1)S(1)} %copy.10), channel_id=1, source_target_pairs={{0,64},{1,65},{2,66},{3,67},{4,68},{5,69},{6,70},{7,71},{8,72},{9,... | collective-permute-start | bytes 737288 | tf_op jit(solution)/shard_map/ppermute | solution.py:39
  5.1 0.9 copy-start
  6.0 0.9 copy-start.1
  7.3 12.3 %collective-permute-start = (bf16[2,21,8,384]{3,2,1,0:T(8,128)(2,1)S(1)}, bf16[2,21,8,384]{3,2,1,0:T(8,128)(2,1)S(1)}, u32[]{:S(2)}, u32[]{:S(2)}) collective-permute-start(bf16[2,21,8,384]{3,2,1,0:T(8,128)(2,1)S(1)} %fold.1), channel_id=1, source_target_pairs={{0,0},{1,1},{2,2},{3,3},{4,4},{5,5},{6,6},{7,7},{8,8},{9,9},{10,10... | collective-permute-start | bytes 774152 | tf_op jit(solution)/shard_map/ppermute | solution.py:39
  8.0 13.6 %collective-permute-start.1 = (bf16[2,21,8,384]{3,2,1,0:T(8,128)(2,1)S(1)}, bf16[2,21,8,384]{3,2,1,0:T(8,128)(2,1)S(1)}, u32[]{:S(2)}, u32[]{:S(2)}) collective-permute-start(bf16[2,21,8,384]{3,2,1,0:T(8,128)(2,1)S(1)} %fold.1), channel_id=1, source_target_pairs={{8,0},{9,1},{10,2},{11,3},{12,4},{13,5},{14,6},{15,7},{0,8},{1,9},... | collective-permute-start | bytes 774152 | tf_op jit(solution)/shard_map/ppermute | solution.py:39
  15.2 6.5 %collective-permute-start.3 = (bf16[8,2,10,384]{3,2,1,0:T(8,128)(2,1)S(1)}, bf16[8,2,10,384]{3,2,1,0:T(8,128)(2,1)S(1)}, u32[]{:S(2)}, u32[]{:S(2)}) collective-permute-start(bf16[8,2,10,384]{3,2,1,0:T(8,128)(2,1)S(1)} %get-tuple-element.51), channel_id=1, source_target_pairs={{0,16},{1,17},{2,18},{3,19},{4,20},{5,21},{6,22},{7,23},{8,24},{9,... | collective-permute-start | bytes 368648 | tf_op jit(solution)/shard_map/ppermute | solution.py:39
  18.3 6.8 %collective-permute-start.4 = (bf16[8,2,10,384]{3,2,1,0:T(8,128)(2,1)S(1)}, bf16[8,2,10,384]{3,2,1,0:T(8,128)(2,1)S(1)}, u32[]{:S(2)}, u32[]{:S(2)}) collective-permute-start(bf16[8,2,10,384]{3,2,1,0:T(8,128)(2,1)S(1)} %get-tuple-element.52), channel_id=1, source_target_pairs={{16,0},{17,1},{18,2},{19,3},{20,4},{21,5},{22,6},{23,7},{24,8},{25... | collective-permute-start | bytes 368648 | tf_op jit(solution)/shard_map/ppermute | solution.py:39
  25.3 15.0 %collective-permute-start.6 = (bf16[2,21,16,384]{3,2,1,0:T(8,128)(2,1)S(1)}, bf16[2,21,16,384]{3,2,1,0:T(8,128)(2,1)S(1)}, u32[]{:S(2)}, u32[]{:S(2)}) collective-permute-start(bf16[2,21,16,384]{3,2,1,0:T(8,128)(2,1)S(1)} %pad_maximum_fusion.1), channel_id=1, source_target_pairs={{14,0},{33,1},{0,2},{35,3},{2,4},{37,5},{4,6},{39,7},{6,8},{41,9},... | collective-permute-start | bytes 1548296 | tf_op jit(solution)/shard_map/ppermute | solution.py:39
  27.8 12.7 %collective-permute-start.7 = (bf16[2,21,16,384]{3,2,1,0:T(8,128)(2,1)S(1)}, bf16[2,21,16,384]{3,2,1,0:T(8,128)(2,1)S(1)}, u32[]{:S(2)}, u32[]{:S(2)}) collective-permute-start(bf16[2,21,16,384]{3,2,1,0:T(8,128)(2,1)S(1)} %pad_maximum_fusion.1), channel_id=1, source_target_pairs={{192,0},{49,1},{194,2},{51,3},{196,4},{53,5},{198,6},{55,7},{200,8... | collective-permute-start | bytes 1548296 | tf_op jit(solution)/shard_map/ppermute | solution.py:39
  27.8 12.9 %collective-permute-start.5 = (bf16[2,21,16,384]{3,2,1,0:T(8,128)(2,1)S(1)}, bf16[2,21,16,384]{3,2,1,0:T(8,128)(2,1)S(1)}, u32[]{:S(2)}, u32[]{:S(2)}) collective-permute-start(bf16[2,21,16,384]{3,2,1,0:T(8,128)(2,1)S(1)} %pad_maximum_fusion.1), channel_id=1, source_target_pairs={{64,0},{17,1},{66,2},{19,3},{68,4},{21,5},{70,6},{23,7},{72,8},{25... | collective-permute-start | bytes 1548296 | tf_op jit(solution)/shard_map/ppermute | solution.py:39
  30.6 8.2 %collective-permute-start.8 = (bf16[8,12,2,384]{3,2,1,0:T(2,128)(2,1)S(1)}, bf16[8,12,2,384]{3,2,1,0:T(2,128)(2,1)S(1)}, u32[]{:S(2)}, u32[]{:S(2)}) collective-permute-start(bf16[8,12,2,384]{3,2,1,0:T(2,128)(2,1)S(1)} %broadcast_select_fusion), channel_id=1, source_target_pairs={{2,1},{1,2},{4,3},{3,4},{6,5},{5,6},{8,7},{7,8},{10,9},{9,10},{12,... | collective-permute-start | bytes 442376 | tf_op jit(solution)/shard_map/ppermute | solution.py:39
  40.2 2.5 %collective-permute-start.9 = (bf16[8,12,12,384]{3,0,2,1:T(8,128)(2,1)S(1)}, bf16[8,12,12,384]{3,0,2,1:T(8,128)(2,1)S(1)}, u32[]{:S(2)}, u32[]{:S(2)}) collective-permute-start(bf16[8,12,12,384]{3,0,2,1:T(8,128)(2,1)S(1)} %copy.12), channel_id=1, source_target_pairs={{1,0},{0,1},{3,2},{2,3},{5,4},{4,5},{7,6},{6,7},{9,8},{8,9},{11,10... | collective-permute-start | bytes 2654216 | tf_op jit(solution)/shard_map/ppermute | solution.py:39
  42.9 7.1 %copy-start.4 = (f32[384]{0:T(512)S(1)}, f32[384]{0:T(512)}, u32[]{:S(2)}) copy-start(f32[384]{0:T(512)} %param.8) | copy-start | bytes 4612
  44.3 10.0 %collective-permute-start.10 = (bf16[2,21,16,384]{3,2,1,0:T(8,128)(2,1)S(1)}, bf16[2,21,16,384]{3,2,1,0:T(8,128)(2,1)S(1)}, u32[]{:S(2)}, u32[]{:S(2)}) collective-permute-start(bf16[2,21,16,384]{3,2,1,0:T(8,128)(2,1)S(1)} %get-tuple-element.30.refs_0_), channel_id=1, source_target_pairs={{16,0},{65,1},{18,2},{67,3},{20,4},{69,5},{22,6},{71,7},{24,8},{73... | collective-permute-start | bytes 1548296 | tf_op jit(solution)/shard_map/ppermute | solution.py:39
  46.7 10.1 %collective-permute-start.11 = (bf16[2,21,16,384]{3,2,1,0:T(8,128)(2,1)S(1)}, bf16[2,21,16,384]{3,2,1,0:T(8,128)(2,1)S(1)}, u32[]{:S(2)}, u32[]{:S(2)}) collective-permute-start(bf16[2,21,16,384]{3,2,1,0:T(8,128)(2,1)S(1)} %get-tuple-element.31.refs_1_), channel_id=1, source_target_pairs={{48,0},{193,1},{50,2},{195,3},{52,4},{197,5},{54,6},{199,7},{56,8}... | collective-permute-start | bytes 1548296 | tf_op jit(solution)/shard_map/ppermute | solution.py:39
  47.6 13.3 %collective-permute-start.14 = (bf16[2,21,16,384]{3,2,1,0:T(8,128)(2,1)S(1)}, bf16[2,21,16,384]{3,2,1,0:T(8,128)(2,1)S(1)}, u32[]{:S(2)}, u32[]{:S(2)}) collective-permute-start(bf16[2,21,16,384]{3,2,1,0:T(8,128)(2,1)S(1)} %get-tuple-element.31.refs_1_), channel_id=1, source_target_pairs={{16,0},{65,1},{18,2},{67,3},{20,4},{69,5},{22,6},{71,7},{24,8},{73... | collective-permute-start | bytes 1548296 | tf_op jit(solution)/shard_map/ppermute | solution.py:39
  50.0 12.3 %collective-permute-start.15 = (bf16[2,21,16,384]{3,2,1,0:T(8,128)(2,1)S(1)}, bf16[2,21,16,384]{3,2,1,0:T(8,128)(2,1)S(1)}, u32[]{:S(2)}, u32[]{:S(2)}) collective-permute-start(bf16[2,21,16,384]{3,2,1,0:T(8,128)(2,1)S(1)} %get-tuple-element.30.refs_0_), channel_id=1, source_target_pairs={{48,0},{193,1},{50,2},{195,3},{52,4},{197,5},{54,6},{199,7},{56,8}... | collective-permute-start | bytes 1548296 | tf_op jit(solution)/shard_map/ppermute | solution.py:39
  56.8 14.1 %collective-permute-start.12 = (bf16[2,21,16,384]{3,2,1,0:T(8,128)(2,1)S(1)}, bf16[2,21,16,384]{3,2,1,0:T(8,128)(2,1)S(1)}, u32[]{:S(2)}, u32[]{:S(2)}) collective-permute-start(bf16[2,21,16,384]{3,2,1,0:T(8,128)(2,1)S(1)} %collective-permute-done.10.refs_2_), channel_id=1, source_target_pairs={{16,0},{65,1},{18,2},{67,3},{20,4},{69,5},{22,6},{71,7},{24,8},{73... | collective-permute-start | bytes 1548296 | tf_op jit(solution)/shard_map/ppermute | solution.py:39
  58.2 12.6 %collective-permute-start.13 = (bf16[2,21,16,384]{3,2,1,0:T(8,128)(2,1)S(1)}, bf16[2,21,16,384]{3,2,1,0:T(8,128)(2,1)S(1)}, u32[]{:S(2)}, u32[]{:S(2)}) collective-permute-start(bf16[2,21,16,384]{3,2,1,0:T(8,128)(2,1)S(1)} %collective-permute-done.11.refs_5_), channel_id=1, source_target_pairs={{48,0},{193,1},{50,2},{195,3},{52,4},{197,5},{54,6},{199,7},{56,8}... | collective-permute-start | bytes 1548296 | tf_op jit(solution)/shard_map/ppermute | solution.py:39
  58.3 12.7 %collective-permute-start.16 = (bf16[2,21,16,384]{3,2,1,0:T(8,128)(2,1)S(1)}, bf16[2,21,16,384]{3,2,1,0:T(8,128)(2,1)S(1)}, u32[]{:S(2)}, u32[]{:S(2)}) collective-permute-start(bf16[2,21,16,384]{3,2,1,0:T(8,128)(2,1)S(1)} %get-tuple-element.40.refs_0_), channel_id=1, source_target_pairs={{16,0},{65,1},{18,2},{67,3},{20,4},{69,5},{22,6},{71,7},{24,8},{73... | collective-permute-start | bytes 1548296 | tf_op jit(solution)/shard_map/ppermute | solution.py:39
  60.9 12.4 %collective-permute-start.17 = (bf16[2,21,16,384]{3,2,1,0:T(8,128)(2,1)S(1)}, bf16[2,21,16,384]{3,2,1,0:T(8,128)(2,1)S(1)}, u32[]{:S(2)}, u32[]{:S(2)}) collective-permute-start(bf16[2,21,16,384]{3,2,1,0:T(8,128)(2,1)S(1)} %get-tuple-element.41.refs_1_), channel_id=1, source_target_pairs={{48,0},{193,1},{50,2},{195,3},{52,4},{197,5},{54,6},{199,7},{56,8}... | collective-permute-start | bytes 1548296 | tf_op jit(solution)/shard_map/ppermute | solution.py:39
  70.8 11.4 %copy-start.5 = (f32[384]{0:T(512)S(1)}, f32[384]{0:T(512)}, u32[]{:S(2)}) copy-start(f32[384]{0:T(512)} %param.10) | copy-start | bytes 4612
  70.9 11.4 %copy-start.6 = (f32[384]{0:T(512)S(1)}, f32[384]{0:T(512)}, u32[]{:S(2)}) copy-start(f32[384]{0:T(512)} %param.11) | copy-start | bytes 4612
  76.4 5.9 %collective-permute-start.18 = (bf16[6,240,384]{2,1,0:T(8,128)(2,1)S(1)}, bf16[6,240,384]{2,1,0:T(8,128)(2,1)S(1)}, u32[]{:S(2)}, u32[]{:S(2)}) collective-permute-start(bf16[6,240,384]{2,1,0:T(8,128)(2,1)S(1)} %get-tuple-element.46), channel_id=1, source_target_pairs={{1,0},{0,1},{3,2},{2,3},{5,4},{4,5},{7,6},{6,7},{9,8},{8,9},{11,10... | collective-permute-start | bytes 3317768 | tf_op jit(solution)/shard_map/ppermute | solution.py:39
  77.3 8.3 %collective-permute-start.21 = (bf16[2,21,16,384]{3,2,1,0:T(8,128)(2,1)S(1)}, bf16[2,21,16,384]{3,2,1,0:T(8,128)(2,1)S(1)}, u32[]{:S(2)}, u32[]{:S(2)}) collective-permute-start(bf16[2,21,16,384]{3,2,1,0:T(8,128)(2,1)S(1)} %get-tuple-element.41.refs_1_), channel_id=1, source_target_pairs={{16,0},{65,1},{18,2},{67,3},{20,4},{69,5},{22,6},{71,7},{24,8},{73... | collective-permute-start | bytes 1548296 | tf_op jit(solution)/shard_map/ppermute | solution.py:39
  79.5 9.4 %collective-permute-start.22 = (bf16[2,21,16,384]{3,2,1,0:T(8,128)(2,1)S(1)}, bf16[2,21,16,384]{3,2,1,0:T(8,128)(2,1)S(1)}, u32[]{:S(2)}, u32[]{:S(2)}) collective-permute-start(bf16[2,21,16,384]{3,2,1,0:T(8,128)(2,1)S(1)} %get-tuple-element.40.refs_0_), channel_id=1, source_target_pairs={{48,0},{193,1},{50,2},{195,3},{52,4},{197,5},{54,6},{199,7},{56,8}... | collective-permute-start | bytes 1548296 | tf_op jit(solution)/shard_map/ppermute | solution.py:39
  79.5 14.1 %collective-permute-start.19 = (bf16[2,21,16,384]{3,2,1,0:T(8,128)(2,1)S(1)}, bf16[2,21,16,384]{3,2,1,0:T(8,128)(2,1)S(1)}, u32[]{:S(2)}, u32[]{:S(2)}) collective-permute-start(bf16[2,21,16,384]{3,2,1,0:T(8,128)(2,1)S(1)} %collective-permute-done.16.refs_2_), channel_id=1, source_target_pairs={{16,0},{65,1},{18,2},{67,3},{20,4},{69,5},{22,6},{71,7},{24,8},{73... | collective-permute-start | bytes 1548296 | tf_op jit(solution)/shard_map/ppermute | solution.py:39
  82.2 12.0 %collective-permute-start.20 = (bf16[2,21,16,384]{3,2,1,0:T(8,128)(2,1)S(1)}, bf16[2,21,16,384]{3,2,1,0:T(8,128)(2,1)S(1)}, u32[]{:S(2)}, u32[]{:S(2)}) collective-permute-start(bf16[2,21,16,384]{3,2,1,0:T(8,128)(2,1)S(1)} %collective-permute-done.17.refs_5_), channel_id=1, source_target_pairs={{48,0},{193,1},{50,2},{195,3},{52,4},{197,5},{54,6},{199,7},{56,8}... | collective-permute-start | bytes 1548296 | tf_op jit(solution)/shard_map/ppermute | solution.py:39
  93.6 4.4 %copy-start.3 = (f32[384]{0:T(512)S(1)}, f32[384]{0:T(512)}, u32[]{:S(2)}) copy-start(f32[384]{0:T(512)} %param.13) | copy-start | bytes 4612
  96.1 2.0 %collective-permute-start.23 = (f32[4,10,8,384]{3,2,1,0:T(8,128)S(1)}, f32[4,10,8,384]{3,2,1,0:T(8,128)S(1)}, u32[]{:S(2)}, u32[]{:S(2)}) collective-permute-start(f32[4,10,8,384]{3,2,1,0:T(8,128)S(1)} %get-tuple-element.50), channel_id=1, source_target_pairs={{1,0},{0,1},{3,2},{2,3},{5,4},{4,5},{7,6},{6,7},{9,8},{8,9},{11,10... | collective-permute-start | bytes 1474568 | tf_op jit(solution)/shard_map/ppermute | solution.py:39

commit v6 on v5

--- a/solution.py
+++ b/solution.py
@@ -341,8 +341,7 @@
             jnp.concatenate([x, beside], axis=2),
         )
 
-    def joined(mine, core):
-        other = swapped(mine)
+    def joined(mine, other, core):
         return jnp.where(
             core == 0,
             jnp.concatenate([mine, other], axis=2),
@@ -359,7 +358,9 @@
         both = jnp.concatenate([z_near(both), z_far(both)], axis=2)
         both, wide = at_once(both, higher(taller(features)))
         one, two = first_ring(both)
-        (one, two), wide = at_once((one, two), joined(wider(wide, core), core))
+        wide = wider(wide, core)
+        (one, two), wide, other = at_once((one, two), wide, swapped(wide))
+        wide = joined(wide, other, core)
         ends, rest = second_ring(one), second_ring_rest(one)
         ends, laid, two = at_once(ends, first_layout(wide, gains[0]), two)
         far = passed_on(*ends)

time: 99.1 us -> 98.6 us (level)
  waiting for transfers between devices: 22 us -> 20.8 us
    ppermute x24, waiting for transfers between devices: 22 us -> 20.8 us  [move(): return lax.ppermute(x, AXES, pairs)]
  transfers between devices with their start and end apart: 24 -> 24, of which waited for: 13 -> 12; matrix products, arithmetic and copies ran while one was open for 2% -> 4% of each run, Pallas kernels for 21% -> 21%
where the time goes in v6:
time: 98.6 us; the launch traced here: 98.3 us
  starting transfers between devices  44.1 us (45%)
  Pallas kernels  25.4 us (26%)
  waiting for transfers between devices  20.8 us (21%)
  local copies, waits for them, and re-layouts  3.99 us (4%)
  other arithmetic  3.75 us (4%)
    ppermute x24, starting transfers between devices, move(): return lax.ppermute(x, AXES, pairs)  44.1 us
    ppermute x24, waiting for transfers between devices, move(): return lax.ppermute(x, AXES, pairs)  20.8 us
    pallas_call x2, Pallas kernels, near_conv(): pl.pallas_call(functools.partial(near_kernel, frames, count), grid=(frame...  13.1 us
    pallas_call x1, Pallas kernels, first_layout(): pl.pallas_call(first_layout_kernel, grid=(8,), out_shape=jax.ShapeDtypeSt...  4.06 us
    pallas_call x1, Pallas kernels, second_layout(): pl.pallas_call(second_layout_kernel, grid=(6,), out_shape=jax.ShapeDtypeS...  3.01 us
    pallas_call x1, Pallas kernels, first_conv(): pl.pallas_call(first_conv_kernel, grid=(3,), out_shape=(jax.ShapeDtypeStr...  2.97 us
    unnamed x16, local copies, waits for them, and re-layouts  2.95 us
  transfers between devices with their start and end apart: 24, of which 12 were waited for; matrix products, arithmetic and copies ran while one was open for 4% of the time, Pallas kernels for 21%

profile of v6, /device:TPU:1, one launch (start us, length us, event | category | flops | bytes accessed | tf_op | source)
XLA Modules:
  0.0 98.3 jit_solution(9765983601001104075)
XLA Ops:
  0.0 1.1 %copy.10 = bf16[4,8,10,384]{3,2,1,0:T(8,128)(2,1)S(1)} copy(bf16[4,8,10,384]{3,1,2,0:T(8,128)(2,1)} %param.7) | data formatting | bytes 491520 | tf_op args[0]
  1.1 4.1 %collective-permute-start.2 = (bf16[4,8,10,384]{3,2,1,0:T(8,128)(2,1)S(1)}, bf16[4,8,10,384]{3,2,1,0:T(8,128)(2,1)S(1)}, u32[]{:S(2)}, u32[]{:S(2)}) collective-permute-start(bf16[4,8,10,384]{3,2,1,0:T(8,128)(2,1)S(1)} %copy.10), channel_id=1, source_target_pairs={{0,64},{1,65},{2,66},{3,67},{4,68},{5,69},{6,70},{7,71},{8,72},{9,... | collective-permute-start | bytes 737288 | tf_op jit(solution)/shard_map/ppermute | solution.py:39
  5.1 0.0 copy-start
  5.1 0.9 copy-done
  6.1 0.9 copy-done.1
  7.0 0.3 fold.1
  7.3 0.7 collective-permute-start
  8.0 7.0 %collective-permute-start.1 = (bf16[2,21,8,384]{3,2,1,0:T(8,128)(2,1)S(1)}, bf16[2,21,8,384]{3,2,1,0:T(8,128)(2,1)S(1)}, u32[]{:S(2)}, u32[]{:S(2)}) collective-permute-start(bf16[2,21,8,384]{3,2,1,0:T(8,128)(2,1)S(1)} %fold.1), channel_id=1, source_target_pairs={{8,0},{9,1},{10,2},{11,3},{12,4},{13,5},{14,6},{15,7},{0,8},{1,9},... | collective-permute-start | bytes 774152 | tf_op jit(solution)/shard_map/ppermute | solution.py:39
  15.0 0.1 copy_dynamic-update-slice_fusion
  15.2 3.1 %collective-permute-start.3 = (bf16[8,2,10,384]{3,2,1,0:T(8,128)(2,1)S(1)}, bf16[8,2,10,384]{3,2,1,0:T(8,128)(2,1)S(1)}, u32[]{:S(2)}, u32[]{:S(2)}) collective-permute-start(bf16[8,2,10,384]{3,2,1,0:T(8,128)(2,1)S(1)} %get-tuple-element.53), channel_id=1, source_target_pairs={{0,16},{1,17},{2,18},{3,19},{4,20},{5,21},{6,22},{7,23},{8,24},{9,... | collective-permute-start | bytes 368648 | tf_op jit(solution)/shard_map/ppermute | solution.py:39
  18.3 1.3 %collective-permute-start.4 = (bf16[8,2,10,384]{3,2,1,0:T(8,128)(2,1)S(1)}, bf16[8,2,10,384]{3,2,1,0:T(8,128)(2,1)S(1)}, u32[]{:S(2)}, u32[]{:S(2)}) collective-permute-start(bf16[8,2,10,384]{3,2,1,0:T(8,128)(2,1)S(1)} %get-tuple-element.54), channel_id=1, source_target_pairs={{16,0},{17,1},{18,2},{19,3},{20,4},{21,5},{22,6},{23,7},{24,8},{25... | collective-permute-start | bytes 368648 | tf_op jit(solution)/shard_map/ppermute | solution.py:39
  19.6 2.0 %collective-permute-done.1 = bf16[2,21,8,384]{3,2,1,0:T(8,128)(2,1)S(1)} collective-permute-done((bf16[2,21,8,384]{3,2,1,0:T(8,128)(2,1)S(1)}, bf16[2,21,8,384]{3,2,1,0:T(8,128)(2,1)S(1)}, u32[]{:S(2)}, u32[]{:S(2)}) %collective-permute-start.1) | collective-permute-done | bytes 258080 | tf_op jit(solution)/shard_map/ppermute | solution.py:39
  21.6 0.1 pad_maximum_fusion.1
  21.7 3.4 %collective-permute-done.4 = bf16[8,2,10,384]{3,2,1,0:T(8,128)(2,1)S(1)} collective-permute-done((bf16[8,2,10,384]{3,2,1,0:T(8,128)(2,1)S(1)}, bf16[8,2,10,384]{3,2,1,0:T(8,128)(2,1)S(1)}, u32[]{:S(2)}, u32[]{:S(2)}) %collective-permute-start.4) | collective-permute-done | bytes 122912 | tf_op jit(solution)/shard_map/ppermute | solution.py:39
  25.1 0.3 pad_maximum_fusion
  25.3 2.5 %collective-permute-start.6 = (bf16[2,21,16,384]{3,2,1,0:T(8,128)(2,1)S(1)}, bf16[2,21,16,384]{3,2,1,0:T(8,128)(2,1)S(1)}, u32[]{:S(2)}, u32[]{:S(2)}) collective-permute-start(bf16[2,21,16,384]{3,2,1,0:T(8,128)(2,1)S(1)} %pad_maximum_fusion.1), channel_id=1, source_target_pairs={{14,0},{33,1},{0,2},{35,3},{2,4},{37,5},{4,6},{39,7},{6,8},{41,9},... | collective-permute-start | bytes 1548296 | tf_op jit(solution)/shard_map/ppermute | solution.py:39
  27.8 2.7 %collective-permute-start.5 = (bf16[2,21,16,384]{3,2,1,0:T(8,128)(2,1)S(1)}, bf16[2,21,16,384]{3,2,1,0:T(8,128)(2,1)S(1)}, u32[]{:S(2)}, u32[]{:S(2)}) collective-permute-start(bf16[2,21,16,384]{3,2,1,0:T(8,128)(2,1)S(1)} %pad_maximum_fusion.1), channel_id=1, source_target_pairs={{64,0},{17,1},{66,2},{19,3},{68,4},{21,5},{70,6},{23,7},{72,8},{25... | collective-permute-start | bytes 1548296 | tf_op jit(solution)/shard_map/ppermute | solution.py:39
  30.5 0.1 broadcast_select_fusion
  30.6 5.1 %collective-permute-start.8 = (bf16[8,12,2,384]{3,2,1,0:T(2,128)(2,1)S(1)}, bf16[8,12,2,384]{3,2,1,0:T(2,128)(2,1)S(1)}, u32[]{:S(2)}, u32[]{:S(2)}) collective-permute-start(bf16[8,12,2,384]{3,2,1,0:T(2,128)(2,1)S(1)} %broadcast_select_fusion), channel_id=1, source_target_pairs={{2,1},{1,2},{4,3},{3,4},{6,5},{5,6},{8,7},{7,8},{10,9},{9,10},{12,... | collective-permute-start | bytes 442376 | tf_op jit(solution)/shard_map/ppermute | solution.py:39
  35.7 0.1 fusion.5
  35.8 3.0 %collective-permute-done.8 = bf16[8,12,2,384]{3,2,1,0:T(2,128)(2,1)S(1)} collective-permute-done((bf16[8,12,2,384]{3,2,1,0:T(2,128)(2,1)S(1)}, bf16[8,12,2,384]{3,2,1,0:T(2,128)(2,1)S(1)}, u32[]{:S(2)}, u32[]{:S(2)}) %collective-permute-start.8) | collective-permute-done | bytes 147488 | tf_op jit(solution)/shard_map/ppermute | solution.py:39
  38.8 0.8 maximum_select_fusion.1
  39.7 0.5 copy.12
  40.2 0.1 collective-permute-start.9
  40.3 0.1 fusion.3
  40.4 0.2 collective-permute-done.7
  40.6 0.1 fusion.4
  40.6 0.1 pad_maximum_fusion.3
  40.8 0.0 copy-start.4
  40.8 0.1 fusion.6
  40.9 0.1 pad_maximum_fusion.2
  41.0 1.7 %collective-permute-done.9 = bf16[8,12,12,384]{3,0,2,1:T(8,128)(2,1)S(1)} collective-permute-done((bf16[8,12,12,384]{3,0,2,1:T(8,128)(2,1)S(1)}, bf16[8,12,12,384]{3,0,2,1:T(8,128)(2,1)S(1)}, u32[]{:S(2)}, u32[]{:S(2)}) %collective-permute-start.9) | collective-permute-done | bytes 884768 | tf_op jit(solution)/shard_map/ppermute | solution.py:39
  42.7 2.3 %collective-permute-start.10 = (bf16[2,21,16,384]{3,2,1,0:T(8,128)(2,1)S(1)}, bf16[2,21,16,384]{3,2,1,0:T(8,128)(2,1)S(1)}, u32[]{:S(2)}, u32[]{:S(2)}) collective-permute-start(bf16[2,21,16,384]{3,2,1,0:T(8,128)(2,1)S(1)} %get-tuple-element.31.refs_0_), channel_id=1, source_target_pairs={{16,0},{65,1},{18,2},{67,3},{20,4},{69,5},{22,6},{71,7},{24,8},{73... | collective-permute-start | bytes 1548296 | tf_op jit(solution)/shard_map/ppermute | solution.py:39
  45.0 0.9 collective-permute-start.11
  45.8 2.5 %collective-permute-start.14 = (bf16[2,21,16,384]{3,2,1,0:T(8,128)(2,1)S(1)}, bf16[2,21,16,384]{3,2,1,0:T(8,128)(2,1)S(1)}, u32[]{:S(2)}, u32[]{:S(2)}) collective-permute-start(bf16[2,21,16,384]{3,2,1,0:T(8,128)(2,1)S(1)} %get-tuple-element.32.refs_1_), channel_id=1, source_target_pairs={{16,0},{65,1},{18,2},{67,3},{20,4},{69,5},{22,6},{71,7},{24,8},{73... | collective-permute-start | bytes 1548296 | tf_op jit(solution)/shard_map/ppermute | solution.py:39
  48.3 0.0 collective-permute-start.15
  48.3 0.2 copy.13
  48.5 1.4 %maximum_select_fusion.x_ref = bf16[8,12,24,384]{3,2,1,0:T(8,128)(2,1)S(1)} fusion(bf16[8,12,12,384]{3,2,1,0:T(8,128)(2,1)S(1)} %copy.13, bf16[8,12,12,384]{3,2,1,0:T(8,128)(2,1)S(1)} %maximum_select_fusion.1, pred[]{:T(512)S(6)} %eq.2), kind=kLoop, calls=%fused_computation | loop fusion | flops 7962624 | bytes 3538945 | tf_op jit(solution)/shard_map/jit(_where)/select_n | solution.py:345
  49.9 4.1 %first_layout.1.laid_ref = bf16[6,8,288,256]{3,2,1,0:T(8,128)(2,1)S(1)} custom-call(bf16[8,12,24,384]{3,2,1,0:T(8,128)(2,1)S(1)} %maximum_select_fusion.x_ref, f32[1,384]{1,0:T(1,128)S(1)} %reshape.10.gain_ref), custom_call_target="tpu_custom_call" | custom-call | tf_op jit(solution)/shard_map/first_layout/pallas_call | solution.py:122
  54.0 1.1 %collective-permute-done.11.refs_5_ = bf16[2,21,16,384]{3,2,1,0:T(8,128)(2,1)S(1)} collective-permute-done((bf16[2,21,16,384]{3,2,1,0:T(8,128)(2,1)S(1)}, bf16[2,21,16,384]{3,2,1,0:T(8,128)(2,1)S(1)}, u32[]{:S(2)}, u32[]{:S(2)}) %collective-permute-start.11) | collective-permute-done | bytes 516128 | tf_op jit(solution)/shard_map/ppermute | solution.py:39
  55.1 1.7 %collective-permute-start.12 = (bf16[2,21,16,384]{3,2,1,0:T(8,128)(2,1)S(1)}, bf16[2,21,16,384]{3,2,1,0:T(8,128)(2,1)S(1)}, u32[]{:S(2)}, u32[]{:S(2)}) collective-permute-start(bf16[2,21,16,384]{3,2,1,0:T(8,128)(2,1)S(1)} %collective-permute-done.10.refs_2_), channel_id=1, source_target_pairs={{16,0},{65,1},{18,2},{67,3},{20,4},{69,5},{22,6},{71,7},{24,8},{73... | collective-permute-start | bytes 1548296 | tf_op jit(solution)/shard_map/ppermute | solution.py:39
  56.8 2.7 %collective-permute-start.16 = (bf16[2,21,16,384]{3,2,1,0:T(8,128)(2,1)S(1)}, bf16[2,21,16,384]{3,2,1,0:T(8,128)(2,1)S(1)}, u32[]{:S(2)}, u32[]{:S(2)}) collective-permute-start(bf16[2,21,16,384]{3,2,1,0:T(8,128)(2,1)S(1)} %get-tuple-element.42.refs_0_), channel_id=1, source_target_pairs={{16,0},{65,1},{18,2},{67,3},{20,4},{69,5},{22,6},{71,7},{24,8},{73... | collective-permute-start | bytes 1548296 | tf_op jit(solution)/shard_map/ppermute | solution.py:39
  59.5 0.5 collective-permute-start.17
  60.0 0.6 collective-permute-done.15.refs_4_
  60.6 8.5 %near_conv.2.near_ref = f32[6,240,384]{2,1,0:T(8,128)S(1)} custom-call(bf16[6,8,288,256]{3,2,1,0:T(8,128)(2,1)S(1)} %first_layout.1.laid_ref, bf16[2,21,16,384]{3,2,1,0:T(8,128)(2,1)S(1)} %get-tuple-element.31.refs_0_, bf16[2,21,16,384]{3,2,1,0:T(8,128)(2,1)S(1)} %get-tuple-element.32.refs_1_, bf16[2,21,16,384]{3,2,1,0:T(8,128)(2,1)S(1)} %collective-permute-done.10.refs_2_, ...), custom_call_target="tpu_custom_call" | custom-call | tf_op jit(solution)/shard_map/near_conv/pallas_call | solution.py:217
  69.1 0.0 copy-start.5
  69.1 0.0 copy-start.6
  69.2 0.0 collective-permute-done.16.refs_2_
  69.2 2.6 %collective-permute-done.17.refs_5_ = bf16[2,21,16,384]{3,2,1,0:T(8,128)(2,1)S(1)} collective-permute-done((bf16[2,21,16,384]{3,2,1,0:T(8,128)(2,1)S(1)}, bf16[2,21,16,384]{3,2,1,0:T(8,128)(2,1)S(1)}, u32[]{:S(2)}, u32[]{:S(2)}) %collective-permute-start.17) | collective-permute-done | bytes 516128 | tf_op jit(solution)/shard_map/ppermute | solution.py:39
  71.8 3.0 %first_conv.1 = (f32[6,240,384]{2,1,0:T(8,128)S(1)}, bf16[6,240,384]{2,1,0:T(8,128)(2,1)S(1)}) custom-call(bf16[6,8,288,256]{3,2,1,0:T(8,128)(2,1)S(1)} %first_layout.1.laid_ref, bf16[2,21,16,384]{3,2,1,0:T(8,128)(2,1)S(1)} %collective-permute-done.12.b0, bf16[2,21,16,384]{3,2,1,0:T(8,128)(2,1)S(1)} %collective-permute-done.13.b1, ...), custom_call_target="tpu_custom_call" | custom-call | tf_op jit(solution)/shard_map/first_conv/pallas_call | solution.py:237
  74.7 2.1 %collective-permute-start.18 = (bf16[6,240,384]{2,1,0:T(8,128)(2,1)S(1)}, bf16[6,240,384]{2,1,0:T(8,128)(2,1)S(1)}, u32[]{:S(2)}, u32[]{:S(2)}) collective-permute-start(bf16[6,240,384]{2,1,0:T(8,128)(2,1)S(1)} %get-tuple-element.48), channel_id=1, source_target_pairs={{1,0},{0,1},{3,2},{2,3},{5,4},{4,5},{7,6},{6,7},{9,8},{8,9},{11,10... | collective-permute-start | bytes 3317768 | tf_op jit(solution)/shard_map/ppermute | solution.py:39
  76.8 2.2 %collective-permute-start.21 = (bf16[2,21,16,384]{3,2,1,0:T(8,128)(2,1)S(1)}, bf16[2,21,16,384]{3,2,1,0:T(8,128)(2,1)S(1)}, u32[]{:S(2)}, u32[]{:S(2)}) collective-permute-start(bf16[2,21,16,384]{3,2,1,0:T(8,128)(2,1)S(1)} %get-tuple-element.43.refs_1_), channel_id=1, source_target_pairs={{16,0},{65,1},{18,2},{67,3},{20,4},{69,5},{22,6},{71,7},{24,8},{73... | collective-permute-start | bytes 1548296 | tf_op jit(solution)/shard_map/ppermute | solution.py:39
  79.0 2.7 %collective-permute-start.19 = (bf16[2,21,16,384]{3,2,1,0:T(8,128)(2,1)S(1)}, bf16[2,21,16,384]{3,2,1,0:T(8,128)(2,1)S(1)}, u32[]{:S(2)}, u32[]{:S(2)}) collective-permute-start(bf16[2,21,16,384]{3,2,1,0:T(8,128)(2,1)S(1)} %collective-permute-done.16.refs_2_), channel_id=1, source_target_pairs={{16,0},{65,1},{18,2},{67,3},{20,4},{69,5},{22,6},{71,7},{24,8},{73... | collective-permute-start | bytes 1548296 | tf_op jit(solution)/shard_map/ppermute | solution.py:39
  81.7 0.0 collective-permute-start.20
  81.7 3.0 %second_layout.1.laid_ref = bf16[6,6,240,256]{3,2,1,0:T(8,128)(2,1)S(1)} custom-call(f32[6,240,384]{2,1,0:T(8,128)S(1)} %get-tuple-element.47.mine_ref, bf16[6,240,384]{2,1,0:T(8,128)(2,1)S(1)} %collective-permute-done.18.other_ref, f32[1,384]{1,0:T(1,128)S(1)} %reshape.11.bias_ref, f32[1,384]{1,0:T(1,128)S(1)} %reshape.12.gain_ref), custom_call_target="tpu_custom_call" | custom-call | tf_op jit(solution)/shard_map/second_layout/pallas_call | solution.py:154
  84.8 0.3 collective-permute-done.21.refs_3_
  85.1 3.4 %collective-permute-done.22.refs_4_ = bf16[2,21,16,384]{3,2,1,0:T(8,128)(2,1)S(1)} collective-permute-done((bf16[2,21,16,384]{3,2,1,0:T(8,128)(2,1)S(1)}, bf16[2,21,16,384]{3,2,1,0:T(8,128)(2,1)S(1)}, u32[]{:S(2)}, u32[]{:S(2)}) %collective-permute-start.22) | collective-permute-done | bytes 516128 | tf_op jit(solution)/shard_map/ppermute | solution.py:39
  88.5 4.6 %near_conv.3.near_ref = f32[4,192,384]{2,1,0:T(8,128)S(1)} custom-call(bf16[6,6,240,256]{3,2,1,0:T(8,128)(2,1)S(1)} %second_layout.1.laid_ref, bf16[2,21,16,384]{3,2,1,0:T(8,128)(2,1)S(1)} %get-tuple-element.42.refs_0_, bf16[2,21,16,384]{3,2,1,0:T(8,128)(2,1)S(1)} %get-tuple-element.43.refs_1_, bf16[2,21,16,384]{3,2,1,0:T(8,128)(2,1)S(1)} %collective-permute-done.16.refs_2_, ...), custom_call_target="tpu_custom_call" | custom-call | tf_op jit(solution)/shard_map/near_conv/pallas_call | solution.py:217
  93.1 0.0 copy-start.3
  93.1 0.6 collective-permute-done.20.b1
  93.7 1.8 %second_conv.1 = (f32[4,10,8,384]{3,2,1,0:T(8,128)S(1)}, f32[4,10,8,384]{3,2,1,0:T(8,128)S(1)}) custom-call(bf16[6,6,240,256]{3,2,1,0:T(8,128)(2,1)S(1)} %second_layout.1.laid_ref, bf16[2,21,16,384]{3,2,1,0:T(8,128)(2,1)S(1)} %collective-permute-done.19.b0, bf16[2,21,16,384]{3,2,1,0:T(8,128)(2,1)S(1)} %collective-permute-done.20.b1, ...), custom_call_target="tpu_custom_call" | custom-call | tf_op jit(solution)/shard_map/second_conv/pallas_call | solution.py:266
  95.6 0.1 collective-permute-start.23
  95.7 1.9 %collective-permute-done.23 = f32[4,10,8,384]{3,2,1,0:T(8,128)S(1)} collective-permute-done((f32[4,10,8,384]{3,2,1,0:T(8,128)S(1)}, f32[4,10,8,384]{3,2,1,0:T(8,128)S(1)}, u32[]{:S(2)}, u32[]{:S(2)}) %collective-permute-start.23) | collective-permute-done | bytes 491552 | tf_op jit(solution)/shard_map/ppermute | solution.py:39
  97.5 0.8 fusion.1
  (26 shorter events, 0.1 us)
Async XLA Ops:
  0.0 15.0 %copy-start.2 = (bf16[4,8,10,384]{3,1,2,0:T(8,128)(2,1)S(1)}, bf16[4,8,10,384]{3,1,2,0:T(8,128)(2,1)}, u32[]{:S(2)}) copy-start(bf16[4,8,10,384]{3,1,2,0:T(8,128)(2,1)} %param.7) | copy-start | bytes 737284
  1.1 13.9 %collective-permute-start.2 = (bf16[4,8,10,384]{3,2,1,0:T(8,128)(2,1)S(1)}, bf16[4,8,10,384]{3,2,1,0:T(8,128)(2,1)S(1)}, u32[]{:S(2)}, u32[]{:S(2)}) collective-permute-start(bf16[4,8,10,384]{3,2,1,0:T(8,128)(2,1)S(1)} %copy.10), channel_id=1, source_target_pairs={{0,64},{1,65},{2,66},{3,67},{4,68},{5,69},{6,70},{7,71},{8,72},{9,... | collective-permute-start | bytes 737288 | tf_op jit(solution)/shard_map/ppermute | solution.py:39
  5.1 0.9 copy-start
  6.0 0.9 copy-start.1
  7.3 12.3 %collective-permute-start = (bf16[2,21,8,384]{3,2,1,0:T(8,128)(2,1)S(1)}, bf16[2,21,8,384]{3,2,1,0:T(8,128)(2,1)S(1)}, u32[]{:S(2)}, u32[]{:S(2)}) collective-permute-start(bf16[2,21,8,384]{3,2,1,0:T(8,128)(2,1)S(1)} %fold.1), channel_id=1, source_target_pairs={{0,0},{1,1},{2,2},{3,3},{4,4},{5,5},{6,6},{7,7},{8,8},{9,9},{10,10... | collective-permute-start | bytes 774152 | tf_op jit(solution)/shard_map/ppermute | solution.py:39
  8.0 13.6 %collective-permute-start.1 = (bf16[2,21,8,384]{3,2,1,0:T(8,128)(2,1)S(1)}, bf16[2,21,8,384]{3,2,1,0:T(8,128)(2,1)S(1)}, u32[]{:S(2)}, u32[]{:S(2)}) collective-permute-start(bf16[2,21,8,384]{3,2,1,0:T(8,128)(2,1)S(1)} %fold.1), channel_id=1, source_target_pairs={{8,0},{9,1},{10,2},{11,3},{12,4},{13,5},{14,6},{15,7},{0,8},{1,9},... | collective-permute-start | bytes 774152 | tf_op jit(solution)/shard_map/ppermute | solution.py:39
  15.2 6.5 %collective-permute-start.3 = (bf16[8,2,10,384]{3,2,1,0:T(8,128)(2,1)S(1)}, bf16[8,2,10,384]{3,2,1,0:T(8,128)(2,1)S(1)}, u32[]{:S(2)}, u32[]{:S(2)}) collective-permute-start(bf16[8,2,10,384]{3,2,1,0:T(8,128)(2,1)S(1)} %get-tuple-element.53), channel_id=1, source_target_pairs={{0,16},{1,17},{2,18},{3,19},{4,20},{5,21},{6,22},{7,23},{8,24},{9,... | collective-permute-start | bytes 368648 | tf_op jit(solution)/shard_map/ppermute | solution.py:39
  18.3 6.8 %collective-permute-start.4 = (bf16[8,2,10,384]{3,2,1,0:T(8,128)(2,1)S(1)}, bf16[8,2,10,384]{3,2,1,0:T(8,128)(2,1)S(1)}, u32[]{:S(2)}, u32[]{:S(2)}) collective-permute-start(bf16[8,2,10,384]{3,2,1,0:T(8,128)(2,1)S(1)} %get-tuple-element.54), channel_id=1, source_target_pairs={{16,0},{17,1},{18,2},{19,3},{20,4},{21,5},{22,6},{23,7},{24,8},{25... | collective-permute-start | bytes 368648 | tf_op jit(solution)/shard_map/ppermute | solution.py:39
  25.3 15.0 %collective-permute-start.6 = (bf16[2,21,16,384]{3,2,1,0:T(8,128)(2,1)S(1)}, bf16[2,21,16,384]{3,2,1,0:T(8,128)(2,1)S(1)}, u32[]{:S(2)}, u32[]{:S(2)}) collective-permute-start(bf16[2,21,16,384]{3,2,1,0:T(8,128)(2,1)S(1)} %pad_maximum_fusion.1), channel_id=1, source_target_pairs={{14,0},{33,1},{0,2},{35,3},{2,4},{37,5},{4,6},{39,7},{6,8},{41,9},... | collective-permute-start | bytes 1548296 | tf_op jit(solution)/shard_map/ppermute | solution.py:39
  27.8 12.7 %collective-permute-start.7 = (bf16[2,21,16,384]{3,2,1,0:T(8,128)(2,1)S(1)}, bf16[2,21,16,384]{3,2,1,0:T(8,128)(2,1)S(1)}, u32[]{:S(2)}, u32[]{:S(2)}) collective-permute-start(bf16[2,21,16,384]{3,2,1,0:T(8,128)(2,1)S(1)} %pad_maximum_fusion.1), channel_id=1, source_target_pairs={{192,0},{49,1},{194,2},{51,3},{196,4},{53,5},{198,6},{55,7},{200,8... | collective-permute-start | bytes 1548296 | tf_op jit(solution)/shard_map/ppermute | solution.py:39
  27.8 12.9 %collective-permute-start.5 = (bf16[2,21,16,384]{3,2,1,0:T(8,128)(2,1)S(1)}, bf16[2,21,16,384]{3,2,1,0:T(8,128)(2,1)S(1)}, u32[]{:S(2)}, u32[]{:S(2)}) collective-permute-start(bf16[2,21,16,384]{3,2,1,0:T(8,128)(2,1)S(1)} %pad_maximum_fusion.1), channel_id=1, source_target_pairs={{64,0},{17,1},{66,2},{19,3},{68,4},{21,5},{70,6},{23,7},{72,8},{25... | collective-permute-start | bytes 1548296 | tf_op jit(solution)/shard_map/ppermute | solution.py:39
  30.6 8.2 %collective-permute-start.8 = (bf16[8,12,2,384]{3,2,1,0:T(2,128)(2,1)S(1)}, bf16[8,12,2,384]{3,2,1,0:T(2,128)(2,1)S(1)}, u32[]{:S(2)}, u32[]{:S(2)}) collective-permute-start(bf16[8,12,2,384]{3,2,1,0:T(2,128)(2,1)S(1)} %broadcast_select_fusion), channel_id=1, source_target_pairs={{2,1},{1,2},{4,3},{3,4},{6,5},{5,6},{8,7},{7,8},{10,9},{9,10},{12,... | collective-permute-start | bytes 442376 | tf_op jit(solution)/shard_map/ppermute | solution.py:39
  40.2 2.5 %collective-permute-start.9 = (bf16[8,12,12,384]{3,0,2,1:T(8,128)(2,1)S(1)}, bf16[8,12,12,384]{3,0,2,1:T(8,128)(2,1)S(1)}, u32[]{:S(2)}, u32[]{:S(2)}) collective-permute-start(bf16[8,12,12,384]{3,0,2,1:T(8,128)(2,1)S(1)} %copy.12), channel_id=1, source_target_pairs={{1,0},{0,1},{3,2},{2,3},{5,4},{4,5},{7,6},{6,7},{9,8},{8,9},{11,10... | collective-permute-start | bytes 2654216 | tf_op jit(solution)/shard_map/ppermute | solution.py:39
  40.8 7.5 %copy-start.4 = (f32[384]{0:T(512)S(1)}, f32[384]{0:T(512)}, u32[]{:S(2)}) copy-start(f32[384]{0:T(512)} %param.8) | copy-start | bytes 4612
  42.7 11.3 %collective-permute-start.10 = (bf16[2,21,16,384]{3,2,1,0:T(8,128)(2,1)S(1)}, bf16[2,21,16,384]{3,2,1,0:T(8,128)(2,1)S(1)}, u32[]{:S(2)}, u32[]{:S(2)}) collective-permute-start(bf16[2,21,16,384]{3,2,1,0:T(8,128)(2,1)S(1)} %get-tuple-element.31.refs_0_), channel_id=1, source_target_pairs={{16,0},{65,1},{18,2},{67,3},{20,4},{69,5},{22,6},{71,7},{24,8},{73... | collective-permute-start | bytes 1548296 | tf_op jit(solution)/shard_map/ppermute | solution.py:39
  45.0 10.1 %collective-permute-start.11 = (bf16[2,21,16,384]{3,2,1,0:T(8,128)(2,1)S(1)}, bf16[2,21,16,384]{3,2,1,0:T(8,128)(2,1)S(1)}, u32[]{:S(2)}, u32[]{:S(2)}) collective-permute-start(bf16[2,21,16,384]{3,2,1,0:T(8,128)(2,1)S(1)} %get-tuple-element.32.refs_1_), channel_id=1, source_target_pairs={{48,0},{193,1},{50,2},{195,3},{52,4},{197,5},{54,6},{199,7},{56,8}... | collective-permute-start | bytes 1548296 | tf_op jit(solution)/shard_map/ppermute | solution.py:39
  45.8 13.6 %collective-permute-start.14 = (bf16[2,21,16,384]{3,2,1,0:T(8,128)(2,1)S(1)}, bf16[2,21,16,384]{3,2,1,0:T(8,128)(2,1)S(1)}, u32[]{:S(2)}, u32[]{:S(2)}) collective-permute-start(bf16[2,21,16,384]{3,2,1,0:T(8,128)(2,1)S(1)} %get-tuple-element.32.refs_1_), channel_id=1, source_target_pairs={{16,0},{65,1},{18,2},{67,3},{20,4},{69,5},{22,6},{71,7},{24,8},{73... | collective-permute-start | bytes 1548296 | tf_op jit(solution)/shard_map/ppermute | solution.py:39
  48.3 12.3 %collective-permute-start.15 = (bf16[2,21,16,384]{3,2,1,0:T(8,128)(2,1)S(1)}, bf16[2,21,16,384]{3,2,1,0:T(8,128)(2,1)S(1)}, u32[]{:S(2)}, u32[]{:S(2)}) collective-permute-start(bf16[2,21,16,384]{3,2,1,0:T(8,128)(2,1)S(1)} %get-tuple-element.31.refs_0_), channel_id=1, source_target_pairs={{48,0},{193,1},{50,2},{195,3},{52,4},{197,5},{54,6},{199,7},{56,8}... | collective-permute-start | bytes 1548296 | tf_op jit(solution)/shard_map/ppermute | solution.py:39
  55.1 14.1 %collective-permute-start.12 = (bf16[2,21,16,384]{3,2,1,0:T(8,128)(2,1)S(1)}, bf16[2,21,16,384]{3,2,1,0:T(8,128)(2,1)S(1)}, u32[]{:S(2)}, u32[]{:S(2)}) collective-permute-start(bf16[2,21,16,384]{3,2,1,0:T(8,128)(2,1)S(1)} %collective-permute-done.10.refs_2_), channel_id=1, source_target_pairs={{16,0},{65,1},{18,2},{67,3},{20,4},{69,5},{22,6},{71,7},{24,8},{73... | collective-permute-start | bytes 1548296 | tf_op jit(solution)/shard_map/ppermute | solution.py:39
  56.8 12.4 %collective-permute-start.13 = (bf16[2,21,16,384]{3,2,1,0:T(8,128)(2,1)S(1)}, bf16[2,21,16,384]{3,2,1,0:T(8,128)(2,1)S(1)}, u32[]{:S(2)}, u32[]{:S(2)}) collective-permute-start(bf16[2,21,16,384]{3,2,1,0:T(8,128)(2,1)S(1)} %collective-permute-done.11.refs_5_), channel_id=1, source_target_pairs={{48,0},{193,1},{50,2},{195,3},{52,4},{197,5},{54,6},{199,7},{56,8}... | collective-permute-start | bytes 1548296 | tf_op jit(solution)/shard_map/ppermute | solution.py:39
  56.8 12.4 %collective-permute-start.16 = (bf16[2,21,16,384]{3,2,1,0:T(8,128)(2,1)S(1)}, bf16[2,21,16,384]{3,2,1,0:T(8,128)(2,1)S(1)}, u32[]{:S(2)}, u32[]{:S(2)}) collective-permute-start(bf16[2,21,16,384]{3,2,1,0:T(8,128)(2,1)S(1)} %get-tuple-element.42.refs_0_), channel_id=1, source_target_pairs={{16,0},{65,1},{18,2},{67,3},{20,4},{69,5},{22,6},{71,7},{24,8},{73... | collective-permute-start | bytes 1548296 | tf_op jit(solution)/shard_map/ppermute | solution.py:39
  59.5 12.3 %collective-permute-start.17 = (bf16[2,21,16,384]{3,2,1,0:T(8,128)(2,1)S(1)}, bf16[2,21,16,384]{3,2,1,0:T(8,128)(2,1)S(1)}, u32[]{:S(2)}, u32[]{:S(2)}) collective-permute-start(bf16[2,21,16,384]{3,2,1,0:T(8,128)(2,1)S(1)} %get-tuple-element.43.refs_1_), channel_id=1, source_target_pairs={{48,0},{193,1},{50,2},{195,3},{52,4},{197,5},{54,6},{199,7},{56,8}... | collective-permute-start | bytes 1548296 | tf_op jit(solution)/shard_map/ppermute | solution.py:39
  69.1 12.6 %copy-start.5 = (f32[384]{0:T(512)S(1)}, f32[384]{0:T(512)}, u32[]{:S(2)}) copy-start(f32[384]{0:T(512)} %param.10) | copy-start | bytes 4612
  69.1 12.6 %copy-start.6 = (f32[384]{0:T(512)S(1)}, f32[384]{0:T(512)}, u32[]{:S(2)}) copy-start(f32[384]{0:T(512)} %param.11) | copy-start | bytes 4612
  74.7 7.0 %collective-permute-start.18 = (bf16[6,240,384]{2,1,0:T(8,128)(2,1)S(1)}, bf16[6,240,384]{2,1,0:T(8,128)(2,1)S(1)}, u32[]{:S(2)}, u32[]{:S(2)}) collective-permute-start(bf16[6,240,384]{2,1,0:T(8,128)(2,1)S(1)} %get-tuple-element.48), channel_id=1, source_target_pairs={{1,0},{0,1},{3,2},{2,3},{5,4},{4,5},{7,6},{6,7},{9,8},{8,9},{11,10... | collective-permute-start | bytes 3317768 | tf_op jit(solution)/shard_map/ppermute | solution.py:39
  76.8 8.2 %collective-permute-start.21 = (bf16[2,21,16,384]{3,2,1,0:T(8,128)(2,1)S(1)}, bf16[2,21,16,384]{3,2,1,0:T(8,128)(2,1)S(1)}, u32[]{:S(2)}, u32[]{:S(2)}) collective-permute-start(bf16[2,21,16,384]{3,2,1,0:T(8,128)(2,1)S(1)} %get-tuple-element.43.refs_1_), channel_id=1, source_target_pairs={{16,0},{65,1},{18,2},{67,3},{20,4},{69,5},{22,6},{71,7},{24,8},{73... | collective-permute-start | bytes 1548296 | tf_op jit(solution)/shard_map/ppermute | solution.py:39
  79.0 9.4 %collective-permute-start.22 = (bf16[2,21,16,384]{3,2,1,0:T(8,128)(2,1)S(1)}, bf16[2,21,16,384]{3,2,1,0:T(8,128)(2,1)S(1)}, u32[]{:S(2)}, u32[]{:S(2)}) collective-permute-start(bf16[2,21,16,384]{3,2,1,0:T(8,128)(2,1)S(1)} %get-tuple-element.42.refs_0_), channel_id=1, source_target_pairs={{48,0},{193,1},{50,2},{195,3},{52,4},{197,5},{54,6},{199,7},{56,8}... | collective-permute-start | bytes 1548296 | tf_op jit(solution)/shard_map/ppermute | solution.py:39
  79.0 14.1 %collective-permute-start.19 = (bf16[2,21,16,384]{3,2,1,0:T(8,128)(2,1)S(1)}, bf16[2,21,16,384]{3,2,1,0:T(8,128)(2,1)S(1)}, u32[]{:S(2)}, u32[]{:S(2)}) collective-permute-start(bf16[2,21,16,384]{3,2,1,0:T(8,128)(2,1)S(1)} %collective-permute-done.16.refs_2_), channel_id=1, source_target_pairs={{16,0},{65,1},{18,2},{67,3},{20,4},{69,5},{22,6},{71,7},{24,8},{73... | collective-permute-start | bytes 1548296 | tf_op jit(solution)/shard_map/ppermute | solution.py:39
  81.7 12.0 %collective-permute-start.20 = (bf16[2,21,16,384]{3,2,1,0:T(8,128)(2,1)S(1)}, bf16[2,21,16,384]{3,2,1,0:T(8,128)(2,1)S(1)}, u32[]{:S(2)}, u32[]{:S(2)}) collective-permute-start(bf16[2,21,16,384]{3,2,1,0:T(8,128)(2,1)S(1)} %collective-permute-done.17.refs_5_), channel_id=1, source_target_pairs={{48,0},{193,1},{50,2},{195,3},{52,4},{197,5},{54,6},{199,7},{56,8}... | collective-permute-start | bytes 1548296 | tf_op jit(solution)/shard_map/ppermute | solution.py:39
  93.1 4.4 %copy-start.3 = (f32[384]{0:T(512)S(1)}, f32[384]{0:T(512)}, u32[]{:S(2)}) copy-start(f32[384]{0:T(512)} %param.13) | copy-start | bytes 4612
  95.6 2.0 %collective-permute-start.23 = (f32[4,10,8,384]{3,2,1,0:T(8,128)S(1)}, f32[4,10,8,384]{3,2,1,0:T(8,128)S(1)}, u32[]{:S(2)}, u32[]{:S(2)}) collective-permute-start(f32[4,10,8,384]{3,2,1,0:T(8,128)S(1)} %get-tuple-element.52), channel_id=1, source_target_pairs={{1,0},{0,1},{3,2},{2,3},{5,4},{4,5},{7,6},{6,7},{9,8},{8,9},{11,10... | collective-permute-start | bytes 1474568 | tf_op jit(solution)/shard_map/ppermute | solution.py:39

commit v7 on v6

--- a/solution.py
+++ b/solution.py
@@ -258,7 +258,7 @@
         for w in range(10):
             at = 192 * f + w
             mine_ref[f, w] = take(total_ref, at + own, 8, 24)
-            sent_ref[f, w] = take(total_ref, at + 10 - own, 8, 24)
+            sent_ref[f, w] = take(total_ref, at + 10 - own, 8, 24).astype(BF)
 
 
 def second_conv(laid, blocks, near):
@@ -268,7 +268,7 @@
         grid=(2,),
         out_shape=(
             jax.ShapeDtypeStruct((4, 10, 8, CHANS), F32),
-            jax.ShapeDtypeStruct((4, 10, 8, CHANS), F32),
+            jax.ShapeDtypeStruct((4, 10, 8, CHANS), BF),
         ),
         in_specs=[whole] * 3 + [pl.BlockSpec((2, 8 * 24, CHANS), lambda f: (f, 0, 0))],
         out_specs=(out, out),
@@ -374,7 +374,7 @@
         near = near_conv(laid, in_order(two, *next_ends, *next_rest), 4, 8 * 24)
         mine, passed = second_conv(laid, far, near)
         own = jnp.transpose(features, (0, 2, 1, 3)).astype(F32)
-        total = mine + swapped(passed) + bias_2 + own
+        total = mine + swapped(passed).astype(F32) + bias_2 + own
         return jnp.transpose(total.astype(BF), (0, 2, 1, 3))
 
     volume = P("t", "h", ("z", "c"), None)

time: 98.6 us -> 98.2 us (level)
  no operation moved by 1% of the time
where the time goes in v7:
time: 98.2 us; the launch traced here: 98 us
  starting transfers between devices  44.1 us (45%)
  Pallas kernels  25.4 us (26%)
  waiting for transfers between devices  20.4 us (21%)
  local copies, waits for them, and re-layouts  3.99 us (4%)
  other arithmetic  3.76 us (4%)
    ppermute x24, starting transfers between devices, move(): return lax.ppermute(x, AXES, pairs)  44.1 us
    ppermute x24, waiting for transfers between devices, move(): return lax.ppermute(x, AXES, pairs)  20.4 us
    pallas_call x2, Pallas kernels, near_conv(): pl.pallas_call(functools.partial(near_kernel, frames, count), grid=(frame...  13.1 us
    pallas_call x1, Pallas kernels, first_layout(): pl.pallas_call(first_layout_kernel, grid=(8,), out_shape=jax.ShapeDtypeSt...  4.06 us
    pallas_call x1, Pallas kernels, second_layout(): pl.pallas_call(second_layout_kernel, grid=(6,), out_shape=jax.ShapeDtypeS...  3.01 us
    pallas_call x1, Pallas kernels, first_conv(): pl.pallas_call(first_conv_kernel, grid=(3,), out_shape=(jax.ShapeDtypeStr...  2.97 us
    unnamed x16, local copies, waits for them, and re-layouts  2.95 us
  transfers between devices with their start and end apart: 24, of which 12 were waited for; matrix products, arithmetic and copies ran while one was open for 4% of the time, Pallas kernels for 21%

profile of v7, /device:TPU:1, one launch (start us, length us, event | category | flops | bytes accessed | tf_op | source)
XLA Modules:
  0.0 98.0 jit_solution(1301704593706865736)
XLA Ops:
  0.0 1.1 %copy.10 = bf16[4,8,10,384]{3,2,1,0:T(8,128)(2,1)S(1)} copy(bf16[4,8,10,384]{3,1,2,0:T(8,128)(2,1)} %param.7) | data formatting | bytes 491520 | tf_op args[0]
  1.1 4.1 %collective-permute-start.2 = (bf16[4,8,10,384]{3,2,1,0:T(8,128)(2,1)S(1)}, bf16[4,8,10,384]{3,2,1,0:T(8,128)(2,1)S(1)}, u32[]{:S(2)}, u32[]{:S(2)}) collective-permute-start(bf16[4,8,10,384]{3,2,1,0:T(8,128)(2,1)S(1)} %copy.10), channel_id=1, source_target_pairs={{0,64},{1,65},{2,66},{3,67},{4,68},{5,69},{6,70},{7,71},{8,72},{9,... | collective-permute-start | bytes 737288 | tf_op jit(solution)/shard_map/ppermute | solution.py:39
  5.1 0.0 copy-start
  5.1 0.9 copy-done
  6.1 0.9 copy-done.1
  7.0 0.3 fold.1
  7.3 0.7 collective-permute-start
  8.0 7.0 %collective-permute-start.1 = (bf16[2,21,8,384]{3,2,1,0:T(8,128)(2,1)S(1)}, bf16[2,21,8,384]{3,2,1,0:T(8,128)(2,1)S(1)}, u32[]{:S(2)}, u32[]{:S(2)}) collective-permute-start(bf16[2,21,8,384]{3,2,1,0:T(8,128)(2,1)S(1)} %fold.1), channel_id=1, source_target_pairs={{8,0},{9,1},{10,2},{11,3},{12,4},{13,5},{14,6},{15,7},{0,8},{1,9},... | collective-permute-start | bytes 774152 | tf_op jit(solution)/shard_map/ppermute | solution.py:39
  15.0 0.1 copy_dynamic-update-slice_fusion
  15.2 3.1 %collective-permute-start.3 = (bf16[8,2,10,384]{3,2,1,0:T(8,128)(2,1)S(1)}, bf16[8,2,10,384]{3,2,1,0:T(8,128)(2,1)S(1)}, u32[]{:S(2)}, u32[]{:S(2)}) collective-permute-start(bf16[8,2,10,384]{3,2,1,0:T(8,128)(2,1)S(1)} %get-tuple-element.53), channel_id=1, source_target_pairs={{0,16},{1,17},{2,18},{3,19},{4,20},{5,21},{6,22},{7,23},{8,24},{9,... | collective-permute-start | bytes 368648 | tf_op jit(solution)/shard_map/ppermute | solution.py:39
  18.3 1.3 %collective-permute-start.4 = (bf16[8,2,10,384]{3,2,1,0:T(8,128)(2,1)S(1)}, bf16[8,2,10,384]{3,2,1,0:T(8,128)(2,1)S(1)}, u32[]{:S(2)}, u32[]{:S(2)}) collective-permute-start(bf16[8,2,10,384]{3,2,1,0:T(8,128)(2,1)S(1)} %get-tuple-element.54), channel_id=1, source_target_pairs={{16,0},{17,1},{18,2},{19,3},{20,4},{21,5},{22,6},{23,7},{24,8},{25... | collective-permute-start | bytes 368648 | tf_op jit(solution)/shard_map/ppermute | solution.py:39
  19.6 2.0 %collective-permute-done.1 = bf16[2,21,8,384]{3,2,1,0:T(8,128)(2,1)S(1)} collective-permute-done((bf16[2,21,8,384]{3,2,1,0:T(8,128)(2,1)S(1)}, bf16[2,21,8,384]{3,2,1,0:T(8,128)(2,1)S(1)}, u32[]{:S(2)}, u32[]{:S(2)}) %collective-permute-start.1) | collective-permute-done | bytes 258080 | tf_op jit(solution)/shard_map/ppermute | solution.py:39
  21.6 0.1 pad_maximum_fusion.1
  21.7 3.4 %collective-permute-done.4 = bf16[8,2,10,384]{3,2,1,0:T(8,128)(2,1)S(1)} collective-permute-done((bf16[8,2,10,384]{3,2,1,0:T(8,128)(2,1)S(1)}, bf16[8,2,10,384]{3,2,1,0:T(8,128)(2,1)S(1)}, u32[]{:S(2)}, u32[]{:S(2)}) %collective-permute-start.4) | collective-permute-done | bytes 122912 | tf_op jit(solution)/shard_map/ppermute | solution.py:39
  25.1 0.3 pad_maximum_fusion
  25.3 2.5 %collective-permute-start.6 = (bf16[2,21,16,384]{3,2,1,0:T(8,128)(2,1)S(1)}, bf16[2,21,16,384]{3,2,1,0:T(8,128)(2,1)S(1)}, u32[]{:S(2)}, u32[]{:S(2)}) collective-permute-start(bf16[2,21,16,384]{3,2,1,0:T(8,128)(2,1)S(1)} %pad_maximum_fusion.1), channel_id=1, source_target_pairs={{14,0},{33,1},{0,2},{35,3},{2,4},{37,5},{4,6},{39,7},{6,8},{41,9},... | collective-permute-start | bytes 1548296 | tf_op jit(solution)/shard_map/ppermute | solution.py:39
  27.8 2.7 %collective-permute-start.5 = (bf16[2,21,16,384]{3,2,1,0:T(8,128)(2,1)S(1)}, bf16[2,21,16,384]{3,2,1,0:T(8,128)(2,1)S(1)}, u32[]{:S(2)}, u32[]{:S(2)}) collective-permute-start(bf16[2,21,16,384]{3,2,1,0:T(8,128)(2,1)S(1)} %pad_maximum_fusion.1), channel_id=1, source_target_pairs={{64,0},{17,1},{66,2},{19,3},{68,4},{21,5},{70,6},{23,7},{72,8},{25... | collective-permute-start | bytes 1548296 | tf_op jit(solution)/shard_map/ppermute | solution.py:39
  30.5 0.1 broadcast_select_fusion
  30.6 5.1 %collective-permute-start.8 = (bf16[8,12,2,384]{3,2,1,0:T(2,128)(2,1)S(1)}, bf16[8,12,2,384]{3,2,1,0:T(2,128)(2,1)S(1)}, u32[]{:S(2)}, u32[]{:S(2)}) collective-permute-start(bf16[8,12,2,384]{3,2,1,0:T(2,128)(2,1)S(1)} %broadcast_select_fusion), channel_id=1, source_target_pairs={{2,1},{1,2},{4,3},{3,4},{6,5},{5,6},{8,7},{7,8},{10,9},{9,10},{12,... | collective-permute-start | bytes 442376 | tf_op jit(solution)/shard_map/ppermute | solution.py:39
  35.7 0.1 fusion.5
  35.8 3.0 %collective-permute-done.8 = bf16[8,12,2,384]{3,2,1,0:T(2,128)(2,1)S(1)} collective-permute-done((bf16[8,12,2,384]{3,2,1,0:T(2,128)(2,1)S(1)}, bf16[8,12,2,384]{3,2,1,0:T(2,128)(2,1)S(1)}, u32[]{:S(2)}, u32[]{:S(2)}) %collective-permute-start.8) | collective-permute-done | bytes 147488 | tf_op jit(solution)/shard_map/ppermute | solution.py:39
  38.8 0.8 maximum_select_fusion.1
  39.7 0.5 copy.12
  40.2 0.1 collective-permute-start.9
  40.3 0.1 fusion.3
  40.4 0.2 collective-permute-done.7
  40.6 0.1 fusion.4
  40.6 0.1 pad_maximum_fusion.3
  40.8 0.0 copy-start.4
  40.8 0.1 fusion.6
  40.9 0.1 pad_maximum_fusion.2
  41.0 1.7 %collective-permute-done.9 = bf16[8,12,12,384]{3,0,2,1:T(8,128)(2,1)S(1)} collective-permute-done((bf16[8,12,12,384]{3,0,2,1:T(8,128)(2,1)S(1)}, bf16[8,12,12,384]{3,0,2,1:T(8,128)(2,1)S(1)}, u32[]{:S(2)}, u32[]{:S(2)}) %collective-permute-start.9) | collective-permute-done | bytes 884768 | tf_op jit(solution)/shard_map/ppermute | solution.py:39
  42.7 2.3 %collective-permute-start.10 = (bf16[2,21,16,384]{3,2,1,0:T(8,128)(2,1)S(1)}, bf16[2,21,16,384]{3,2,1,0:T(8,128)(2,1)S(1)}, u32[]{:S(2)}, u32[]{:S(2)}) collective-permute-start(bf16[2,21,16,384]{3,2,1,0:T(8,128)(2,1)S(1)} %get-tuple-element.31.refs_0_), channel_id=1, source_target_pairs={{16,0},{65,1},{18,2},{67,3},{20,4},{69,5},{22,6},{71,7},{24,8},{73... | collective-permute-start | bytes 1548296 | tf_op jit(solution)/shard_map/ppermute | solution.py:39
  45.0 0.9 collective-permute-start.11
  45.8 2.5 %collective-permute-start.14 = (bf16[2,21,16,384]{3,2,1,0:T(8,128)(2,1)S(1)}, bf16[2,21,16,384]{3,2,1,0:T(8,128)(2,1)S(1)}, u32[]{:S(2)}, u32[]{:S(2)}) collective-permute-start(bf16[2,21,16,384]{3,2,1,0:T(8,128)(2,1)S(1)} %get-tuple-element.32.refs_1_), channel_id=1, source_target_pairs={{16,0},{65,1},{18,2},{67,3},{20,4},{69,5},{22,6},{71,7},{24,8},{73... | collective-permute-start | bytes 1548296 | tf_op jit(solution)/shard_map/ppermute | solution.py:39
  48.3 0.0 collective-permute-start.15
  48.3 0.2 copy.13
  48.5 1.4 %maximum_select_fusion.x_ref = bf16[8,12,24,384]{3,2,1,0:T(8,128)(2,1)S(1)} fusion(bf16[8,12,12,384]{3,2,1,0:T(8,128)(2,1)S(1)} %copy.13, bf16[8,12,12,384]{3,2,1,0:T(8,128)(2,1)S(1)} %maximum_select_fusion.1, pred[]{:T(512)S(6)} %eq.2), kind=kLoop, calls=%fused_computation | loop fusion | flops 7962624 | bytes 3538945 | tf_op jit(solution)/shard_map/jit(_where)/select_n | solution.py:345
  49.9 4.1 %first_layout.1.laid_ref = bf16[6,8,288,256]{3,2,1,0:T(8,128)(2,1)S(1)} custom-call(bf16[8,12,24,384]{3,2,1,0:T(8,128)(2,1)S(1)} %maximum_select_fusion.x_ref, f32[1,384]{1,0:T(1,128)S(1)} %reshape.10.gain_ref), custom_call_target="tpu_custom_call" | custom-call | tf_op jit(solution)/shard_map/first_layout/pallas_call | solution.py:122
  54.0 1.1 %collective-permute-done.11.refs_5_ = bf16[2,21,16,384]{3,2,1,0:T(8,128)(2,1)S(1)} collective-permute-done((bf16[2,21,16,384]{3,2,1,0:T(8,128)(2,1)S(1)}, bf16[2,21,16,384]{3,2,1,0:T(8,128)(2,1)S(1)}, u32[]{:S(2)}, u32[]{:S(2)}) %collective-permute-start.11) | collective-permute-done | bytes 516128 | tf_op jit(solution)/shard_map/ppermute | solution.py:39
  55.1 1.7 %collective-permute-start.12 = (bf16[2,21,16,384]{3,2,1,0:T(8,128)(2,1)S(1)}, bf16[2,21,16,384]{3,2,1,0:T(8,128)(2,1)S(1)}, u32[]{:S(2)}, u32[]{:S(2)}) collective-permute-start(bf16[2,21,16,384]{3,2,1,0:T(8,128)(2,1)S(1)} %collective-permute-done.10.refs_2_), channel_id=1, source_target_pairs={{16,0},{65,1},{18,2},{67,3},{20,4},{69,5},{22,6},{71,7},{24,8},{73... | collective-permute-start | bytes 1548296 | tf_op jit(solution)/shard_map/ppermute | solution.py:39
  56.8 2.7 %collective-permute-start.16 = (bf16[2,21,16,384]{3,2,1,0:T(8,128)(2,1)S(1)}, bf16[2,21,16,384]{3,2,1,0:T(8,128)(2,1)S(1)}, u32[]{:S(2)}, u32[]{:S(2)}) collective-permute-start(bf16[2,21,16,384]{3,2,1,0:T(8,128)(2,1)S(1)} %get-tuple-element.42.refs_0_), channel_id=1, source_target_pairs={{16,0},{65,1},{18,2},{67,3},{20,4},{69,5},{22,6},{71,7},{24,8},{73... | collective-permute-start | bytes 1548296 | tf_op jit(solution)/shard_map/ppermute | solution.py:39
  59.5 0.5 collective-permute-start.17
  60.0 0.6 collective-permute-done.15.refs_4_
  60.6 8.5 %near_conv.2.near_ref = f32[6,240,384]{2,1,0:T(8,128)S(1)} custom-call(bf16[6,8,288,256]{3,2,1,0:T(8,128)(2,1)S(1)} %first_layout.1.laid_ref, bf16[2,21,16,384]{3,2,1,0:T(8,128)(2,1)S(1)} %get-tuple-element.31.refs_0_, bf16[2,21,16,384]{3,2,1,0:T(8,128)(2,1)S(1)} %get-tuple-element.32.refs_1_, bf16[2,21,16,384]{3,2,1,0:T(8,128)(2,1)S(1)} %collective-permute-done.10.refs_2_, ...), custom_call_target="tpu_custom_call" | custom-call | tf_op jit(solution)/shard_map/near_conv/pallas_call | solution.py:217
  69.1 0.0 copy-start.5
  69.1 0.0 copy-start.6
  69.2 0.0 collective-permute-done.16.refs_2_
  69.2 2.6 %collective-permute-done.17.refs_5_ = bf16[2,21,16,384]{3,2,1,0:T(8,128)(2,1)S(1)} collective-permute-done((bf16[2,21,16,384]{3,2,1,0:T(8,128)(2,1)S(1)}, bf16[2,21,16,384]{3,2,1,0:T(8,128)(2,1)S(1)}, u32[]{:S(2)}, u32[]{:S(2)}) %collective-permute-start.17) | collective-permute-done | bytes 516128 | tf_op jit(solution)/shard_map/ppermute | solution.py:39
  71.8 3.0 %first_conv.1 = (f32[6,240,384]{2,1,0:T(8,128)S(1)}, bf16[6,240,384]{2,1,0:T(8,128)(2,1)S(1)}) custom-call(bf16[6,8,288,256]{3,2,1,0:T(8,128)(2,1)S(1)} %first_layout.1.laid_ref, bf16[2,21,16,384]{3,2,1,0:T(8,128)(2,1)S(1)} %collective-permute-done.12.b0, bf16[2,21,16,384]{3,2,1,0:T(8,128)(2,1)S(1)} %collective-permute-done.13.b1, ...), custom_call_target="tpu_custom_call" | custom-call | tf_op jit(solution)/shard_map/first_conv/pallas_call | solution.py:237
  74.7 2.1 %collective-permute-start.18 = (bf16[6,240,384]{2,1,0:T(8,128)(2,1)S(1)}, bf16[6,240,384]{2,1,0:T(8,128)(2,1)S(1)}, u32[]{:S(2)}, u32[]{:S(2)}) collective-permute-start(bf16[6,240,384]{2,1,0:T(8,128)(2,1)S(1)} %get-tuple-element.48), channel_id=1, source_target_pairs={{1,0},{0,1},{3,2},{2,3},{5,4},{4,5},{7,6},{6,7},{9,8},{8,9},{11,10... | collective-permute-start | bytes 3317768 | tf_op jit(solution)/shard_map/ppermute | solution.py:39
  76.8 2.2 %collective-permute-start.21 = (bf16[2,21,16,384]{3,2,1,0:T(8,128)(2,1)S(1)}, bf16[2,21,16,384]{3,2,1,0:T(8,128)(2,1)S(1)}, u32[]{:S(2)}, u32[]{:S(2)}) collective-permute-start(bf16[2,21,16,384]{3,2,1,0:T(8,128)(2,1)S(1)} %get-tuple-element.43.refs_1_), channel_id=1, source_target_pairs={{16,0},{65,1},{18,2},{67,3},{20,4},{69,5},{22,6},{71,7},{24,8},{73... | collective-permute-start | bytes 1548296 | tf_op jit(solution)/shard_map/ppermute | solution.py:39
  79.0 2.7 %collective-permute-start.19 = (bf16[2,21,16,384]{3,2,1,0:T(8,128)(2,1)S(1)}, bf16[2,21,16,384]{3,2,1,0:T(8,128)(2,1)S(1)}, u32[]{:S(2)}, u32[]{:S(2)}) collective-permute-start(bf16[2,21,16,384]{3,2,1,0:T(8,128)(2,1)S(1)} %collective-permute-done.16.refs_2_), channel_id=1, source_target_pairs={{16,0},{65,1},{18,2},{67,3},{20,4},{69,5},{22,6},{71,7},{24,8},{73... | collective-permute-start | bytes 1548296 | tf_op jit(solution)/shard_map/ppermute | solution.py:39
  81.7 0.0 collective-permute-start.20
  81.7 3.0 %second_layout.1.laid_ref = bf16[6,6,240,256]{3,2,1,0:T(8,128)(2,1)S(1)} custom-call(f32[6,240,384]{2,1,0:T(8,128)S(1)} %get-tuple-element.47.mine_ref, bf16[6,240,384]{2,1,0:T(8,128)(2,1)S(1)} %collective-permute-done.18.other_ref, f32[1,384]{1,0:T(1,128)S(1)} %reshape.11.bias_ref, f32[1,384]{1,0:T(1,128)S(1)} %reshape.12.gain_ref), custom_call_target="tpu_custom_call" | custom-call | tf_op jit(solution)/shard_map/second_layout/pallas_call | solution.py:154
  84.8 0.3 collective-permute-done.21.refs_3_
  85.1 3.4 %collective-permute-done.22.refs_4_ = bf16[2,21,16,384]{3,2,1,0:T(8,128)(2,1)S(1)} collective-permute-done((bf16[2,21,16,384]{3,2,1,0:T(8,128)(2,1)S(1)}, bf16[2,21,16,384]{3,2,1,0:T(8,128)(2,1)S(1)}, u32[]{:S(2)}, u32[]{:S(2)}) %collective-permute-start.22) | collective-permute-done | bytes 516128 | tf_op jit(solution)/shard_map/ppermute | solution.py:39
  88.5 4.6 %near_conv.3.near_ref = f32[4,192,384]{2,1,0:T(8,128)S(1)} custom-call(bf16[6,6,240,256]{3,2,1,0:T(8,128)(2,1)S(1)} %second_layout.1.laid_ref, bf16[2,21,16,384]{3,2,1,0:T(8,128)(2,1)S(1)} %get-tuple-element.42.refs_0_, bf16[2,21,16,384]{3,2,1,0:T(8,128)(2,1)S(1)} %get-tuple-element.43.refs_1_, bf16[2,21,16,384]{3,2,1,0:T(8,128)(2,1)S(1)} %collective-permute-done.16.refs_2_, ...), custom_call_target="tpu_custom_call" | custom-call | tf_op jit(solution)/shard_map/near_conv/pallas_call | solution.py:217
  93.1 0.0 copy-start.3
  93.1 0.6 collective-permute-done.20.b1
  93.7 1.9 %second_conv.1 = (f32[4,10,8,384]{3,2,1,0:T(8,128)S(1)}, bf16[4,10,8,384]{3,2,1,0:T(8,128)(2,1)S(1)}) custom-call(bf16[6,6,240,256]{3,2,1,0:T(8,128)(2,1)S(1)} %second_layout.1.laid_ref, bf16[2,21,16,384]{3,2,1,0:T(8,128)(2,1)S(1)} %collective-permute-done.19.b0, bf16[2,21,16,384]{3,2,1,0:T(8,128)(2,1)S(1)} %collective-permute-done.20.b1, ...), custom_call_target="tpu_custom_call" | custom-call | tf_op jit(solution)/shard_map/second_conv/pallas_call | solution.py:266
  95.6 0.1 collective-permute-start.23
  95.7 1.5 %collective-permute-done.23 = bf16[4,10,8,384]{3,2,1,0:T(8,128)(2,1)S(1)} collective-permute-done((bf16[4,10,8,384]{3,2,1,0:T(8,128)(2,1)S(1)}, bf16[4,10,8,384]{3,2,1,0:T(8,128)(2,1)S(1)}, u32[]{:S(2)}, u32[]{:S(2)}) %collective-permute-start.23) | collective-permute-done | bytes 245792 | tf_op jit(solution)/shard_map/ppermute | solution.py:39
  97.2 0.8 fusion.1
  (26 shorter events, 0.1 us)
Async XLA Ops:
  0.0 15.0 %copy-start.2 = (bf16[4,8,10,384]{3,1,2,0:T(8,128)(2,1)S(1)}, bf16[4,8,10,384]{3,1,2,0:T(8,128)(2,1)}, u32[]{:S(2)}) copy-start(bf16[4,8,10,384]{3,1,2,0:T(8,128)(2,1)} %param.7) | copy-start | bytes 737284
  1.1 13.9 %collective-permute-start.2 = (bf16[4,8,10,384]{3,2,1,0:T(8,128)(2,1)S(1)}, bf16[4,8,10,384]{3,2,1,0:T(8,128)(2,1)S(1)}, u32[]{:S(2)}, u32[]{:S(2)}) collective-permute-start(bf16[4,8,10,384]{3,2,1,0:T(8,128)(2,1)S(1)} %copy.10), channel_id=1, source_target_pairs={{0,64},{1,65},{2,66},{3,67},{4,68},{5,69},{6,70},{7,71},{8,72},{9,... | collective-permute-start | bytes 737288 | tf_op jit(solution)/shard_map/ppermute | solution.py:39
  5.1 0.9 copy-start
  6.0 0.9 copy-start.1
  7.3 12.3 %collective-permute-start = (bf16[2,21,8,384]{3,2,1,0:T(8,128)(2,1)S(1)}, bf16[2,21,8,384]{3,2,1,0:T(8,128)(2,1)S(1)}, u32[]{:S(2)}, u32[]{:S(2)}) collective-permute-start(bf16[2,21,8,384]{3,2,1,0:T(8,128)(2,1)S(1)} %fold.1), channel_id=1, source_target_pairs={{0,0},{1,1},{2,2},{3,3},{4,4},{5,5},{6,6},{7,7},{8,8},{9,9},{10,10... | collective-permute-start | bytes 774152 | tf_op jit(solution)/shard_map/ppermute | solution.py:39
  8.0 13.6 %collective-permute-start.1 = (bf16[2,21,8,384]{3,2,1,0:T(8,128)(2,1)S(1)}, bf16[2,21,8,384]{3,2,1,0:T(8,128)(2,1)S(1)}, u32[]{:S(2)}, u32[]{:S(2)}) collective-permute-start(bf16[2,21,8,384]{3,2,1,0:T(8,128)(2,1)S(1)} %fold.1), channel_id=1, source_target_pairs={{8,0},{9,1},{10,2},{11,3},{12,4},{13,5},{14,6},{15,7},{0,8},{1,9},... | collective-permute-start | bytes 774152 | tf_op jit(solution)/shard_map/ppermute | solution.py:39
  15.2 6.5 %collective-permute-start.3 = (bf16[8,2,10,384]{3,2,1,0:T(8,128)(2,1)S(1)}, bf16[8,2,10,384]{3,2,1,0:T(8,128)(2,1)S(1)}, u32[]{:S(2)}, u32[]{:S(2)}) collective-permute-start(bf16[8,2,10,384]{3,2,1,0:T(8,128)(2,1)S(1)} %get-tuple-element.53), channel_id=1, source_target_pairs={{0,16},{1,17},{2,18},{3,19},{4,20},{5,21},{6,22},{7,23},{8,24},{9,... | collective-permute-start | bytes 368648 | tf_op jit(solution)/shard_map/ppermute | solution.py:39
  18.3 6.8 %collective-permute-start.4 = (bf16[8,2,10,384]{3,2,1,0:T(8,128)(2,1)S(1)}, bf16[8,2,10,384]{3,2,1,0:T(8,128)(2,1)S(1)}, u32[]{:S(2)}, u32[]{:S(2)}) collective-permute-start(bf16[8,2,10,384]{3,2,1,0:T(8,128)(2,1)S(1)} %get-tuple-element.54), channel_id=1, source_target_pairs={{16,0},{17,1},{18,2},{19,3},{20,4},{21,5},{22,6},{23,7},{24,8},{25... | collective-permute-start | bytes 368648 | tf_op jit(solution)/shard_map/ppermute | solution.py:39
  25.3 15.0 %collective-permute-start.6 = (bf16[2,21,16,384]{3,2,1,0:T(8,128)(2,1)S(1)}, bf16[2,21,16,384]{3,2,1,0:T(8,128)(2,1)S(1)}, u32[]{:S(2)}, u32[]{:S(2)}) collective-permute-start(bf16[2,21,16,384]{3,2,1,0:T(8,128)(2,1)S(1)} %pad_maximum_fusion.1), channel_id=1, source_target_pairs={{14,0},{33,1},{0,2},{35,3},{2,4},{37,5},{4,6},{39,7},{6,8},{41,9},... | collective-permute-start | bytes 1548296 | tf_op jit(solution)/shard_map/ppermute | solution.py:39
  27.8 12.7 %collective-permute-start.7 = (bf16[2,21,16,384]{3,2,1,0:T(8,128)(2,1)S(1)}, bf16[2,21,16,384]{3,2,1,0:T(8,128)(2,1)S(1)}, u32[]{:S(2)}, u32[]{:S(2)}) collective-permute-start(bf16[2,21,16,384]{3,2,1,0:T(8,128)(2,1)S(1)} %pad_maximum_fusion.1), channel_id=1, source_target_pairs={{192,0},{49,1},{194,2},{51,3},{196,4},{53,5},{198,6},{55,7},{200,8... | collective-permute-start | bytes 1548296 | tf_op jit(solution)/shard_map/ppermute | solution.py:39
  27.8 12.9 %collective-permute-start.5 = (bf16[2,21,16,384]{3,2,1,0:T(8,128)(2,1)S(1)}, bf16[2,21,16,384]{3,2,1,0:T(8,128)(2,1)S(1)}, u32[]{:S(2)}, u32[]{:S(2)}) collective-permute-start(bf16[2,21,16,384]{3,2,1,0:T(8,128)(2,1)S(1)} %pad_maximum_fusion.1), channel_id=1, source_target_pairs={{64,0},{17,1},{66,2},{19,3},{68,4},{21,5},{70,6},{23,7},{72,8},{25... | collective-permute-start | bytes 1548296 | tf_op jit(solution)/shard_map/ppermute | solution.py:39
  30.6 8.2 %collective-permute-start.8 = (bf16[8,12,2,384]{3,2,1,0:T(2,128)(2,1)S(1)}, bf16[8,12,2,384]{3,2,1,0:T(2,128)(2,1)S(1)}, u32[]{:S(2)}, u32[]{:S(2)}) collective-permute-start(bf16[8,12,2,384]{3,2,1,0:T(2,128)(2,1)S(1)} %broadcast_select_fusion), channel_id=1, source_target_pairs={{2,1},{1,2},{4,3},{3,4},{6,5},{5,6},{8,7},{7,8},{10,9},{9,10},{12,... | collective-permute-start | bytes 442376 | tf_op jit(solution)/shard_map/ppermute | solution.py:39
  40.2 2.5 %collective-permute-start.9 = (bf16[8,12,12,384]{3,0,2,1:T(8,128)(2,1)S(1)}, bf16[8,12,12,384]{3,0,2,1:T(8,128)(2,1)S(1)}, u32[]{:S(2)}, u32[]{:S(2)}) collective-permute-start(bf16[8,12,12,384]{3,0,2,1:T(8,128)(2,1)S(1)} %copy.12), channel_id=1, source_target_pairs={{1,0},{0,1},{3,2},{2,3},{5,4},{4,5},{7,6},{6,7},{9,8},{8,9},{11,10... | collective-permute-start | bytes 2654216 | tf_op jit(solution)/shard_map/ppermute | solution.py:39
  40.8 7.5 %copy-start.4 = (f32[384]{0:T(512)S(1)}, f32[384]{0:T(512)}, u32[]{:S(2)}) copy-start(f32[384]{0:T(512)} %param.8) | copy-start | bytes 4612
  42.7 11.3 %collective-permute-start.10 = (bf16[2,21,16,384]{3,2,1,0:T(8,128)(2,1)S(1)}, bf16[2,21,16,384]{3,2,1,0:T(8,128)(2,1)S(1)}, u32[]{:S(2)}, u32[]{:S(2)}) collective-permute-start(bf16[2,21,16,384]{3,2,1,0:T(8,128)(2,1)S(1)} %get-tuple-element.31.refs_0_), channel_id=1, source_target_pairs={{16,0},{65,1},{18,2},{67,3},{20,4},{69,5},{22,6},{71,7},{24,8},{73... | collective-permute-start | bytes 1548296 | tf_op jit(solution)/shard_map/ppermute | solution.py:39
  45.0 10.1 %collective-permute-start.11 = (bf16[2,21,16,384]{3,2,1,0:T(8,128)(2,1)S(1)}, bf16[2,21,16,384]{3,2,1,0:T(8,128)(2,1)S(1)}, u32[]{:S(2)}, u32[]{:S(2)}) collective-permute-start(bf16[2,21,16,384]{3,2,1,0:T(8,128)(2,1)S(1)} %get-tuple-element.32.refs_1_), channel_id=1, source_target_pairs={{48,0},{193,1},{50,2},{195,3},{52,4},{197,5},{54,6},{199,7},{56,8}... | collective-permute-start | bytes 1548296 | tf_op jit(solution)/shard_map/ppermute | solution.py:39
  45.8 13.6 %collective-permute-start.14 = (bf16[2,21,16,384]{3,2,1,0:T(8,128)(2,1)S(1)}, bf16[2,21,16,384]{3,2,1,0:T(8,128)(2,1)S(1)}, u32[]{:S(2)}, u32[]{:S(2)}) collective-permute-start(bf16[2,21,16,384]{3,2,1,0:T(8,128)(2,1)S(1)} %get-tuple-element.32.refs_1_), channel_id=1, source_target_pairs={{16,0},{65,1},{18,2},{67,3},{20,4},{69,5},{22,6},{71,7},{24,8},{73... | collective-permute-start | bytes 1548296 | tf_op jit(solution)/shard_map/ppermute | solution.py:39
  48.3 12.3 %collective-permute-start.15 = (bf16[2,21,16,384]{3,2,1,0:T(8,128)(2,1)S(1)}, bf16[2,21,16,384]{3,2,1,0:T(8,128)(2,1)S(1)}, u32[]{:S(2)}, u32[]{:S(2)}) collective-permute-start(bf16[2,21,16,384]{3,2,1,0:T(8,128)(2,1)S(1)} %get-tuple-element.31.refs_0_), channel_id=1, source_target_pairs={{48,0},{193,1},{50,2},{195,3},{52,4},{197,5},{54,6},{199,7},{56,8}... | collective-permute-start | bytes 1548296 | tf_op jit(solution)/shard_map/ppermute | solution.py:39
  55.1 14.1 %collective-permute-start.12 = (bf16[2,21,16,384]{3,2,1,0:T(8,128)(2,1)S(1)}, bf16[2,21,16,384]{3,2,1,0:T(8,128)(2,1)S(1)}, u32[]{:S(2)}, u32[]{:S(2)}) collective-permute-start(bf16[2,21,16,384]{3,2,1,0:T(8,128)(2,1)S(1)} %collective-permute-done.10.refs_2_), channel_id=1, source_target_pairs={{16,0},{65,1},{18,2},{67,3},{20,4},{69,5},{22,6},{71,7},{24,8},{73... | collective-permute-start | bytes 1548296 | tf_op jit(solution)/shard_map/ppermute | solution.py:39
  56.8 12.4 %collective-permute-start.13 = (bf16[2,21,16,384]{3,2,1,0:T(8,128)(2,1)S(1)}, bf16[2,21,16,384]{3,2,1,0:T(8,128)(2,1)S(1)}, u32[]{:S(2)}, u32[]{:S(2)}) collective-permute-start(bf16[2,21,16,384]{3,2,1,0:T(8,128)(2,1)S(1)} %collective-permute-done.11.refs_5_), channel_id=1, source_target_pairs={{48,0},{193,1},{50,2},{195,3},{52,4},{197,5},{54,6},{199,7},{56,8}... | collective-permute-start | bytes 1548296 | tf_op jit(solution)/shard_map/ppermute | solution.py:39
  56.8 12.4 %collective-permute-start.16 = (bf16[2,21,16,384]{3,2,1,0:T(8,128)(2,1)S(1)}, bf16[2,21,16,384]{3,2,1,0:T(8,128)(2,1)S(1)}, u32[]{:S(2)}, u32[]{:S(2)}) collective-permute-start(bf16[2,21,16,384]{3,2,1,0:T(8,128)(2,1)S(1)} %get-tuple-element.42.refs_0_), channel_id=1, source_target_pairs={{16,0},{65,1},{18,2},{67,3},{20,4},{69,5},{22,6},{71,7},{24,8},{73... | collective-permute-start | bytes 1548296 | tf_op jit(solution)/shard_map/ppermute | solution.py:39
  59.5 12.3 %collective-permute-start.17 = (bf16[2,21,16,384]{3,2,1,0:T(8,128)(2,1)S(1)}, bf16[2,21,16,384]{3,2,1,0:T(8,128)(2,1)S(1)}, u32[]{:S(2)}, u32[]{:S(2)}) collective-permute-start(bf16[2,21,16,384]{3,2,1,0:T(8,128)(2,1)S(1)} %get-tuple-element.43.refs_1_), channel_id=1, source_target_pairs={{48,0},{193,1},{50,2},{195,3},{52,4},{197,5},{54,6},{199,7},{56,8}... | collective-permute-start | bytes 1548296 | tf_op jit(solution)/shard_map/ppermute | solution.py:39
  69.1 12.6 %copy-start.5 = (f32[384]{0:T(512)S(1)}, f32[384]{0:T(512)}, u32[]{:S(2)}) copy-start(f32[384]{0:T(512)} %param.10) | copy-start | bytes 4612
  69.1 12.6 %copy-start.6 = (f32[384]{0:T(512)S(1)}, f32[384]{0:T(512)}, u32[]{:S(2)}) copy-start(f32[384]{0:T(512)} %param.11) | copy-start | bytes 4612
  74.7 7.0 %collective-permute-start.18 = (bf16[6,240,384]{2,1,0:T(8,128)(2,1)S(1)}, bf16[6,240,384]{2,1,0:T(8,128)(2,1)S(1)}, u32[]{:S(2)}, u32[]{:S(2)}) collective-permute-start(bf16[6,240,384]{2,1,0:T(8,128)(2,1)S(1)} %get-tuple-element.48), channel_id=1, source_target_pairs={{1,0},{0,1},{3,2},{2,3},{5,4},{4,5},{7,6},{6,7},{9,8},{8,9},{11,10... | collective-permute-start | bytes 3317768 | tf_op jit(solution)/shard_map/ppermute | solution.py:39
  76.8 8.2 %collective-permute-start.21 = (bf16[2,21,16,384]{3,2,1,0:T(8,128)(2,1)S(1)}, bf16[2,21,16,384]{3,2,1,0:T(8,128)(2,1)S(1)}, u32[]{:S(2)}, u32[]{:S(2)}) collective-permute-start(bf16[2,21,16,384]{3,2,1,0:T(8,128)(2,1)S(1)} %get-tuple-element.43.refs_1_), channel_id=1, source_target_pairs={{16,0},{65,1},{18,2},{67,3},{20,4},{69,5},{22,6},{71,7},{24,8},{73... | collective-permute-start | bytes 1548296 | tf_op jit(solution)/shard_map/ppermute | solution.py:39
  79.0 9.4 %collective-permute-start.22 = (bf16[2,21,16,384]{3,2,1,0:T(8,128)(2,1)S(1)}, bf16[2,21,16,384]{3,2,1,0:T(8,128)(2,1)S(1)}, u32[]{:S(2)}, u32[]{:S(2)}) collective-permute-start(bf16[2,21,16,384]{3,2,1,0:T(8,128)(2,1)S(1)} %get-tuple-element.42.refs_0_), channel_id=1, source_target_pairs={{48,0},{193,1},{50,2},{195,3},{52,4},{197,5},{54,6},{199,7},{56,8}... | collective-permute-start | bytes 1548296 | tf_op jit(solution)/shard_map/ppermute | solution.py:39
  79.0 14.1 %collective-permute-start.19 = (bf16[2,21,16,384]{3,2,1,0:T(8,128)(2,1)S(1)}, bf16[2,21,16,384]{3,2,1,0:T(8,128)(2,1)S(1)}, u32[]{:S(2)}, u32[]{:S(2)}) collective-permute-start(bf16[2,21,16,384]{3,2,1,0:T(8,128)(2,1)S(1)} %collective-permute-done.16.refs_2_), channel_id=1, source_target_pairs={{16,0},{65,1},{18,2},{67,3},{20,4},{69,5},{22,6},{71,7},{24,8},{73... | collective-permute-start | bytes 1548296 | tf_op jit(solution)/shard_map/ppermute | solution.py:39
  81.7 12.0 %collective-permute-start.20 = (bf16[2,21,16,384]{3,2,1,0:T(8,128)(2,1)S(1)}, bf16[2,21,16,384]{3,2,1,0:T(8,128)(2,1)S(1)}, u32[]{:S(2)}, u32[]{:S(2)}) collective-permute-start(bf16[2,21,16,384]{3,2,1,0:T(8,128)(2,1)S(1)} %collective-permute-done.17.refs_5_), channel_id=1, source_target_pairs={{48,0},{193,1},{50,2},{195,3},{52,4},{197,5},{54,6},{199,7},{56,8}... | collective-permute-start | bytes 1548296 | tf_op jit(solution)/shard_map/ppermute | solution.py:39
  93.1 4.1 %copy-start.3 = (f32[384]{0:T(512)S(1)}, f32[384]{0:T(512)}, u32[]{:S(2)}) copy-start(f32[384]{0:T(512)} %param.13) | copy-start | bytes 4612
  95.6 1.6 %collective-permute-start.23 = (bf16[4,10,8,384]{3,2,1,0:T(8,128)(2,1)S(1)}, bf16[4,10,8,384]{3,2,1,0:T(8,128)(2,1)S(1)}, u32[]{:S(2)}, u32[]{:S(2)}) collective-permute-start(bf16[4,10,8,384]{3,2,1,0:T(8,128)(2,1)S(1)} %get-tuple-element.52), channel_id=1, source_target_pairs={{1,0},{0,1},{3,2},{2,3},{5,4},{4,5},{7,6},{6,7},{9,8},{8,9},{11,10... | collective-permute-start | bytes 737288 | tf_op jit(solution)/shard_map/ppermute | solution.py:39
